TPU v7x, 32 devices: a whole 2x2x4 slice. The times are simulated.
32 devices in a mesh: group: 4 (over y, x), tile: 8 (over z, core).
Axes of the slice: x: 2, y: 2, z: 4, core: 2. Of those that a mesh axis runs over, the one named last changes fastest.
Arguments:
- tracer: float32 [16, 64, 2048], P(None, 'group', 'tile'), may hold values from -6 to 6
- east_speed: float32 [16, 64, 2048], P(None, 'group', 'tile'), may hold values from -0.5 to 0.5
- north_speed: float32 [16, 64, 2048], P(None, 'group', 'tile'), may hold values from -0.5 to 0.5
- mixing: float32 [15, 64, 2048], P(None, 'group', 'tile'), may hold values from 0.1 to 3
- depth_levels: int32 [64, 2048], P('group', 'tile'), may hold values from 0 to 16
- sensitivity: float32 [16, 64, 2048], P(None, 'group', 'tile'), may hold values from -6 to 6
Outputs:
- final_state: float32 [16, 64, 2048], P(None, 'group', 'tile')
- adjoint_state: float32 [16, 64, 2048], P(None, 'group', 'tile')
All inputs are finite; a program needn't handle non-finite values.
Results may differ from a plain program's by a relative error of at most 0.0001.
Values sent between devices are 32-bit elements; how exact they have to be, the bound alone decides.
No kernel may reach another device: no remote copies, remote signals or barrier semaphores. Data moves between devices by JAX's collectives and lax.ppermute only.
A program may use at most 64 MiB of HBM per device.

v0:
```python
import jax
import jax.numpy as jnp
from jax import lax
from jax.sharding import PartitionSpec as P

diffusivity = 0.1
uptake = 0.2


def extended(value, sides, width):
    for axis, dim in sides:
        devices, length = (lax.axis_size(axis), value.shape[dim])
        up = [(i, (i + 1) % devices) for i in range(devices - 1)]
        down = [(j, i) for i, j in up]
        last = lax.slice_in_dim(value, length - width, length, axis=dim)
        initial = lax.slice_in_dim(value, 0, width, axis=dim)
        before = lax.ppermute(last, axis, up)
        after = lax.ppermute(initial, axis, down)
        value = jnp.concatenate([before, value, after], axis=dim)
    return value


def interval(source, first_index, last_index, along_axis):
    return lax.slice_in_dim(source, first_index, last_index, axis=along_axis)


def trim_margin(source, margin):
    return source[:, margin : source.shape[1] - margin, margin : source.shape[2] - margin]


def trim_all(factors, margin):
    return tuple((trim_margin(member, margin) for member in factors))


def flux_change(tracer_field, face_speed, wet_mask, along_axis):
    extent = tracer_field.shape[along_axis]
    open_face = interval(wet_mask, 2, extent - 1, along_axis) * interval(
        wet_mask, 1, extent - 2, along_axis
    )
    inner = interval(tracer_field, 2, extent - 1, along_axis)
    behind = interval(tracer_field, 1, extent - 2, along_axis)
    outer = interval(tracer_field, 3, extent, along_axis) + interval(
        tracer_field, 0, extent - 3, along_axis
    )
    face_flux = open_face * (
        interval(face_speed, 2, extent - 1, along_axis) * (7.0 * (inner + behind) - outer) / 12.0
        - diffusivity * (inner - behind)
    )
    faces_total = face_flux.shape[along_axis]
    return interval(face_flux, 0, faces_total - 1, along_axis) - interval(
        face_flux, 1, faces_total, along_axis
    )


def explicit_step(tracer_field, east_face, north_face, wet_mask):
    across = flux_change(tracer_field, east_face, wet_mask, 2)
    across = across[:, 2 : across.shape[1] - 2, :]
    north_term = flux_change(tracer_field, north_face, wet_mask, 1)
    north_term = north_term[:, :, 2 : north_term.shape[2] - 2]
    middle = trim_margin(tracer_field, 2)
    return trim_margin(wet_mask, 2) * (middle + across + north_term - uptake * middle * middle)


def flux_reverse(weight, face_speed, wet_mask, along_axis):
    extent = weight.shape[along_axis]
    open_face = interval(wet_mask, 1, extent, along_axis) * interval(
        wet_mask, 0, extent - 1, along_axis
    )
    face_jump = interval(weight, 1, extent, along_axis) - interval(
        weight, 0, extent - 1, along_axis
    )
    carried = open_face * interval(face_speed, 1, extent, along_axis) * face_jump / 12.0
    spread = diffusivity * open_face * face_jump
    face_count = extent - 1
    moved = (
        7.0
        * (
            interval(carried, 1, face_count - 2, along_axis)
            + interval(carried, 2, face_count - 1, along_axis)
        )
        - interval(carried, 0, face_count - 3, along_axis)
        - interval(carried, 3, face_count, along_axis)
    )
    mixed = interval(spread, 2, face_count - 1, along_axis) - interval(
        spread, 1, face_count - 2, along_axis
    )
    return moved + mixed


def adjoint_explicit(weight, state_now, east_face, north_face, wet_mask):
    across = flux_reverse(weight, east_face, wet_mask, 2)
    across = across[:, 2 : across.shape[1] - 2, :]
    north_term = flux_reverse(weight, north_face, wet_mask, 1)
    north_term = north_term[:, :, 2 : north_term.shape[2] - 2]
    middle = trim_margin(weight, 2)
    return middle + across + north_term - 2.0 * uptake * state_now * middle


def factorize(mixing_field, wet_mask):
    links = mixing_field * wet_mask[:-1] * wet_mask[1:]
    layers = wet_mask.shape[0]
    zero_plane = jnp.zeros_like(wet_mask[0])
    uppers = []
    inverses = []
    above_link = zero_plane
    above_upper = zero_plane
    for position in range(layers):
        below_link = links[position] if position < layers - 1 else zero_plane
        pivot_sum = 1.0 + above_link + below_link + above_link * above_upper
        inverse = 1.0 / pivot_sum
        upper_term = -below_link * inverse
        uppers.append(upper_term)
        inverses.append(inverse)
        above_link = below_link
        above_upper = upper_term
    return (jnp.stack(uppers), jnp.stack(inverses), links)


def column_solve(factors, right_side):
    uppers, inverses, links = factors
    layers = right_side.shape[0]
    current = right_side[0] * inverses[0]
    forward_pass = [current]
    for position in range(1, layers):
        current = (right_side[position] + links[position - 1] * current) * inverses[position]
        forward_pass.append(current)
    result = [current]
    for position in range(layers - 2, -1, -1):
        current = forward_pass[position] - uppers[position] * current
        result.append(current)
    return jnp.stack(result[::-1])


def shards(tracer, east_speed, north_speed, mixing, depth_levels, sensitivity):
    layers = tracer.shape[0]
    zero_level = jnp.zeros_like(mixing[:1])
    depth_float = depth_levels.astype(jnp.float32)[None]
    packed = jnp.concatenate(
        [tracer, east_speed, north_speed, mixing, zero_level, depth_float], axis=0
    )
    packed_more = jnp.concatenate([packed, sensitivity], axis=0)
    widened = extended(packed_more, (("group", 1), ("tile", 2)), 4)
    tracer_wide = widened[:layers]
    east_wide = widened[layers : 2 * layers]
    north_wide = widened[2 * layers : 3 * layers]
    mixing_wide = widened[3 * layers : 4 * layers - 1]
    depth_wide = widened[4 * layers]
    levels = lax.broadcasted_iota(jnp.float32, tracer_wide.shape, 0)
    wet_wide = jnp.where(levels < depth_wide[None], 1.0, 0.0).astype(jnp.float32)
    factors = factorize(mixing_wide, wet_wide)
    near_factors = trim_all(factors, 2)
    inner_factors = trim_all(factors, 4)
    east_near = trim_margin(east_wide, 2)
    north_near = trim_margin(north_wide, 2)
    wet_near = trim_margin(wet_wide, 2)
    first_state = column_solve(
        near_factors, explicit_step(tracer_wide, east_wide, north_wide, wet_wide)
    )
    final_state = column_solve(
        inner_factors, explicit_step(first_state, east_near, north_near, wet_near)
    )
    sensitivity_wide = widened[4 * layers + 1 : 5 * layers + 1]
    gradient_wide = wet_wide * column_solve(factors, sensitivity_wide)
    middle_adjoint = adjoint_explicit(gradient_wide, first_state, east_wide, north_wide, wet_wide)
    gradient_near = wet_near * column_solve(near_factors, middle_adjoint)
    adjoint = adjoint_explicit(gradient_near, tracer, east_near, north_near, wet_near)
    return (final_state, adjoint)


def solution(mesh):
    in_specs = (
        P(None, "group", "tile"),
        P(None, "group", "tile"),
        P(None, "group", "tile"),
        P(None, "group", "tile"),
        P("group", "tile"),
        P(None, "group", "tile"),
    )
    out_specs = (P(None, "group", "tile"), P(None, "group", "tile"))
    return jax.shard_map(shards, mesh=mesh, in_specs=in_specs, out_specs=out_specs, check_vma=False)
```

profile of v0, /device:TPU:12, one launch (start us, length us, event | category | flops | bytes accessed | tf_op | source)
XLA Modules:
  0.0 59.4 jit_solution(16387298173062515258)
XLA Ops:
  0.7 1.0 %constant_dynamic-update-slice_fusion.6 = f32[81,16,256]{2,1,0:T(8,128)S(1)} fusion(f32[16,16,256]{2,1,0:T(8,128)} %param.6), kind=kLoop, calls=%fused_computation.113 | loop fusion | bytes 524288
  1.7 1.0 %constant_dynamic-update-slice_fusion.5 = f32[81,16,256]{2,1,0:T(8,128)S(1)} fusion(f32[81,16,256]{2,1,0:T(8,128)S(1)} %constant_dynamic-update-slice_fusion.6, f32[16,16,256]{2,1,0:T(8,128)} %param.7), kind=kLoop, calls=%fused_computation.112 | loop fusion | bytes 524288
  2.7 1.0 %constant_dynamic-update-slice_fusion.4 = f32[81,16,256]{2,1,0:T(8,128)S(1)} fusion(f32[81,16,256]{2,1,0:T(8,128)S(1)} %constant_dynamic-update-slice_fusion.5, f32[16,16,256]{2,1,0:T(8,128)} %param.8), kind=kLoop, calls=%fused_computation.111 | loop fusion | bytes 524288
  3.7 0.1 fusion.163
  3.9 3.3 %collective-permute-start.1 = (f32[81,4,256]{2,0,1:T(8,128)S(1)}, f32[81,4,256]{2,0,1:T(8,128)S(1)}, u32[]{:S(2)}, u32[]{:S(2)}) collective-permute-start(f32[81,4,256]{2,0,1:T(8,128)S(1)} %copy.22), channel_id=1, source_target_pairs={{8,0},{16,8},{24,16},{9,1},{17,9},{25,17},{10,2},{18,10},{26,18},{... | collective-permute-start | bytes 995336 | tf_op jit(solution)/shard_map/ppermute | solution.py:18
  7.4 2.5 %collective-permute-start = (f32[81,4,256]{2,0,1:T(8,128)S(1)}, f32[81,4,256]{2,0,1:T(8,128)S(1)}, u32[]{:S(2)}, u32[]{:S(2)}) collective-permute-start(f32[81,4,256]{2,0,1:T(8,128)S(1)} %copy.21), channel_id=1, source_target_pairs={{0,8},{8,16},{16,24},{1,9},{9,17},{17,25},{2,10},{10,18},{18,26},{... | collective-permute-start | bytes 995336 | tf_op jit(solution)/shard_map/ppermute | solution.py:17
  9.9 6.2 %collective-permute-done.1 = f32[81,4,256]{2,0,1:T(8,128)S(1)} collective-permute-done((f32[81,4,256]{2,0,1:T(8,128)S(1)}, f32[81,4,256]{2,0,1:T(8,128)S(1)}, u32[]{:S(2)}, u32[]{:S(2)}) %collective-permute-start.1) | collective-permute-done | bytes 331808 | tf_op jit(solution)/shard_map/ppermute | solution.py:18
  16.1 0.1 copy.24
  16.2 7.4 %collective-permute-done = f32[81,4,256]{2,0,1:T(8,128)S(1)} collective-permute-done((f32[81,4,256]{2,0,1:T(8,128)S(1)}, f32[81,4,256]{2,0,1:T(8,128)S(1)}, u32[]{:S(2)}, u32[]{:S(2)}) %collective-permute-start) | collective-permute-done | bytes 331808 | tf_op jit(solution)/shard_map/ppermute | solution.py:17
  23.7 0.1 copy.23
  23.8 0.3 pad_maximum_fusion.1
  24.1 0.3 fusion.162
  24.5 0.4 copy.26
  24.9 1.9 %collective-permute-start.3 = (f32[81,24,4]{0,1,2:T(8,128)S(1)}, f32[81,24,4]{0,1,2:T(8,128)S(1)}, u32[]{:S(2)}, u32[]{:S(2)}) collective-permute-start(f32[81,24,4]{0,1,2:T(8,128)S(1)} %copy.26), channel_id=1, source_target_pairs={{1,0},{2,1},{3,2},{4,3},{5,4},{6,5},{7,6},{9,8},{10,9},{11,10},{12... | collective-permute-start | bytes 93320 | tf_op jit(solution)/shard_map/ppermute | solution.py:18
  26.9 0.4 copy.25
  27.3 2.6 %collective-permute-start.2 = (f32[81,24,4]{0,1,2:T(8,128)S(1)}, f32[81,24,4]{0,1,2:T(8,128)S(1)}, u32[]{:S(2)}, u32[]{:S(2)}) collective-permute-start(f32[81,24,4]{0,1,2:T(8,128)S(1)} %copy.25), channel_id=1, source_target_pairs={{0,1},{1,2},{2,3},{3,4},{4,5},{5,6},{6,7},{8,9},{9,10},{10,11},{11... | collective-permute-start | bytes 93320 | tf_op jit(solution)/shard_map/ppermute | solution.py:17
  29.9 0.5 copy.28
  30.3 2.3 %collective-permute-done.2 = f32[81,24,4]{0,1,2:T(8,128)S(1)} collective-permute-done((f32[81,24,4]{0,1,2:T(8,128)S(1)}, f32[81,24,4]{0,1,2:T(8,128)S(1)}, u32[]{:S(2)}, u32[]{:S(2)}) %collective-permute-start.2) | collective-permute-done | bytes 31136 | tf_op jit(solution)/shard_map/ppermute | solution.py:17
  32.7 0.5 copy.27
  33.2 0.8 %maximum_bitcast_fusion = f32[24,264]{1,0:T(8,128)S(1)} fusion(f32[81,24,4]{2,1,0:T(8,128)S(1)} %copy.28, f32[81,24,4]{2,1,0:T(8,128)S(1)} %copy.27, f32[81,4,256]{2,1,0:T(4,128)} %copy-done, f32[81,16,256]{2,1,0:T(8,128)S(1)} %constant_dynamic-update-slice_fusion, f32[81,4,256]{2,1,0:T(4,128)} %copy-done.2), kind=kLoop, calls=%fused_computation.271 | loop fusion | flops 25344 | bytes 2078208 | tf_op jit(solution)/shard_map/lt | solution.py:149
  34.0 0.1 copy-done.1
  34.2 1.8 %pad_maximum_fusion = f32[81,24,264]{2,1,0:T(8,128)S(1)} fusion(f32[81,24,4]{2,1,0:T(8,128)S(1)} %copy.28, f32[81,4,256]{2,1,0:T(4,128)S(1)} %copy-done.1, f32[81,16,256]{2,1,0:T(8,128)S(1)} %constant_dynamic-update-slice_fusion, f32[81,4,256]{2,1,0:T(4,128)S(1)} %copy-done.3, f32[81,24,4]{2,1,0:T(8,128)S(1)} %copy.27), kind=kLoop, calls=%fused_computation | loop fusion | flops 2052864 | bytes 4105728 | tf_op jit(solution)/shard_map/concatenate | solution.py:19
  36.2 0.5 fusion.32
  36.6 1.0 %fusion.38 = f32[16,24,261]{2,1,0:T(8,128)S(1)} fusion(f32[81,24,264]{2,1,0:T(8,128)S(1)} %pad_maximum_fusion, f32[16,24,264]{2,1,0:T(8,128)S(1)} %fusion.39), kind=kLoop, calls=%fused_computation.73 | loop fusion | flops 1102464 | bytes 3207168 | tf_op jit(solution)/shard_map/mul | solution.py:45
  37.6 0.2 fusion.174
  37.9 0.5 constant_dynamic-update-slice_fusion.54
  38.4 0.8 %fusion.1 = f32[16,20,260]{2,1,0:T(8,128)S(1)} fusion(f32[16,20,264]{2,1,0:T(8,128)S(1)} %get-tuple-element.134, f32[16,20,264]{2,1,0:T(8,128)S(1)} %get-tuple-element.133, f32[16,24,260]{2,1,0:T(8,128)S(1)} %get-tuple-element.132, f32[16,24,260]{2,1,0:T(8,128)S(1)} %get-tuple-element.131, f32[81,24,264]{2,1,0:T(8,128)S(1)} %pad_maximum_fusion, ...), kind=kLoop, calls=%fused_computation.4 | loop fusion | flops 665600 | bytes 2329600 | tf_op jit(solution)/shard_map/mul | solution.py:61
  39.3 0.4 fusion.84
  39.7 0.3 constant_dynamic-update-slice_fusion.22
  40.7 0.8 %fusion.26 = f32[16,20,257]{2,1,0:T(8,128)S(1)} fusion(f32[16,20,260]{2,1,0:T(8,128)S(1)} %constant_dynamic-update-slice_fusion.7, f32[81,24,4]{2,1,0:T(8,128)S(1)} %copy.28, f32[81,4,256]{2,1,0:T(4,128)S(1)} %copy-done.1, f32[81,16,256]{2,1,0:T(8,128)S(1)} %constant_dynamic-update-slice_fusion, f32[81,4,256]{2,1,0:T(4,128)S(1)} %copy-done.3, ...), kind=kLoop, calls=%fused_computation.52 | loop fusion | flops 1151360 | bytes 4324480 | tf_op jit(solution)/shard_map/mul | solution.py:45
  41.6 0.7 %fusion.21 = f32[16,17,260]{2,1,0:T(8,128)S(1)} fusion(f32[16,20,260]{2,1,0:T(8,128)S(1)} %constant_dynamic-update-slice_fusion.7, f32[81,24,264]{2,1,0:T(8,128)S(1)} %pad_maximum_fusion, f32[16,24,264]{2,1,0:T(8,128)S(1)} %fusion.39), kind=kLoop, calls=%fused_computation.45 | loop fusion | flops 777920 | bytes 2263040 | tf_op jit(solution)/shard_map/mul | solution.py:45
  42.2 0.5 constant_dynamic-update-slice_fusion.52
  42.7 0.4 constant_dynamic-update-slice_fusion.51
  43.1 0.5 constant_dynamic-update-slice_fusion.50
  43.6 0.4 constant_dynamic-update-slice_fusion.49
  44.0 0.4 constant_dynamic-update-slice_fusion.48
  44.5 0.4 constant_dynamic-update-slice_fusion.47
  44.9 0.4 constant_dynamic-update-slice_fusion.46
  45.4 0.4 constant_dynamic-update-slice_fusion.45
  45.8 0.4 constant_dynamic-update-slice_fusion.44
  46.2 0.6 %constant_dynamic-update-slice_fusion.43 = f32[16,24,264]{2,1,0:T(8,128)S(1)} fusion(f32[16,24,264]{2,1,0:T(8,128)S(1)} %constant_dynamic-update-slice_fusion.44, f32[81,24,4]{2,1,0:T(8,128)S(1)} %copy.28, f32[81,4,256]{2,1,0:T(4,128)S(1)} %copy-done.1, f32[81,16,256]{2,1,0:T(8,128)S(1)} %constant_dynamic-update-slice_fusion, ...), kind=kLoop, calls=%fused_computation.150 | loop fusion | flops 836352 | bytes 5087232
  46.9 0.4 constant_dynamic-update-slice_fusion.42
  47.3 0.4 constant_dynamic-update-slice_fusion.41
  47.7 0.4 constant_dynamic-update-slice_fusion.40
  48.1 0.4 constant_dynamic-update-slice_fusion.39
  48.6 0.6 fusion.16
  49.2 0.3 fusion.11
  49.5 0.4 fusion.169
  49.9 0.2 fusion.170
  50.1 0.5 fusion.168
  50.6 1.2 %fusion.8 = f32[16,20,260]{2,1,0:T(8,128)S(1)} fusion(f32[16,20,264]{2,1,0:T(8,128)S(1)} %get-tuple-element.124, f32[16,20,264]{2,1,0:T(8,128)S(1)} %get-tuple-element.123, f32[16,20,264]{2,1,0:T(8,128)S(1)} %get-tuple-element.120, f32[16,20,264]{2,1,0:T(8,128)S(1)} %get-tuple-element.121, f32[16,20,264]{2,1,0:T(8,128)S(1)} %get-tuple-element.122, ...), kind=kLoop, calls=%fused_computation.18 | loop fusion | flops 1414400 | bytes 4992000 | tf_op jit(solution)/shard_map/sub | solution.py:96
  51.8 0.4 fusion.54
  52.2 0.3 constant_dynamic-update-slice_fusion.70
  53.3 0.2 slice_multiply_fusion.12
  53.5 0.7 %fusion.5 = (f32[16,20,259]{2,1,0:T(8,128)S(1)}, f32[16,20,259]{2,1,0:T(8,128)S(1)}) fusion(f32[81,24,264]{2,1,0:T(8,128)S(1)} %pad_maximum_fusion, f32[16,24,264]{2,1,0:T(8,128)S(1)} %fusion.39, f32[16,20,260]{2,1,0:T(8,128)S(1)} %slice_multiply_fusion.12), kind=kLoop, calls=%fused_computation.13 | loop fusion | flops 580160 | bytes 2320640 | tf_op jit(solution)/shard_map/div | solution.py:72
  54.2 0.6 %fusion.3 = (f32[16,19,260]{2,1,0:T(8,128)S(1)}, f32[16,19,260]{2,1,0:T(8,128)S(1)}) fusion(f32[81,24,264]{2,1,0:T(8,128)S(1)} %pad_maximum_fusion, f32[16,24,264]{2,1,0:T(8,128)S(1)} %fusion.39, f32[16,20,260]{2,1,0:T(8,128)S(1)} %slice_multiply_fusion.12), kind=kLoop, calls=%fused_computation.8 | loop fusion | flops 553280 | bytes 2213120 | tf_op jit(solution)/shard_map/div | solution.py:72
  54.8 0.2 fusion.172
  55.1 0.4 fusion.41
  55.5 0.2 slice_multiply_fusion.20
  55.7 0.2 constant_dynamic-update-slice_fusion.38
  56.4 0.3 fusion.165
  56.8 0.4 fusion.164
  57.3 0.8 %copy-done.4 = f32[16,16,256]{2,1,0:T(8,128)S(1)} copy-done((f32[16,16,256]{2,1,0:T(8,128)S(1)}, f32[16,16,256]{2,1,0:T(8,128)}, u32[]{:S(2)}) %copy-start.4) | copy-done | bytes 262168
  58.1 1.3 %fusion.44 = f32[16,16,256]{2,1,0:T(8,128)} fusion(f32[16,16,260]{2,1,0:T(8,128)S(1)} %get-tuple-element.112, f32[16,16,260]{2,1,0:T(8,128)S(1)} %get-tuple-element.111, f32[16,16,260]{2,1,0:T(8,128)S(1)} %get-tuple-element.108, f32[16,16,260]{2,1,0:T(8,128)S(1)} %get-tuple-element.109, f32[16,16,260]{2,1,0:T(8,128)S(1)} %get-tuple-element.110, ...), kind=kLoop, calls=%fused_computation.90 | loop fusion | flops 1114112 | bytes 3932160 | tf_op jit(solution)/shard_map/sub | solution.py:96
  (78 shorter events, 2.9 us)
Async XLA Ops:
  0.6 3.0 %copy-start.6 = (f32[15,16,256]{2,1,0:T(8,128)S(1)}, f32[15,16,256]{2,1,0:T(8,128)}, u32[]{:S(2)}) copy-start(f32[15,16,256]{2,1,0:T(8,128)} %param.9) | copy-start | bytes 737284
  0.6 3.0 %copy-start.7 = (s32[16,256]{1,0:T(8,128)S(1)}, s32[16,256]{1,0:T(8,128)}, u32[]{:S(2)}) copy-start(s32[16,256]{1,0:T(8,128)} %param.10) | copy-start | bytes 49156
  0.7 3.1 %copy-start.5 = (f32[16,16,256]{2,1,0:T(8,128)S(1)}, f32[16,16,256]{2,1,0:T(8,128)}, u32[]{:S(2)}) copy-start(f32[16,16,256]{2,1,0:T(8,128)} %param.11) | copy-start | bytes 786436
  3.9 12.1 %collective-permute-start.1 = (f32[81,4,256]{2,0,1:T(8,128)S(1)}, f32[81,4,256]{2,0,1:T(8,128)S(1)}, u32[]{:S(2)}, u32[]{:S(2)}) collective-permute-start(f32[81,4,256]{2,0,1:T(8,128)S(1)} %copy.22), channel_id=1, source_target_pairs={{8,0},{16,8},{24,16},{9,1},{17,9},{25,17},{10,2},{18,10},{26,18},{... | collective-permute-start | bytes 995336 | tf_op jit(solution)/shard_map/ppermute | solution.py:18
  7.4 16.3 %collective-permute-start = (f32[81,4,256]{2,0,1:T(8,128)S(1)}, f32[81,4,256]{2,0,1:T(8,128)S(1)}, u32[]{:S(2)}, u32[]{:S(2)}) collective-permute-start(f32[81,4,256]{2,0,1:T(8,128)S(1)} %copy.21), channel_id=1, source_target_pairs={{0,8},{8,16},{16,24},{1,9},{9,17},{17,25},{2,10},{10,18},{18,26},{... | collective-permute-start | bytes 995336 | tf_op jit(solution)/shard_map/ppermute | solution.py:17
  16.2 8.2 %copy-start = (f32[81,4,256]{2,1,0:T(4,128)}, f32[81,4,256]{2,1,0:T(4,128)S(1)}, u32[]{:S(2)}) copy-start(f32[81,4,256]{2,1,0:T(4,128)S(1)} %copy.24) | copy-start | bytes 995332
  23.8 0.7 %copy-start.2 = (f32[81,4,256]{2,1,0:T(4,128)}, f32[81,4,256]{2,1,0:T(4,128)S(1)}, u32[]{:S(2)}) copy-start(f32[81,4,256]{2,1,0:T(4,128)S(1)} %copy.23) | copy-start | bytes 995332
  24.9 5.0 %collective-permute-start.3 = (f32[81,24,4]{0,1,2:T(8,128)S(1)}, f32[81,24,4]{0,1,2:T(8,128)S(1)}, u32[]{:S(2)}, u32[]{:S(2)}) collective-permute-start(f32[81,24,4]{0,1,2:T(8,128)S(1)} %copy.26), channel_id=1, source_target_pairs={{1,0},{2,1},{3,2},{4,3},{5,4},{6,5},{7,6},{9,8},{10,9},{11,10},{12... | collective-permute-start | bytes 93320 | tf_op jit(solution)/shard_map/ppermute | solution.py:18
  27.3 5.4 %collective-permute-start.2 = (f32[81,24,4]{0,1,2:T(8,128)S(1)}, f32[81,24,4]{0,1,2:T(8,128)S(1)}, u32[]{:S(2)}, u32[]{:S(2)}) collective-permute-start(f32[81,24,4]{0,1,2:T(8,128)S(1)} %copy.25), channel_id=1, source_target_pairs={{0,1},{1,2},{2,3},{3,4},{4,5},{5,6},{6,7},{8,9},{9,10},{10,11},{11... | collective-permute-start | bytes 93320 | tf_op jit(solution)/shard_map/ppermute | solution.py:17
  33.2 1.0 %copy-start.1 = (f32[81,4,256]{2,1,0:T(4,128)S(1)}, f32[81,4,256]{2,1,0:T(4,128)}, u32[]{:S(2)}) copy-start(f32[81,4,256]{2,1,0:T(4,128)} %copy-done) | copy-start | bytes 995332
  33.2 1.1 %copy-start.3 = (f32[81,4,256]{2,1,0:T(4,128)S(1)}, f32[81,4,256]{2,1,0:T(4,128)}, u32[]{:S(2)}) copy-start(f32[81,4,256]{2,1,0:T(4,128)} %copy-done.2) | copy-start | bytes 995332
  57.1 1.0 %copy-start.4 = (f32[16,16,256]{2,1,0:T(8,128)S(1)}, f32[16,16,256]{2,1,0:T(8,128)}, u32[]{:S(2)}) copy-start(f32[16,16,256]{2,1,0:T(8,128)} %param.6) | copy-start | bytes 786436
  57.3 2.1 %copy-start.8 = (f32[16,16,256]{2,1,0:T(8,128)}, f32[16,16,256]{2,1,0:T(8,128)S(1)}, u32[]{:S(2)}) copy-start(f32[16,16,256]{2,1,0:T(8,128)S(1)} %constant_dynamic-update-slice_fusion.23) | copy-start | bytes 786436
where the time goes:
time: 59.7 us; the launch traced here: 59.4 us
  other arithmetic  22.5 us (38%)
  waiting for transfers between devices  16 us (27%)
  starting transfers between devices  10.4 us (17%)
  local copies, waits for them, and re-layouts  9.24 us (15%)
  between operations  1.31 us (2%)
    ppermute x2, waiting for transfers between devices, extended(): before = lax.ppermute(last, axis, up)  9.76 us
    unnamed x39, other arithmetic  8.81 us
    ppermute x2, waiting for transfers between devices, extended(): after = lax.ppermute(initial, axis, down)  6.2 us
    ppermute x2, starting transfers between devices, extended(): after = lax.ppermute(initial, axis, down)  5.28 us
    ppermute x2, starting transfers between devices, extended(): before = lax.ppermute(last, axis, up)  5.12 us
    unnamed x44, local copies, waits for them, and re-layouts  4.2 us
    mul x4, other arithmetic, flux_change(): open_face * (interval(face_speed, 2, extent - 1, along_axis) * (7.0 * (in...  2.94 us
    sub x2, other arithmetic, adjoint_explicit(): return middle + across + north_term - 2.0 * uptake * state_now * middle  2.53 us
  transfers between devices with their start and end apart: 4, of which 3 were waited for; matrix products, arithmetic and copies ran while one was open for 2% of the time, Pallas kernels for 0%

commit v1 on v0

v1 whole, which is shorter than its diff:
```python
import functools

import jax
import jax.numpy as jnp
from jax import lax
from jax.experimental import pallas as pl
from jax.experimental.pallas import tpu as pltpu
from jax.sharding import PartitionSpec as P

diffusivity = 0.1
uptake = 0.2
lanes = 128
sublanes = 8


def lane_tracer_after(k):
    return 4 * k


def lane_tracer_before(k):
    return (4 * k - 2) % lanes


def lane_weight_after(k):
    return 64 + 2 * k


def lane_weight_before(k):
    return 63 + 2 * k


def lane_carried(k):
    return 96 + k


def lane_speed(k):
    return 112 + k


lane_depth = 62


def turned(value, shift, axis):
    return pltpu.roll(value, shift % value.shape[axis], axis)


def lane_index(shape):
    return lax.broadcasted_iota(jnp.int32, shape, 1)


def row_index(shape):
    return lax.broadcasted_iota(jnp.int32, shape, 0)


def explicit_flux(c, speed, is_open, axis, size):
    behind = turned(c, 1, axis)
    outer = turned(c, -1, axis) + turned(c, 2, axis)
    flux = jnp.where(is_open, speed * (7.0 * (c + behind) - outer) - diffusivity * (c - behind), 0.0)
    change = flux - turned(flux, -1, axis)
    return lax.slice_in_dim(change, 0, size, axis=axis)


def reverse_flux(h, speed, is_open, halo_carried, in_halo, axis, size):
    jump = jnp.where(is_open, h - turned(h, 1, axis), 0.0)
    carried = speed * jump
    tail = lax.slice_in_dim(carried, size, carried.shape[axis], axis=axis)
    tail = jnp.where(in_halo, halo_carried, tail)
    carried = jnp.concatenate([lax.slice_in_dim(carried, 0, size, axis=axis), tail], axis=axis)
    spread = diffusivity * jump
    seven = 7.0 * carried
    total = (seven - spread) + turned(seven + spread, -1, axis) - turned(carried, 1, axis) - turned(carried, -2, axis)
    return lax.slice_in_dim(total, 0, size, axis=axis)


def pack_columns(k, c, h, speed, open_x, before, after):
    rows = c.shape[0]
    lane = lane_index((rows, lanes))
    c_first, c_last = c[:, :lanes], c[:, -lanes:]
    h_first, h_last = h[:, :lanes], h[:, -lanes:]
    s_first, s_last = speed[:, :lanes], speed[:, -lanes:]
    o_first, o_last = open_x[:, :lanes], open_x[:, -lanes:]
    g_first = jnp.where(o_first, s_first * (h_first - turned(h_first, 1, 1)), 0.0)
    g_last = jnp.where(o_last, s_last * (h_last - turned(h_last, 1, 1)), 0.0)
    at = lane_tracer_before(k)
    before = jnp.where((lane == at) | (lane == at + 1), turned(c_last, at - (lanes - 2), 1), before)
    at = lane_weight_before(k)
    before = jnp.where(lane == at, turned(h_last, at - (lanes - 1), 1), before)
    at = lane_carried(k)
    before = jnp.where(lane == at, turned(g_last, at - (lanes - 1), 1), before)
    after = jnp.where(lane == at, turned(g_first, at - 1, 1), after)
    at = lane_tracer_after(k)
    after = jnp.where((lane == at) | (lane == at + 1), turned(c_first, at, 1), after)
    at = lane_weight_after(k)
    after = jnp.where(lane == at, turned(h_first, at, 1), after)
    return before, after


def pack_rows(k, levels, c, h, speed, open_y, even, pay_even, pay_odd):
    size = c.shape[0]
    last = slice(size - sublanes, size)
    first = slice(0, sublanes)
    g_last = jnp.where(open_y[last], speed[last] * (h[last] - turned(h[last], 1, 0)), 0.0)
    g_first = jnp.where(open_y[first], speed[first] * (h[first] - turned(h[first], 1, 0)), 0.0)
    up = (c[size - 2 : size - 1], c[size - 1 :], h[size - 1 :], g_last[sublanes - 1 :])
    down = (c[0:1], c[1:2], h[0:1], g_first[1:2])
    for item in range(4):
        at = item * levels + k
        pay_even[at : at + 1, :] = jnp.where(even, up[item], down[item])
        pay_odd[at : at + 1, :] = jnp.where(even, down[item], up[item])


def parities():
    return lax.rem(lax.axis_index("group"), 2) == 0, lax.rem(lax.axis_index("tile"), 2) == 0


def factor_kernel(
    tracer, east, north, mixing, depth, sensitivity, inverse, weight, pay_even, pay_odd, pay_core, pay_chip, passed
):
    levels, rows, columns = tracer.shape
    even_y, even_x = parities()
    deep = depth[...]
    shallow_x = jnp.minimum(deep, turned(deep, 1, 1))
    shallow_y = jnp.minimum(deep, turned(deep, 1, 0))
    above = jnp.zeros((rows, columns), jnp.float32)
    share = above
    current = above
    for k in range(levels):
        below = jnp.where(k + 1 < deep, mixing[k], 0.0) if k < levels - 1 else jnp.zeros_like(above)
        inv = 1.0 / (1.0 + below + (above - above * share))
        current = (sensitivity[k] + above * current) * inv
        share = below * inv
        above = below
        inverse[k] = inv
        passed[k] = current
    lane = lane_index((rows, lanes))
    depth_float = deep.astype(jnp.float32)
    at_depth = lane == lane_depth
    before = jnp.where(at_depth, turned(depth_float[:, -lanes:], lane_depth - (lanes - 1), 1), 0.0)
    after = jnp.where(at_depth, turned(depth_float[:, :lanes], lane_depth, 1), 0.0)
    for k in range(levels - 1, -1, -1):
        if k < levels - 1:
            share = jnp.where(k + 1 < deep, mixing[k], 0.0) * inverse[k]
            current = passed[k] + share * current
        h = jnp.where(k < deep, current, 0.0)
        weight[k] = h
        c = tracer[k]
        speed_x = east[k] * (1.0 / 12.0)
        speed_y = north[k] * (1.0 / 12.0)
        before, after = pack_columns(k, c, h, speed_x, k < shallow_x, before, after)
        at = lane_speed(k)
        after = jnp.where(lane == at, turned(speed_x[:, :lanes], at, 1), after)
        pack_rows(k, levels, c, h, speed_y, k < shallow_y, even_y, pay_even, pay_odd)
        at = 4 * levels + k
        pay_even[at : at + 1, :] = speed_y[0:1]
        pay_odd[at : at + 1, :] = speed_y[0:1]
    at = 5 * levels
    depth_up = jnp.broadcast_to(depth_float[rows - 1 :], (sublanes, columns))
    depth_down = jnp.broadcast_to(depth_float[0:1], (sublanes, columns))
    pay_even[at : at + sublanes, :] = jnp.where(even_y, depth_up, depth_down)
    pay_odd[at : at + sublanes, :] = jnp.where(even_y, depth_down, depth_up)
    pay_core[...] = jnp.where(even_x, before, after)
    pay_chip[...] = jnp.where(even_x, after, before)


def halo_rows(k, item, levels, lower, upper, size):
    columns = lower.shape[1]
    row = row_index((sublanes, columns))

    def line(ref, which):
        at = which * levels + k
        return jnp.broadcast_to(ref[at : at + 1, :], (sublanes, columns))

    if item == "tracer":
        tile = jnp.where(row == 0, line(upper, 0), line(upper, 1))
        return jnp.where(row == sublanes - 2, line(lower, 0), jnp.where(row == sublanes - 1, line(lower, 1), tile))
    if item == "weight":
        return jnp.where(row == 0, line(upper, 2), line(lower, 2))
    if item == "carried":
        return jnp.where(row == 1, line(upper, 3), line(lower, 3))
    return line(upper, 4)


def halo_lanes(k, merged, before, after):
    lane = lane_index(merged.shape)
    c = turned(merged, -lane_tracer_after(k), 1)
    h = turned(merged, -lane_weight_after(k), 1)
    at = lane_carried(k)
    g = jnp.where(lane == 1, turned(after, 1 - at, 1), turned(before, lanes - 1 - at, 1))
    return c, h, g


def merge_lanes(before, after):
    lane = lane_index(before.shape)
    c_after = (lane < 62) & (lax.rem(lane, 4) < 2)
    h_after = (lane > 62) & (lane < 96) & (lax.rem(lane, 2) == 0)
    return jnp.where(c_after | h_after, after, before)


def take_rows(even, got_even, got_odd, lower, upper):
    a, b = got_even[...], got_odd[...]
    lower[...] = jnp.where(even, b, a)
    upper[...] = jnp.where(even, a, b)


def take_lanes(even, got_core, got_chip):
    a, b = got_core[...], got_chip[...]
    return jnp.where(even, b, a), jnp.where(even, a, b)


def shallow_faces(deep, before, after, lower, upper, levels):
    rows, columns = deep.shape
    lane = lane_index((rows, lanes))
    tail = jnp.where(lane == 0, turned(after, -lane_depth, 1), turned(before, lanes - 1 - lane_depth, 1))
    ring_x = jnp.concatenate([deep, tail], axis=1)
    at = 5 * levels
    row = row_index((sublanes, columns))
    tail = jnp.where(row == 0, upper[at : at + sublanes, :], lower[at : at + sublanes, :])
    ring_y = jnp.concatenate([deep, tail], axis=0)
    return jnp.minimum(ring_x, turned(ring_x, 1, 1)), jnp.minimum(ring_y, turned(ring_y, 1, 0))


def step_level(k, levels, c, h, east_k, north_k, faces, statics, halos):
    rows, columns = c.shape
    shallow_x, shallow_y = faces
    lower1, upper1, after1 = statics
    lower, upper, merged, before, after = halos
    open_x, open_y = k < shallow_x, k < shallow_y
    c_tail, h_tail, g_tail = halo_lanes(k, merged, before, after)
    speed_x = jnp.concatenate([east_k * (1.0 / 12.0), turned(after1, -lane_speed(k), 1)], axis=1)
    speed_y = jnp.concatenate([north_k * (1.0 / 12.0), halo_rows(k, "speed", levels, lower1, upper1, rows)], axis=0)
    lane = lane_index((rows, lanes))
    row = row_index((sublanes, columns))
    lanes_given = (lane == 1) | (lane == lanes - 1)
    rows_given = (row == 1) | (row == sublanes - 1)
    c_x = jnp.concatenate([c, c_tail], axis=1)
    forward = explicit_flux(c_x, speed_x, open_x, 1, columns)
    c_y = jnp.concatenate([c, halo_rows(k, "tracer", levels, lower, upper, rows)], axis=0)
    forward = forward + explicit_flux(c_y, speed_y, open_y, 0, rows)
    h_x = jnp.concatenate([h, h_tail], axis=1)
    backward = reverse_flux(h_x, speed_x, open_x, g_tail, lanes_given, 1, columns)
    h_y = jnp.concatenate([h, halo_rows(k, "weight", levels, lower, upper, rows)], axis=0)
    given = halo_rows(k, "carried", levels, lower, upper, rows)
    backward = backward + reverse_flux(h_y, speed_y, open_y, given, rows_given, 0, rows)
    return forward, h + backward


def first_kernel(
    tracer, east, north, mixing, depth, inverse, weight, got_even, got_odd, got_core, got_chip,
    state, weight_next, pay_even, pay_odd, pay_core, pay_chip, passed, linear, lower, upper,
):
    levels, rows, columns = tracer.shape
    even_y, even_x = parities()
    take_rows(even_y, got_even, got_odd, lower, upper)
    before, after = take_lanes(even_x, got_core, got_chip)
    merged = merge_lanes(before, after)
    deep = depth[...]
    depth_float = deep.astype(jnp.float32)
    faces = shallow_faces(depth_float, before, after, lower, upper, levels)
    current = jnp.zeros((rows, columns), jnp.float32)
    above = current
    for k in range(levels):
        c, h = tracer[k], weight[k]
        forward, back = step_level(
            k, levels, c, h, east[k], north[k], faces, (lower, upper, after), (lower, upper, merged, before, after)
        )
        linear[k] = back
        right = jnp.where(k < deep, c + forward - uptake * c * c, 0.0)
        current = (right + above * current) * inverse[k]
        passed[k] = current
        if k < levels - 1:
            above = jnp.where(k + 1 < deep, mixing[k], 0.0)
    state[levels - 1] = current
    for k in range(levels - 2, -1, -1):
        current = passed[k] + (jnp.where(k + 1 < deep, mixing[k], 0.0) * inverse[k]) * current
        state[k] = current
    current = jnp.zeros((rows, columns), jnp.float32)
    for k in range(levels):
        right = linear[k] - (2.0 * uptake) * state[k] * weight[k]
        if k > 0:
            right = right + jnp.where(k < deep, mixing[k - 1], 0.0) * current
        current = right * inverse[k]
        passed[k] = current
    packed_before = jnp.zeros((rows, lanes), jnp.float32)
    packed_after = packed_before
    shallow_x, shallow_y = faces[0][:, :columns], faces[1][:rows]
    for k in range(levels - 1, -1, -1):
        if k < levels - 1:
            current = passed[k] + (jnp.where(k + 1 < deep, mixing[k], 0.0) * inverse[k]) * current
        h = jnp.where(k < deep, current, 0.0)
        weight_next[k] = h
        c = state[k]
        packed_before, packed_after = pack_columns(
            k, c, h, east[k] * (1.0 / 12.0), k < shallow_x, packed_before, packed_after
        )
        pack_rows(k, levels, c, h, north[k] * (1.0 / 12.0), k < shallow_y, even_y, pay_even, pay_odd)
    pay_core[...] = jnp.where(even_x, packed_before, packed_after)
    pay_chip[...] = jnp.where(even_x, packed_after, packed_before)


def second_kernel(
    tracer, east, north, mixing, depth, inverse, state, weight, got1_even, got1_odd, got1_core, got1_chip,
    got_even, got_odd, got_core, got_chip, final, adjoint, passed, lower1, upper1, lower, upper,
):
    levels, rows, columns = tracer.shape
    even_y, even_x = parities()
    take_rows(even_y, got1_even, got1_odd, lower1, upper1)
    take_rows(even_y, got_even, got_odd, lower, upper)
    before1, after1 = take_lanes(even_x, got1_core, got1_chip)
    before, after = take_lanes(even_x, got_core, got_chip)
    merged = merge_lanes(before, after)
    deep = depth[...]
    faces = shallow_faces(deep.astype(jnp.float32), before1, after1, lower1, upper1, levels)
    current = jnp.zeros((rows, columns), jnp.float32)
    above = current
    for k in range(levels):
        c, h = state[k], weight[k]
        forward, back = step_level(
            k, levels, c, h, east[k], north[k], faces, (lower1, upper1, after1), (lower, upper, merged, before, after)
        )
        adjoint[k] = back - (2.0 * uptake) * tracer[k] * h
        right = jnp.where(k < deep, c + forward - uptake * c * c, 0.0)
        current = (right + above * current) * inverse[k]
        passed[k] = current
        if k < levels - 1:
            above = jnp.where(k + 1 < deep, mixing[k], 0.0)
    final[levels - 1] = current
    for k in range(levels - 2, -1, -1):
        current = passed[k] + (jnp.where(k + 1 < deep, mixing[k], 0.0) * inverse[k]) * current
        final[k] = current


def pairs(axis, parity):
    devices = lax.axis_size(axis)
    swaps = []
    for i in range(parity, devices - 1, 2):
        swaps += [(i, i + 1), (i + 1, i)]
    return swaps


def exchange(pay_even, pay_odd, pay_core, pay_chip):
    got_core = lax.ppermute(pay_core, "tile", pairs("tile", 0))
    got_chip = lax.ppermute(pay_chip, "tile", pairs("tile", 1))
    got_odd = lax.ppermute(pay_odd, "group", pairs("group", 1))
    got_even = lax.ppermute(pay_even, "group", pairs("group", 0))
    return got_even, got_odd, got_core, got_chip


def shards(tracer, east_speed, north_speed, mixing, depth_levels, sensitivity):
    levels, rows, columns = tracer.shape
    f32 = jnp.float32
    field = jax.ShapeDtypeStruct((levels, rows, columns), f32)
    edge = jax.ShapeDtypeStruct((rows, lanes), f32)
    first_size = 5 * levels + sublanes
    second_size = 4 * levels
    block = pltpu.VMEM((levels, rows, columns), f32)
    params = pltpu.CompilerParams(vmem_limit_bytes=32 * 1024 * 1024)

    def lines(size):
        return jax.ShapeDtypeStruct((size, columns), f32)

    def space(size):
        return pltpu.VMEM((size, columns), f32)

    inverse, weight, *messages = pl.pallas_call(
        factor_kernel,
        out_shape=(field, field, lines(first_size), lines(first_size), edge, edge),
        scratch_shapes=[block],
        compiler_params=params,
    )(tracer, east_speed, north_speed, mixing, depth_levels, sensitivity)
    got1 = exchange(*messages)
    state, weight_next, *messages = pl.pallas_call(
        first_kernel,
        out_shape=(field, field, lines(second_size), lines(second_size), edge, edge),
        scratch_shapes=[block, block, space(first_size), space(first_size)],
        compiler_params=params,
    )(tracer, east_speed, north_speed, mixing, depth_levels, inverse, weight, *got1)
    got2 = exchange(*messages)
    final, adjoint = pl.pallas_call(
        second_kernel,
        out_shape=(field, field),
        scratch_shapes=[block, space(first_size), space(first_size), space(second_size), space(second_size)],
        compiler_params=params,
    )(tracer, east_speed, north_speed, mixing, depth_levels, inverse, state, weight_next, *got1, *got2)
    return final, adjoint


def solution(mesh):
    block = P(None, "group", "tile")
    in_specs = (block, block, block, block, P("group", "tile"), block)
    return jax.shard_map(shards, mesh=mesh, in_specs=in_specs, out_specs=(block, block), check_vma=False)
```

time: 59.7 us -> 35.5 us (0.59)
  the two profiles are of different devices: /device:TPU:12 before, /device:TPU:13 now
where the time goes in v1:
time: 35.5 us; the launch traced here: 35.1 us
  starting transfers between devices  15.6 us (44%)
  Pallas kernels  9.89 us (28%)
  local copies, waits for them, and re-layouts  5.46 us (15%)
  waiting for transfers between devices  3.51 us (10%)
  between operations  0.72 us (2%)
    ppermute x2, starting transfers between devices, exchange(): got_chip = lax.ppermute(pay_chip, 'tile', pairs('tile', 1))  6.39 us
    ppermute x2, starting transfers between devices, exchange(): got_odd = lax.ppermute(pay_odd, 'group', pairs('group', 1))  6.17 us
    unnamed x14, local copies, waits for them, and re-layouts  5.46 us
    pallas_call x1, Pallas kernels, shards(): pl.pallas_call(first_kernel, out_shape=(field, field, lines(second_size),...  5.03 us
    pallas_call x1, Pallas kernels, shards(): pl.pallas_call(second_kernel, out_shape=(field, field), scratch_shapes=[b...  4.31 us
    ppermute x2, waiting for transfers between devices, exchange(): got_chip = lax.ppermute(pay_chip, 'tile', pairs('tile', 1))  3.49 us
    ppermute x2, starting transfers between devices, exchange(): got_core = lax.ppermute(pay_core, 'tile', pairs('tile', 0))  1.67 us
    ppermute x2, starting transfers between devices, exchange(): got_even = lax.ppermute(pay_even, 'group', pairs('group', 0))  1.35 us
  transfers between devices with their start and end apart: 8, of which 2 were waited for; matrix products, arithmetic and copies ran while one was open for 0% of the time, Pallas kernels for 0%

profile of v1, /device:TPU:13, one launch (start us, length us, event | category | flops | bytes accessed | tf_op | source)
XLA Modules:
  0.0 35.1 jit_solution(16307048224318078820)
XLA Ops:
  0.6 0.0 copy-start
  0.6 0.9 %copy-done = f32[16,16,256]{2,1,0:T(8,128)S(1)} copy-done((f32[16,16,256]{2,1,0:T(8,128)S(1)}, f32[16,16,256]{2,1,0:T(8,128)}, u32[]{:S(2)}) %copy-start) | copy-done | bytes 262168
  1.6 0.0 copy-start.1
  1.6 0.9 %copy-done.1 = f32[16,16,256]{2,1,0:T(8,128)S(1)} copy-done((f32[16,16,256]{2,1,0:T(8,128)S(1)}, f32[16,16,256]{2,1,0:T(8,128)}, u32[]{:S(2)}) %copy-start.1) | copy-done | bytes 262168
  2.5 0.0 copy-start.2
  2.5 0.9 %copy-done.2 = f32[16,16,256]{2,1,0:T(8,128)S(1)} copy-done((f32[16,16,256]{2,1,0:T(8,128)S(1)}, f32[16,16,256]{2,1,0:T(8,128)}, u32[]{:S(2)}) %copy-start.2) | copy-done | bytes 262168
  3.5 0.0 copy-start.3
  3.5 0.9 %copy-done.3 = f32[15,16,256]{2,1,0:T(8,128)S(1)} copy-done((f32[15,16,256]{2,1,0:T(8,128)S(1)}, f32[15,16,256]{2,1,0:T(8,128)}, u32[]{:S(2)}) %copy-start.3) | copy-done | bytes 245784
  4.4 0.0 copy-start.4
  4.4 0.9 %copy-done.4 = f32[16,16,256]{2,1,0:T(8,128)S(1)} copy-done((f32[16,16,256]{2,1,0:T(8,128)S(1)}, f32[16,16,256]{2,1,0:T(8,128)}, u32[]{:S(2)}) %copy-start.4) | copy-done | bytes 262168
  5.4 0.0 copy-start.5
  5.4 0.7 %copy-done.5 = s32[16,256]{1,0:T(8,128)S(1)} copy-done((s32[16,256]{1,0:T(8,128)S(1)}, s32[16,256]{1,0:T(8,128)}, u32[]{:S(2)}) %copy-start.5) | copy-done | bytes 16408
  6.1 0.0 copy-start.6
  6.1 0.5 %shard_map.77 = (f32[16,16,256]{2,1,0:T(8,128)S(1)}, f32[16,16,256]{2,1,0:T(8,128)S(1)}, f32[88,256]{1,0:T(8,128)S(1)}, f32[88,256]{1,0:T(8,128)S(1)}, f32[16,128]{1,0:T(8,128)S(1)}, /*index=5*/f32[16,128]{1,0:T(8,128)S(1)}) custom-call(f32[16,16,256]{2,1,0:T(8,128)S(1)} %copy-done, f32[16,16,256]{2,1,0:T(8,128)S(1)} %copy-done.1, ...), custom_call_target="tpu_custom_call" | custom-call | tf_op jit(solution)/shard_map/pallas_call | solution.py:364
  6.7 1.3 %collective-permute-start = (f32[88,256]{1,0:T(8,128)S(1)}, f32[88,256]{1,0:T(8,128)S(1)}, u32[]{:S(2)}, u32[]{:S(2)}) collective-permute-start(f32[88,256]{1,0:T(8,128)S(1)} %get-tuple-element.16), channel_id=1, source_target_pairs={{0,8},{8,0},{16,24},{24,16},{1,9},{9,1},{17,25},{25,17},{2,10},{10... | collective-permute-start | bytes 270344 | tf_op jit(solution)/shard_map/ppermute | solution.py:344
  7.9 2.1 %collective-permute-start.1 = (f32[88,256]{1,0:T(8,128)S(1)}, f32[88,256]{1,0:T(8,128)S(1)}, u32[]{:S(2)}, u32[]{:S(2)}) collective-permute-start(f32[88,256]{1,0:T(8,128)S(1)} %get-tuple-element.17), channel_id=1, source_target_pairs={{8,16},{16,8},{9,17},{17,9},{10,18},{18,10},{11,19},{19,11},{12,20... | collective-permute-start | bytes 270344 | tf_op jit(solution)/shard_map/ppermute | solution.py:343
  10.0 1.3 %collective-permute-start.2 = (f32[16,128]{1,0:T(8,128)S(1)}, f32[16,128]{1,0:T(8,128)S(1)}, u32[]{:S(2)}, u32[]{:S(2)}) collective-permute-start(f32[16,128]{1,0:T(8,128)S(1)} %get-tuple-element.18), channel_id=1, source_target_pairs={{0,1},{1,0},{2,3},{3,2},{4,5},{5,4},{6,7},{7,6},{8,9},{9,8},{10,11... | collective-permute-start | bytes 24584 | tf_op jit(solution)/shard_map/ppermute | solution.py:341
  11.3 3.1 %collective-permute-start.3 = (f32[16,128]{1,0:T(8,128)S(1)}, f32[16,128]{1,0:T(8,128)S(1)}, u32[]{:S(2)}, u32[]{:S(2)}) collective-permute-start(f32[16,128]{1,0:T(8,128)S(1)} %get-tuple-element.19), channel_id=1, source_target_pairs={{1,2},{2,1},{3,4},{4,3},{5,6},{6,5},{9,10},{10,9},{11,12},{12,11},... | collective-permute-start | bytes 24584 | tf_op jit(solution)/shard_map/ppermute | solution.py:342
  14.4 0.0 collective-permute-done.2.got_core.got1_core
  14.5 1.8 %collective-permute-done.3.got_chip.got1_chip = f32[16,128]{1,0:T(8,128)S(1)} collective-permute-done((f32[16,128]{1,0:T(8,128)S(1)}, f32[16,128]{1,0:T(8,128)S(1)}, u32[]{:S(2)}, u32[]{:S(2)}) %collective-permute-start.3) | collective-permute-done | bytes 8224 | tf_op jit(solution)/shard_map/ppermute | solution.py:342
  16.3 0.0 collective-permute-done.got_even.got1_even
  16.3 0.0 collective-permute-done.1.got_odd.got1_odd
  16.3 0.0 copy-done.6
  16.3 5.0 %shard_map.78 = (f32[16,16,256]{2,1,0:T(8,128)S(1)}, f32[16,16,256]{2,1,0:T(8,128)S(1)}, f32[64,256]{1,0:T(8,128)S(1)}, f32[64,256]{1,0:T(8,128)S(1)}, f32[16,128]{1,0:T(8,128)S(1)}, /*index=5*/f32[16,128]{1,0:T(8,128)S(1)}) custom-call(f32[16,16,256]{2,1,0:T(8,128)S(1)} %copy-done, f32[16,16,256]{2,1,0:T(8,128)S(1)} %copy-done.1, ...), custom_call_target="tpu_custom_call" | custom-call | tf_op jit(solution)/shard_map/pallas_call | solution.py:371
  21.3 0.1 collective-permute-start.4
  21.4 4.1 %collective-permute-start.5 = (f32[64,256]{1,0:T(8,128)S(1)}, f32[64,256]{1,0:T(8,128)S(1)}, u32[]{:S(2)}, u32[]{:S(2)}) collective-permute-start(f32[64,256]{1,0:T(8,128)S(1)} %get-tuple-element.23), channel_id=1, source_target_pairs={{8,16},{16,8},{9,17},{17,9},{10,18},{18,10},{11,19},{19,11},{12,20... | collective-permute-start | bytes 196616 | tf_op jit(solution)/shard_map/ppermute | solution.py:343
  25.5 0.4 %collective-permute-start.6 = (f32[16,128]{1,0:T(8,128)S(1)}, f32[16,128]{1,0:T(8,128)S(1)}, u32[]{:S(2)}, u32[]{:S(2)}) collective-permute-start(f32[16,128]{1,0:T(8,128)S(1)} %get-tuple-element.24), channel_id=1, source_target_pairs={{0,1},{1,0},{2,3},{3,2},{4,5},{5,4},{6,7},{7,6},{8,9},{9,8},{10,11... | collective-permute-start | bytes 24584 | tf_op jit(solution)/shard_map/ppermute | solution.py:341
  25.9 3.3 %collective-permute-start.7 = (f32[16,128]{1,0:T(8,128)S(1)}, f32[16,128]{1,0:T(8,128)S(1)}, u32[]{:S(2)}, u32[]{:S(2)}) collective-permute-start(f32[16,128]{1,0:T(8,128)S(1)} %get-tuple-element.25), channel_id=1, source_target_pairs={{1,2},{2,1},{3,4},{4,3},{5,6},{6,5},{9,10},{10,9},{11,12},{12,11},... | collective-permute-start | bytes 24584 | tf_op jit(solution)/shard_map/ppermute | solution.py:342
  29.2 0.0 collective-permute-done.6.got_core
  29.2 1.7 %collective-permute-done.7.got_chip = f32[16,128]{1,0:T(8,128)S(1)} collective-permute-done((f32[16,128]{1,0:T(8,128)S(1)}, f32[16,128]{1,0:T(8,128)S(1)}, u32[]{:S(2)}, u32[]{:S(2)}) %collective-permute-start.7) | collective-permute-done | bytes 8224 | tf_op jit(solution)/shard_map/ppermute | solution.py:342
  30.8 0.0 collective-permute-done.4.got_even
  30.8 0.0 collective-permute-done.5.got_odd
  30.8 4.3 %shard_map.79 = (f32[16,16,256]{2,1,0:T(8,128)}, f32[16,16,256]{2,1,0:T(8,128)}) custom-call(f32[16,16,256]{2,1,0:T(8,128)S(1)} %copy-done, f32[16,16,256]{2,1,0:T(8,128)S(1)} %copy-done.1, f32[16,16,256]{2,1,0:T(8,128)S(1)} %copy-done.2, f32[15,16,256]{2,1,0:T(8,128)S(1)} %copy-done.3, s32[16,256]{1,0:T(8,128)S(1)} %copy-done.6, ...), custom_call_target="tpu_custom_call" | custom-call | tf_op jit(solution)/shard_map/pallas_call | solution.py:378
Async XLA Ops:
  0.6 1.0 %copy-start = (f32[16,16,256]{2,1,0:T(8,128)S(1)}, f32[16,16,256]{2,1,0:T(8,128)}, u32[]{:S(2)}) copy-start(f32[16,16,256]{2,1,0:T(8,128)} %tracer.5) | copy-start | bytes 786436
  1.6 0.9 %copy-start.1 = (f32[16,16,256]{2,1,0:T(8,128)S(1)}, f32[16,16,256]{2,1,0:T(8,128)}, u32[]{:S(2)}) copy-start(f32[16,16,256]{2,1,0:T(8,128)} %east.5) | copy-start | bytes 786436
  2.5 0.9 %copy-start.2 = (f32[16,16,256]{2,1,0:T(8,128)S(1)}, f32[16,16,256]{2,1,0:T(8,128)}, u32[]{:S(2)}) copy-start(f32[16,16,256]{2,1,0:T(8,128)} %north.5) | copy-start | bytes 786436
  3.5 0.9 %copy-start.3 = (f32[15,16,256]{2,1,0:T(8,128)S(1)}, f32[15,16,256]{2,1,0:T(8,128)}, u32[]{:S(2)}) copy-start(f32[15,16,256]{2,1,0:T(8,128)} %mixing.5) | copy-start | bytes 737284
  4.4 0.9 %copy-start.4 = (f32[16,16,256]{2,1,0:T(8,128)S(1)}, f32[16,16,256]{2,1,0:T(8,128)}, u32[]{:S(2)}) copy-start(f32[16,16,256]{2,1,0:T(8,128)} %sensitivity.1) | copy-start | bytes 786436
  5.4 0.7 %copy-start.5 = (s32[16,256]{1,0:T(8,128)S(1)}, s32[16,256]{1,0:T(8,128)}, u32[]{:S(2)}) copy-start(s32[16,256]{1,0:T(8,128)} %depth.5) | copy-start | bytes 49156
  6.1 10.2 %copy-start.6 = (s32[16,256]{1,0:T(8,128)S(1)}, s32[16,256]{1,0:T(8,128)}, u32[]{:S(2)}) copy-start(s32[16,256]{1,0:T(8,128)} %depth.5) | copy-start | bytes 49156
  6.7 9.6 %collective-permute-start = (f32[88,256]{1,0:T(8,128)S(1)}, f32[88,256]{1,0:T(8,128)S(1)}, u32[]{:S(2)}, u32[]{:S(2)}) collective-permute-start(f32[88,256]{1,0:T(8,128)S(1)} %get-tuple-element.16), channel_id=1, source_target_pairs={{0,8},{8,0},{16,24},{24,16},{1,9},{9,1},{17,25},{25,17},{2,10},{10... | collective-permute-start | bytes 270344 | tf_op jit(solution)/shard_map/ppermute | solution.py:344
  7.9 8.4 %collective-permute-start.1 = (f32[88,256]{1,0:T(8,128)S(1)}, f32[88,256]{1,0:T(8,128)S(1)}, u32[]{:S(2)}, u32[]{:S(2)}) collective-permute-start(f32[88,256]{1,0:T(8,128)S(1)} %get-tuple-element.17), channel_id=1, source_target_pairs={{8,16},{16,8},{9,17},{17,9},{10,18},{18,10},{11,19},{19,11},{12,20... | collective-permute-start | bytes 270344 | tf_op jit(solution)/shard_map/ppermute | solution.py:343
  10.0 4.4 %collective-permute-start.2 = (f32[16,128]{1,0:T(8,128)S(1)}, f32[16,128]{1,0:T(8,128)S(1)}, u32[]{:S(2)}, u32[]{:S(2)}) collective-permute-start(f32[16,128]{1,0:T(8,128)S(1)} %get-tuple-element.18), channel_id=1, source_target_pairs={{0,1},{1,0},{2,3},{3,2},{4,5},{5,4},{6,7},{7,6},{8,9},{9,8},{10,11... | collective-permute-start | bytes 24584 | tf_op jit(solution)/shard_map/ppermute | solution.py:341
  11.3 5.0 %collective-permute-start.3 = (f32[16,128]{1,0:T(8,128)S(1)}, f32[16,128]{1,0:T(8,128)S(1)}, u32[]{:S(2)}, u32[]{:S(2)}) collective-permute-start(f32[16,128]{1,0:T(8,128)S(1)} %get-tuple-element.19), channel_id=1, source_target_pairs={{1,2},{2,1},{3,4},{4,3},{5,6},{6,5},{9,10},{10,9},{11,12},{12,11},... | collective-permute-start | bytes 24584 | tf_op jit(solution)/shard_map/ppermute | solution.py:342
  21.3 9.5 %collective-permute-start.4 = (f32[64,256]{1,0:T(8,128)S(1)}, f32[64,256]{1,0:T(8,128)S(1)}, u32[]{:S(2)}, u32[]{:S(2)}) collective-permute-start(f32[64,256]{1,0:T(8,128)S(1)} %get-tuple-element.22), channel_id=1, source_target_pairs={{0,8},{8,0},{16,24},{24,16},{1,9},{9,1},{17,25},{25,17},{2,10},{10... | collective-permute-start | bytes 196616 | tf_op jit(solution)/shard_map/ppermute | solution.py:344
  21.4 9.4 %collective-permute-start.5 = (f32[64,256]{1,0:T(8,128)S(1)}, f32[64,256]{1,0:T(8,128)S(1)}, u32[]{:S(2)}, u32[]{:S(2)}) collective-permute-start(f32[64,256]{1,0:T(8,128)S(1)} %get-tuple-element.23), channel_id=1, source_target_pairs={{8,16},{16,8},{9,17},{17,9},{10,18},{18,10},{11,19},{19,11},{12,20... | collective-permute-start | bytes 196616 | tf_op jit(solution)/shard_map/ppermute | solution.py:343
  25.5 3.7 %collective-permute-start.6 = (f32[16,128]{1,0:T(8,128)S(1)}, f32[16,128]{1,0:T(8,128)S(1)}, u32[]{:S(2)}, u32[]{:S(2)}) collective-permute-start(f32[16,128]{1,0:T(8,128)S(1)} %get-tuple-element.24), channel_id=1, source_target_pairs={{0,1},{1,0},{2,3},{3,2},{4,5},{5,4},{6,7},{7,6},{8,9},{9,8},{10,11... | collective-permute-start | bytes 24584 | tf_op jit(solution)/shard_map/ppermute | solution.py:341
  25.9 5.0 %collective-permute-start.7 = (f32[16,128]{1,0:T(8,128)S(1)}, f32[16,128]{1,0:T(8,128)S(1)}, u32[]{:S(2)}, u32[]{:S(2)}) collective-permute-start(f32[16,128]{1,0:T(8,128)S(1)} %get-tuple-element.25), channel_id=1, source_target_pairs={{1,2},{2,1},{3,4},{4,3},{5,6},{6,5},{9,10},{10,9},{11,12},{12,11},... | collective-permute-start | bytes 24584 | tf_op jit(solution)/shard_map/ppermute | solution.py:342

commit v2 on v1

--- a/solution.py
+++ b/solution.py
@@ -52,24 +52,45 @@
     return lax.broadcasted_iota(jnp.int32, shape, 0)
 
 
-def explicit_flux(c, speed, is_open, axis, size):
-    behind = turned(c, 1, axis)
-    outer = turned(c, -1, axis) + turned(c, 2, axis)
-    flux = jnp.where(is_open, speed * (7.0 * (c + behind) - outer) - diffusivity * (c - behind), 0.0)
-    change = flux - turned(flux, -1, axis)
-    return lax.slice_in_dim(change, 0, size, axis=axis)
-
-
-def reverse_flux(h, speed, is_open, halo_carried, in_halo, axis, size):
-    jump = jnp.where(is_open, h - turned(h, 1, axis), 0.0)
-    carried = speed * jump
-    tail = lax.slice_in_dim(carried, size, carried.shape[axis], axis=axis)
-    tail = jnp.where(in_halo, halo_carried, tail)
-    carried = jnp.concatenate([lax.slice_in_dim(carried, 0, size, axis=axis), tail], axis=axis)
-    spread = diffusivity * jump
-    seven = 7.0 * carried
-    total = (seven - spread) + turned(seven + spread, -1, axis) - turned(carried, 1, axis) - turned(carried, -2, axis)
-    return lax.slice_in_dim(total, 0, size, axis=axis)
+def split(value, axis):
+    step = lanes if axis == 2 else sublanes
+    return [lax.slice_in_dim(value, i, i + step, axis=axis) for i in range(0, value.shape[axis], step)]
+
+
+def shifted(ring, shift, axis, count):
+    span = ring[0].shape[axis]
+    moved = [turned(tile, shift, axis) for tile in ring]
+    place = lax.broadcasted_iota(jnp.int32, ring[0].shape, axis)
+    if shift > 0:
+        return [jnp.where(place < shift, moved[i - 1], moved[i]) for i in range(count)]
+    return [jnp.where(place >= span + shift, moved[(i + 1) % len(ring)], moved[i]) for i in range(count)]
+
+
+def explicit_flux(ring, speeds, opens, axis):
+    full = len(ring)
+    behind = shifted(ring, 1, axis, full)
+    ahead = shifted(ring, -1, axis, full)
+    far = shifted(ring, 2, axis, full)
+    flux = [
+        jnp.where(o, s * (7.0 * (c + b) - (a + f)) - diffusivity * (c - b), 0.0)
+        for c, b, a, f, s, o in zip(ring, behind, ahead, far, speeds, opens)
+    ]
+    following = shifted(flux, -1, axis, full - 1)
+    return [g - n for g, n in zip(flux, following)]
+
+
+def reverse_flux(ring, speeds, opens, halo_carried, in_halo, axis):
+    full = len(ring)
+    behind = shifted(ring, 1, axis, full)
+    jump = [jnp.where(o, h - b, 0.0) for h, b, o in zip(ring, behind, opens)]
+    carried = [s * j for s, j in zip(speeds, jump)]
+    carried[-1] = jnp.where(in_halo, halo_carried, carried[-1])
+    seven = [7.0 * g for g in carried]
+    spread = [diffusivity * j for j in jump]
+    ahead = shifted([a + b for a, b in zip(seven, spread)], -1, axis, full - 1)
+    back = shifted(carried, 1, axis, full - 1)
+    far = shifted(carried, -2, axis, full - 1)
+    return [(a - b) + c - d - e for a, b, c, d, e in zip(seven, spread, ahead, back, far)]
 
 
 def pack_columns(k, c, h, speed, open_x, before, after):
@@ -114,8 +135,23 @@
 
 
 def factor_kernel(
-    tracer, east, north, mixing, depth, sensitivity, inverse, weight, pay_even, pay_odd, pay_core, pay_chip, passed
+    tracer_far, east_far, north_far, mixing_far, depth_far, sensitivity_far,
+    tracer, east, north, mixing, depth, inverse, weight, pay_even, pay_odd, pay_core, pay_chip,
+    sensitivity, passed, arrived,
 ):
+    order = (
+        (depth_far, depth),
+        (mixing_far, mixing),
+        (sensitivity_far, sensitivity),
+        (tracer_far, tracer),
+        (east_far, east),
+        (north_far, north),
+    )
+    copies = [pltpu.make_async_copy(far, near, arrived.at[i]) for i, (far, near) in enumerate(order)]
+    for copy in copies:
+        copy.start()
+    for copy in copies[:3]:
+        copy.wait()
     levels, rows, columns = tracer.shape
     even_y, even_x = parities()
     deep = depth[...]
@@ -137,6 +173,8 @@
     at_depth = lane == lane_depth
     before = jnp.where(at_depth, turned(depth_float[:, -lanes:], lane_depth - (lanes - 1), 1), 0.0)
     after = jnp.where(at_depth, turned(depth_float[:, :lanes], lane_depth, 1), 0.0)
+    for copy in copies[3:]:
+        copy.wait()
     for k in range(levels - 1, -1, -1):
         if k < levels - 1:
             share = jnp.where(k + 1 < deep, mixing[k], 0.0) * inverse[k]
@@ -219,29 +257,43 @@
     return jnp.minimum(ring_x, turned(ring_x, 1, 1)), jnp.minimum(ring_y, turned(ring_y, 1, 0))
 
 
-def step_level(k, levels, c, h, east_k, north_k, faces, statics, halos):
-    rows, columns = c.shape
+def step_levels(first, levels, c, h, east_part, north_part, faces, statics, halos):
+    count, rows, columns = c.shape
     shallow_x, shallow_y = faces
     lower1, upper1, after1 = statics
     lower, upper, merged, before, after = halos
-    open_x, open_y = k < shallow_x, k < shallow_y
-    c_tail, h_tail, g_tail = halo_lanes(k, merged, before, after)
-    speed_x = jnp.concatenate([east_k * (1.0 / 12.0), turned(after1, -lane_speed(k), 1)], axis=1)
-    speed_y = jnp.concatenate([north_k * (1.0 / 12.0), halo_rows(k, "speed", levels, lower1, upper1, rows)], axis=0)
-    lane = lane_index((rows, lanes))
-    row = row_index((sublanes, columns))
+    inside = range(first, first + count)
+    tails = [halo_lanes(k, merged, before, after) for k in inside]
+    c_tail, h_tail, g_tail = (jnp.stack([tail[i] for tail in tails]) for i in range(3))
+    s_tail = jnp.stack([turned(after1, -lane_speed(k), 1) for k in inside])
+
+    def stacked(item):
+        return jnp.stack([halo_rows(k, item, levels, lower, upper, rows) for k in inside])
+
+    s_rows = jnp.stack([halo_rows(k, "speed", levels, lower1, upper1, rows) for k in inside])
+    lane = lax.broadcasted_iota(jnp.int32, (count, rows, lanes), 2)
+    row = lax.broadcasted_iota(jnp.int32, (count, sublanes, columns), 1)
     lanes_given = (lane == 1) | (lane == lanes - 1)
     rows_given = (row == 1) | (row == sublanes - 1)
-    c_x = jnp.concatenate([c, c_tail], axis=1)
-    forward = explicit_flux(c_x, speed_x, open_x, 1, columns)
-    c_y = jnp.concatenate([c, halo_rows(k, "tracer", levels, lower, upper, rows)], axis=0)
-    forward = forward + explicit_flux(c_y, speed_y, open_y, 0, rows)
-    h_x = jnp.concatenate([h, h_tail], axis=1)
-    backward = reverse_flux(h_x, speed_x, open_x, g_tail, lanes_given, 1, columns)
-    h_y = jnp.concatenate([h, halo_rows(k, "weight", levels, lower, upper, rows)], axis=0)
-    given = halo_rows(k, "carried", levels, lower, upper, rows)
-    backward = backward + reverse_flux(h_y, speed_y, open_y, given, rows_given, 0, rows)
+
+    def opened(shallow, axis):
+        level = lax.broadcasted_iota(jnp.int32, (count,) + shallow.shape, 0).astype(jnp.float32) + float(first)
+        return split(level < shallow[None], axis)
+
+    speeds = split(east_part * (1.0 / 12.0), 2) + [s_tail]
+    opens = opened(shallow_x, 2)
+    forward = jnp.concatenate(explicit_flux(split(c, 2) + [c_tail], speeds, opens, 2), axis=2)
+    backward = jnp.concatenate(reverse_flux(split(h, 2) + [h_tail], speeds, opens, g_tail, lanes_given, 2), axis=2)
+    speeds = split(north_part * (1.0 / 12.0), 1) + [s_rows]
+    opens = opened(shallow_y, 1)
+    forward = forward + jnp.concatenate(explicit_flux(split(c, 1) + [stacked("tracer")], speeds, opens, 1), axis=1)
+    carried = stacked("carried")
+    ring = split(h, 1) + [stacked("weight")]
+    backward = backward + jnp.concatenate(reverse_flux(ring, speeds, opens, carried, rows_given, 1), axis=1)
     return forward, h + backward
+
+
+group_size = 8
 
 
 def first_kernel(
@@ -258,13 +310,15 @@
     faces = shallow_faces(depth_float, before, after, lower, upper, levels)
     current = jnp.zeros((rows, columns), jnp.float32)
     above = current
+    for k in range(0, levels, group_size):
+        part = slice(k, min(k + group_size, levels))
+        c, h = tracer[part], weight[part]
+        halos = (lower, upper, merged, before, after)
+        forward, back = step_levels(k, levels, c, h, east[part], north[part], faces, (lower, upper, after), halos)
+        linear[part] = back
+        passed[part] = c + forward - uptake * c * c
     for k in range(levels):
-        c, h = tracer[k], weight[k]
-        forward, back = step_level(
-            k, levels, c, h, east[k], north[k], faces, (lower, upper, after), (lower, upper, merged, before, after)
-        )
-        linear[k] = back
-        right = jnp.where(k < deep, c + forward - uptake * c * c, 0.0)
+        right = jnp.where(k < deep, passed[k], 0.0)
         current = (right + above * current) * inverse[k]
         passed[k] = current
         if k < levels - 1:
@@ -299,8 +353,16 @@
 
 def second_kernel(
     tracer, east, north, mixing, depth, inverse, state, weight, got1_even, got1_odd, got1_core, got1_chip,
-    got_even, got_odd, got_core, got_chip, final, adjoint, passed, lower1, upper1, lower, upper,
+    got_even, got_odd, got_core, got_chip, final_far, adjoint_far,
+    final, adjoint, passed, lower1, upper1, lower, upper, sent,
 ):
+    copies = []
+
+    def send(near, far, part):
+        copy = pltpu.make_async_copy(near.at[part], far.at[part], sent.at[len(copies)])
+        copy.start()
+        copies.append(copy)
+
     levels, rows, columns = tracer.shape
     even_y, even_x = parities()
     take_rows(even_y, got1_even, got1_odd, lower1, upper1)
@@ -312,13 +374,16 @@
     faces = shallow_faces(deep.astype(jnp.float32), before1, after1, lower1, upper1, levels)
     current = jnp.zeros((rows, columns), jnp.float32)
     above = current
+    for k in range(0, levels, group_size):
+        part = slice(k, min(k + group_size, levels))
+        c, h = state[part], weight[part]
+        halos = (lower, upper, merged, before, after)
+        forward, back = step_levels(k, levels, c, h, east[part], north[part], faces, (lower1, upper1, after1), halos)
+        adjoint[part] = back - (2.0 * uptake) * tracer[part] * h
+        send(adjoint, adjoint_far, part)
+        passed[part] = c + forward - uptake * c * c
     for k in range(levels):
-        c, h = state[k], weight[k]
-        forward, back = step_level(
-            k, levels, c, h, east[k], north[k], faces, (lower1, upper1, after1), (lower, upper, merged, before, after)
-        )
-        adjoint[k] = back - (2.0 * uptake) * tracer[k] * h
-        right = jnp.where(k < deep, c + forward - uptake * c * c, 0.0)
+        right = jnp.where(k < deep, passed[k], 0.0)
         current = (right + above * current) * inverse[k]
         passed[k] = current
         if k < levels - 1:
@@ -327,6 +392,10 @@
     for k in range(levels - 2, -1, -1):
         current = passed[k] + (jnp.where(k + 1 < deep, mixing[k], 0.0) * inverse[k]) * current
         final[k] = current
+        if k % group_size == 0:
+            send(final, final_far, slice(k, min(k + group_size, levels)))
+    for copy in copies:
+        copy.wait()
 
 
 def pairs(axis, parity):
@@ -361,26 +430,34 @@
     def space(size):
         return pltpu.VMEM((size, columns), f32)
 
-    inverse, weight, *messages = pl.pallas_call(
+    far = pl.BlockSpec(memory_space=pl.ANY)
+    given = (tracer, east_speed, north_speed, mixing, depth_levels)
+    near = tuple(jax.ShapeDtypeStruct(array.shape, array.dtype) for array in given)
+    *outcome, pay_even, pay_odd, pay_core, pay_chip = pl.pallas_call(
         factor_kernel,
-        out_shape=(field, field, lines(first_size), lines(first_size), edge, edge),
-        scratch_shapes=[block],
+        in_specs=[far] * 6,
+        out_shape=near + (field, field, lines(first_size), lines(first_size), edge, edge),
+        scratch_shapes=[block, block, pltpu.SemaphoreType.DMA((6,))],
         compiler_params=params,
-    )(tracer, east_speed, north_speed, mixing, depth_levels, sensitivity)
+    )(*[pltpu.with_memory_space_constraint(a, pltpu.HBM) for a in given], pltpu.with_memory_space_constraint(sensitivity, pltpu.HBM))
+    *given, inverse, weight = outcome
+    messages = (pay_even, pay_odd, pay_core, pay_chip)
     got1 = exchange(*messages)
     state, weight_next, *messages = pl.pallas_call(
         first_kernel,
         out_shape=(field, field, lines(second_size), lines(second_size), edge, edge),
         scratch_shapes=[block, block, space(first_size), space(first_size)],
         compiler_params=params,
-    )(tracer, east_speed, north_speed, mixing, depth_levels, inverse, weight, *got1)
+    )(*given, inverse, weight, *got1)
     got2 = exchange(*messages)
+    sends = pltpu.SemaphoreType.DMA((2 * -(-levels // group_size),))
     final, adjoint = pl.pallas_call(
         second_kernel,
+        out_specs=[far] * 2,
         out_shape=(field, field),
-        scratch_shapes=[block, space(first_size), space(first_size), space(second_size), space(second_size)],
+        scratch_shapes=[block, block, block, space(first_size), space(first_size), space(second_size), space(second_size), sends],
         compiler_params=params,
-    )(tracer, east_speed, north_speed, mixing, depth_levels, inverse, state, weight_next, *got1, *got2)
+    )(*given, inverse, state, weight_next, *got1, *got2)
     return final, adjoint
 
 

time: 35.5 us -> 27.7 us (0.78)
  local copies, waits for them, and re-layouts: 5.46 us -> 0 us
  Pallas kernels: 9.89 us -> 7.63 us
    unnamed x14 -> x0, local copies, waits for them, and re-layouts: 5.46 us -> none
    pallas_call x1, Pallas kernels: 5.03 us -> 2.85 us  [shards(): pl.pallas_call(first_kernel, out_shape=(field, field, lines(second_size),...]
where the time goes in v2:
time: 27.7 us; the launch traced here: 27.4 us
  starting transfers between devices  15.6 us (56%)
  Pallas kernels  7.63 us (28%)
  waiting for transfers between devices  3.51 us (13%)
  between operations  0.71 us (3%)
    ppermute x2, starting transfers between devices, exchange(): got_chip = lax.ppermute(pay_chip, 'tile', pairs('tile', 1))  6.39 us
    ppermute x2, starting transfers between devices, exchange(): got_odd = lax.ppermute(pay_odd, 'group', pairs('group', 1))  6.17 us
    ppermute x2, waiting for transfers between devices, exchange(): got_chip = lax.ppermute(pay_chip, 'tile', pairs('tile', 1))  3.49 us
    pallas_call x1, Pallas kernels, shards(): pl.pallas_call(first_kernel, out_shape=(field, field, lines(second_size),...  2.85 us
    pallas_call x1, Pallas kernels, shards(): pl.pallas_call(second_kernel, out_specs=[far] * 2, out_shape=(field, fiel...  2.48 us
    pallas_call x1, Pallas kernels, shards(): pl.pallas_call(factor_kernel, in_specs=[far] * 6, out_shape=near + (field...  2.3 us
    ppermute x2, starting transfers between devices, exchange(): got_core = lax.ppermute(pay_core, 'tile', pairs('tile', 0))  1.67 us
    ppermute x2, starting transfers between devices, exchange(): got_even = lax.ppermute(pay_even, 'group', pairs('group', 0))  1.35 us
  transfers between devices with their start and end apart: 8, of which 2 were waited for; matrix products, arithmetic and copies ran while one was open for 0% of the time, Pallas kernels for 0%

profile of v2, /device:TPU:13, one launch (start us, length us, event | category | flops | bytes accessed | tf_op | source)
XLA Modules:
  0.0 27.4 jit_solution(14092322340048066835)
XLA Ops:
  0.6 2.3 %shard_map.77 = (f32[16,16,256]{2,1,0:T(8,128)S(1)}, f32[16,16,256]{2,1,0:T(8,128)S(1)}, f32[16,16,256]{2,1,0:T(8,128)S(1)}, f32[15,16,256]{2,1,0:T(8,128)S(1)},...) custom-call(f32[16,16,256]{2,1,0:T(8,128)} %tracer_far.1, ...), custom_call_target="tpu_custom_call" | custom-call | tf_op jit(solution)/shard_map/pallas_call | solution.py:436
  2.9 1.3 %collective-permute-start = (f32[88,256]{1,0:T(8,128)S(1)}, f32[88,256]{1,0:T(8,128)S(1)}, u32[]{:S(2)}, u32[]{:S(2)}) collective-permute-start(f32[88,256]{1,0:T(8,128)S(1)} %get-tuple-element.26), channel_id=1, source_target_pairs={{0,8},{8,0},{16,24},{24,16},{1,9},{9,1},{17,25},{25,17},{2,10},{10... | collective-permute-start | bytes 270344 | tf_op jit(solution)/shard_map/ppermute | solution.py:413
  4.2 2.1 %collective-permute-start.1 = (f32[88,256]{1,0:T(8,128)S(1)}, f32[88,256]{1,0:T(8,128)S(1)}, u32[]{:S(2)}, u32[]{:S(2)}) collective-permute-start(f32[88,256]{1,0:T(8,128)S(1)} %get-tuple-element.27), channel_id=1, source_target_pairs={{8,16},{16,8},{9,17},{17,9},{10,18},{18,10},{11,19},{19,11},{12,20... | collective-permute-start | bytes 270344 | tf_op jit(solution)/shard_map/ppermute | solution.py:412
  6.3 1.3 %collective-permute-start.2 = (f32[16,128]{1,0:T(8,128)S(1)}, f32[16,128]{1,0:T(8,128)S(1)}, u32[]{:S(2)}, u32[]{:S(2)}) collective-permute-start(f32[16,128]{1,0:T(8,128)S(1)} %get-tuple-element.28), channel_id=1, source_target_pairs={{0,1},{1,0},{2,3},{3,2},{4,5},{5,4},{6,7},{7,6},{8,9},{9,8},{10,11... | collective-permute-start | bytes 24584 | tf_op jit(solution)/shard_map/ppermute | solution.py:410
  7.6 3.1 %collective-permute-start.3 = (f32[16,128]{1,0:T(8,128)S(1)}, f32[16,128]{1,0:T(8,128)S(1)}, u32[]{:S(2)}, u32[]{:S(2)}) collective-permute-start(f32[16,128]{1,0:T(8,128)S(1)} %get-tuple-element.29), channel_id=1, source_target_pairs={{1,2},{2,1},{3,4},{4,3},{5,6},{6,5},{9,10},{10,9},{11,12},{12,11},... | collective-permute-start | bytes 24584 | tf_op jit(solution)/shard_map/ppermute | solution.py:411
  10.7 0.0 collective-permute-done.2.got_core.got1_core
  10.7 1.8 %collective-permute-done.3.got_chip.got1_chip = f32[16,128]{1,0:T(8,128)S(1)} collective-permute-done((f32[16,128]{1,0:T(8,128)S(1)}, f32[16,128]{1,0:T(8,128)S(1)}, u32[]{:S(2)}, u32[]{:S(2)}) %collective-permute-start.3) | collective-permute-done | bytes 8224 | tf_op jit(solution)/shard_map/ppermute | solution.py:411
  12.6 0.0 collective-permute-done.got_even.got1_even
  12.6 0.0 collective-permute-done.1.got_odd.got1_odd
  12.6 2.8 %shard_map.78 = (f32[16,16,256]{2,1,0:T(8,128)S(1)}, f32[16,16,256]{2,1,0:T(8,128)S(1)}, f32[64,256]{1,0:T(8,128)S(1)}, f32[64,256]{1,0:T(8,128)S(1)}, f32[16,128]{1,0:T(8,128)S(1)}, /*index=5*/f32[16,128]{1,0:T(8,128)S(1)}) custom-call(f32[16,16,256]{2,1,0:T(8,128)S(1)} %get-tuple-element.19.tracer, f32[16,16,256]{2,1,0:T(8,128)S(1)} %get-tuple-element.20.east, ...), custom_call_target="tpu_custom_call" | custom-call | tf_op jit(solution)/shard_map/pallas_call | solution.py:446
  15.4 0.1 collective-permute-start.4
  15.5 4.1 %collective-permute-start.5 = (f32[64,256]{1,0:T(8,128)S(1)}, f32[64,256]{1,0:T(8,128)S(1)}, u32[]{:S(2)}, u32[]{:S(2)}) collective-permute-start(f32[64,256]{1,0:T(8,128)S(1)} %get-tuple-element.33), channel_id=1, source_target_pairs={{8,16},{16,8},{9,17},{17,9},{10,18},{18,10},{11,19},{19,11},{12,20... | collective-permute-start | bytes 196616 | tf_op jit(solution)/shard_map/ppermute | solution.py:412
  19.6 0.4 %collective-permute-start.6 = (f32[16,128]{1,0:T(8,128)S(1)}, f32[16,128]{1,0:T(8,128)S(1)}, u32[]{:S(2)}, u32[]{:S(2)}) collective-permute-start(f32[16,128]{1,0:T(8,128)S(1)} %get-tuple-element.34), channel_id=1, source_target_pairs={{0,1},{1,0},{2,3},{3,2},{4,5},{5,4},{6,7},{7,6},{8,9},{9,8},{10,11... | collective-permute-start | bytes 24584 | tf_op jit(solution)/shard_map/ppermute | solution.py:410
  20.0 3.3 %collective-permute-start.7 = (f32[16,128]{1,0:T(8,128)S(1)}, f32[16,128]{1,0:T(8,128)S(1)}, u32[]{:S(2)}, u32[]{:S(2)}) collective-permute-start(f32[16,128]{1,0:T(8,128)S(1)} %get-tuple-element.35), channel_id=1, source_target_pairs={{1,2},{2,1},{3,4},{4,3},{5,6},{6,5},{9,10},{10,9},{11,12},{12,11},... | collective-permute-start | bytes 24584 | tf_op jit(solution)/shard_map/ppermute | solution.py:411
  23.3 0.0 collective-permute-done.6.got_core
  23.3 1.7 %collective-permute-done.7.got_chip = f32[16,128]{1,0:T(8,128)S(1)} collective-permute-done((f32[16,128]{1,0:T(8,128)S(1)}, f32[16,128]{1,0:T(8,128)S(1)}, u32[]{:S(2)}, u32[]{:S(2)}) %collective-permute-start.7) | collective-permute-done | bytes 8224 | tf_op jit(solution)/shard_map/ppermute | solution.py:411
  24.9 0.0 collective-permute-done.4.got_even
  24.9 0.0 collective-permute-done.5.got_odd
  24.9 2.5 %shard_map.79 = (f32[16,16,256]{2,1,0:T(8,128)}, f32[16,16,256]{2,1,0:T(8,128)}) custom-call(f32[16,16,256]{2,1,0:T(8,128)S(1)} %get-tuple-element.19.tracer, f32[16,16,256]{2,1,0:T(8,128)S(1)} %get-tuple-element.20.east, f32[16,16,256]{2,1,0:T(8,128)S(1)} %get-tuple-element.21.north, f32[15,16,256]{2,1,0:T(8,128)S(1)} %get-tuple-element.22.mixing, ...), custom_call_target="tpu_custom_call" | custom-call | tf_op jit(solution)/shard_map/pallas_call | solution.py:454
Async XLA Ops:
  2.9 9.6 %collective-permute-start = (f32[88,256]{1,0:T(8,128)S(1)}, f32[88,256]{1,0:T(8,128)S(1)}, u32[]{:S(2)}, u32[]{:S(2)}) collective-permute-start(f32[88,256]{1,0:T(8,128)S(1)} %get-tuple-element.26), channel_id=1, source_target_pairs={{0,8},{8,0},{16,24},{24,16},{1,9},{9,1},{17,25},{25,17},{2,10},{10... | collective-permute-start | bytes 270344 | tf_op jit(solution)/shard_map/ppermute | solution.py:413
  4.2 8.4 %collective-permute-start.1 = (f32[88,256]{1,0:T(8,128)S(1)}, f32[88,256]{1,0:T(8,128)S(1)}, u32[]{:S(2)}, u32[]{:S(2)}) collective-permute-start(f32[88,256]{1,0:T(8,128)S(1)} %get-tuple-element.27), channel_id=1, source_target_pairs={{8,16},{16,8},{9,17},{17,9},{10,18},{18,10},{11,19},{19,11},{12,20... | collective-permute-start | bytes 270344 | tf_op jit(solution)/shard_map/ppermute | solution.py:412
  6.3 4.4 %collective-permute-start.2 = (f32[16,128]{1,0:T(8,128)S(1)}, f32[16,128]{1,0:T(8,128)S(1)}, u32[]{:S(2)}, u32[]{:S(2)}) collective-permute-start(f32[16,128]{1,0:T(8,128)S(1)} %get-tuple-element.28), channel_id=1, source_target_pairs={{0,1},{1,0},{2,3},{3,2},{4,5},{5,4},{6,7},{7,6},{8,9},{9,8},{10,11... | collective-permute-start | bytes 24584 | tf_op jit(solution)/shard_map/ppermute | solution.py:410
  7.6 5.0 %collective-permute-start.3 = (f32[16,128]{1,0:T(8,128)S(1)}, f32[16,128]{1,0:T(8,128)S(1)}, u32[]{:S(2)}, u32[]{:S(2)}) collective-permute-start(f32[16,128]{1,0:T(8,128)S(1)} %get-tuple-element.29), channel_id=1, source_target_pairs={{1,2},{2,1},{3,4},{4,3},{5,6},{6,5},{9,10},{10,9},{11,12},{12,11},... | collective-permute-start | bytes 24584 | tf_op jit(solution)/shard_map/ppermute | solution.py:411
  15.4 9.5 %collective-permute-start.4 = (f32[64,256]{1,0:T(8,128)S(1)}, f32[64,256]{1,0:T(8,128)S(1)}, u32[]{:S(2)}, u32[]{:S(2)}) collective-permute-start(f32[64,256]{1,0:T(8,128)S(1)} %get-tuple-element.32), channel_id=1, source_target_pairs={{0,8},{8,0},{16,24},{24,16},{1,9},{9,1},{17,25},{25,17},{2,10},{10... | collective-permute-start | bytes 196616 | tf_op jit(solution)/shard_map/ppermute | solution.py:413
  15.5 9.4 %collective-permute-start.5 = (f32[64,256]{1,0:T(8,128)S(1)}, f32[64,256]{1,0:T(8,128)S(1)}, u32[]{:S(2)}, u32[]{:S(2)}) collective-permute-start(f32[64,256]{1,0:T(8,128)S(1)} %get-tuple-element.33), channel_id=1, source_target_pairs={{8,16},{16,8},{9,17},{17,9},{10,18},{18,10},{11,19},{19,11},{12,20... | collective-permute-start | bytes 196616 | tf_op jit(solution)/shard_map/ppermute | solution.py:412
  19.6 3.7 %collective-permute-start.6 = (f32[16,128]{1,0:T(8,128)S(1)}, f32[16,128]{1,0:T(8,128)S(1)}, u32[]{:S(2)}, u32[]{:S(2)}) collective-permute-start(f32[16,128]{1,0:T(8,128)S(1)} %get-tuple-element.34), channel_id=1, source_target_pairs={{0,1},{1,0},{2,3},{3,2},{4,5},{5,4},{6,7},{7,6},{8,9},{9,8},{10,11... | collective-permute-start | bytes 24584 | tf_op jit(solution)/shard_map/ppermute | solution.py:410
  20.0 5.0 %collective-permute-start.7 = (f32[16,128]{1,0:T(8,128)S(1)}, f32[16,128]{1,0:T(8,128)S(1)}, u32[]{:S(2)}, u32[]{:S(2)}) collective-permute-start(f32[16,128]{1,0:T(8,128)S(1)} %get-tuple-element.35), channel_id=1, source_target_pairs={{1,2},{2,1},{3,4},{4,3},{5,6},{6,5},{9,10},{10,9},{11,12},{12,11},... | collective-permute-start | bytes 24584 | tf_op jit(solution)/shard_map/ppermute | solution.py:411

commit v3 on v2

v3 whole, which is shorter than its diff:
```python
import jax
import jax.numpy as jnp
from jax import lax
from jax.experimental import pallas as pl
from jax.experimental.pallas import tpu as pltpu
from jax.sharding import PartitionSpec as P

diffusivity = 0.1
uptake = 0.2
lanes = 128
sublanes = 8
group_size = 8

slot = 8


def turned(value, shift, axis):
    return pltpu.roll(value, shift % value.shape[axis], axis)


def index(shape, axis):
    return lax.broadcasted_iota(jnp.int32, shape, axis)


def parities():
    return lax.rem(lax.axis_index("group"), 2) == 0, lax.rem(lax.axis_index("tile"), 2) == 0


def split(value, axis):
    step = lanes if axis == 2 else sublanes
    return [lax.slice_in_dim(value, i, i + step, axis=axis) for i in range(0, value.shape[axis], step)]


def shifted(tiles, shift, axis, edge):
    span = tiles[0].shape[axis]
    moved = [turned(tile, shift, axis) for tile in tiles]
    place = index(tiles[0].shape, axis)
    if shift > 0:
        return [jnp.where(place < shift, a, b) for a, b in zip([edge] + moved[:-1], moved)]
    return [jnp.where(place >= span + shift, a, b) for a, b in zip(moved[1:] + [edge], moved)]


def face_flux(c, behind, ahead, far, speed, is_open):
    flux = speed * (7.0 * (c + behind) - (ahead + far)) - diffusivity * (c - behind)
    return jnp.where(is_open, flux, 0.0)


def explicit_flux(tiles, speeds, opens, axis, edges):
    edge_behind, edge_far, edge_ahead, edge_flux = edges
    behind = shifted(tiles, 1, axis, edge_behind)
    ahead = shifted(tiles, -1, axis, edge_ahead)
    far = shifted(tiles, 2, axis, edge_far)
    flux = [face_flux(*each) for each in zip(tiles, behind, ahead, far, speeds, opens)]
    following = shifted(flux, -1, axis, edge_flux)
    return jnp.concatenate([g - n for g, n in zip(flux, following)], axis=axis)


def reverse_flux(tiles, speeds, opens, axis, edges):
    edge_behind, edge_sum, edge_carried, edge_far = edges
    behind = shifted(tiles, 1, axis, edge_behind)
    jump = [jnp.where(o, h - b, 0.0) for h, b, o in zip(tiles, behind, opens)]
    carried = [s * j for s, j in zip(speeds, jump)]
    seven = [7.0 * g for g in carried]
    spread = [diffusivity * j for j in jump]
    ahead = shifted([a + b for a, b in zip(seven, spread)], -1, axis, edge_sum)
    back = shifted(carried, 1, axis, edge_carried)
    far = shifted(carried, -2, axis, edge_far)
    parts = zip(seven, spread, ahead, back, far)
    return jnp.concatenate([(a - b) + c - d - e for a, b, c, d, e in parts], axis=axis)


def pack_last(k, tile, packed):
    lane = index(packed.shape, 1) - slot * k
    return jnp.where((lane >= 0) & (lane < 4), turned(tile, slot * k + 4, 1), packed)


def pack_first(k, tile, packed):
    lane = index(packed.shape, 1) - slot * k
    return jnp.where((lane >= 2) & (lane < 6), turned(tile, slot * k + 2, 1), packed)


def repeated(first_slot):
    value = jnp.where(index(first_slot.shape, 1) < slot, first_slot, 0.0)
    width = slot
    while width < lanes:
        value = value + turned(value, width, 1)
        width *= 2
    return value


def pack_rows(k, levels, c, h, speed, open_y, up, down):
    size = c.shape[0]
    last = slice(size - sublanes, size)
    first = slice(0, sublanes)
    g_last = jnp.where(open_y[last], speed[last] * (h[last] - turned(h[last], 1, 0)), 0.0)
    g_first = jnp.where(open_y[first], speed[first] * (h[first] - turned(h[first], 1, 0)), 0.0)
    above = (c[size - 2 : size - 1], c[size - 1 :], h[size - 1 :], g_last[sublanes - 1 :])
    below = (c[0:1], c[1:2], h[0:1], g_first[1:2])
    for item in range(4):
        at = item * levels + k
        up[at : at + 1, :] = above[item]
        down[at : at + 1, :] = below[item]


def choose(flag, ref_true, ref_false, into):
    into[...] = jnp.where(flag, ref_true[...], ref_false[...])


def factor_kernel(
    tracer_far, east_far, north_far, mixing_far, depth_far, sensitivity_far,
    tracer, east, north, mixing, depth, inverse, weight, pay_even, pay_odd, pay_chip, pay_core, up,
    sensitivity, passed, down, arrived,
):
    order = (
        (depth_far, depth),
        (mixing_far, mixing),
        (sensitivity_far, sensitivity),
        (tracer_far, tracer),
        (east_far, east),
        (north_far, north),
    )
    copies = [pltpu.make_async_copy(far, near, arrived.at[i]) for i, (far, near) in enumerate(order)]
    for copy in copies:
        copy.start()
    for copy in copies[:3]:
        copy.wait()
    levels, rows, columns = tracer.shape
    even_y, even_x = parities()
    deep = depth[...]
    shallow_y = jnp.minimum(deep, turned(deep, 1, 0))
    above = jnp.zeros((rows, columns), jnp.float32)
    share = above
    current = above
    for k in range(levels):
        below = jnp.where(k + 1 < deep, mixing[k], 0.0) if k < levels - 1 else jnp.zeros_like(above)
        inv = 1.0 / (1.0 + below + (above - above * share))
        current = (sensitivity[k] + above * current) * inv
        share = below * inv
        above = below
        inverse[k] = inv
        passed[k] = current
    for copy in copies[3:]:
        copy.wait()
    last = [jnp.zeros((rows, lanes), jnp.float32)] * 3
    first = last
    for k in range(levels - 1, -1, -1):
        if k < levels - 1:
            share = jnp.where(k + 1 < deep, mixing[k], 0.0) * inverse[k]
            current = passed[k] + share * current
        h = jnp.where(k < deep, current, 0.0)
        weight[k] = h
        c = tracer[k]
        speed_x = east[k] * (1.0 / 12.0)
        speed_y = north[k] * (1.0 / 12.0)
        items = (c, h, speed_x)
        last = [pack_last(k, item[:, -lanes:], packed) for item, packed in zip(items, last)]
        first = [pack_first(k, item[:, :lanes], packed) for item, packed in zip(items, first)]
        pack_rows(k, levels, c, h, speed_y, k < shallow_y, up, down)
        at = 4 * levels + k
        down[at : at + 1, :] = speed_y[0:1]
    depth_float = deep.astype(jnp.float32)
    at = 5 * levels
    up[4 * levels : at, :] = jnp.zeros((levels, columns), jnp.float32)
    up[at : at + sublanes, :] = jnp.broadcast_to(depth_float[rows - 1 :], (sublanes, columns))
    down[at : at + sublanes, :] = jnp.broadcast_to(depth_float[0:1], (sublanes, columns))
    choose(even_y, up, down, pay_even)
    choose(even_y, down, up, pay_odd)
    last.append(repeated(turned(depth_float[:, -lanes:], 4, 1)))
    first.append(repeated(turned(depth_float[:, :lanes], 2, 1)))
    last, first = jnp.concatenate(last, axis=1), jnp.concatenate(first, axis=1)
    pay_chip[...] = jnp.where(even_x, first, last)
    pay_core[...] = jnp.where(even_x, last, first)


def edges_y(levels, lower, upper, own, given, edge):
    rows_of = lambda ref, item: ref[item * levels : (item + 1) * levels, :]
    c, c_next, h, carried_next = (rows_of(upper, i) for i in range(4))
    c_two, c_one, h_one = (rows_of(own, i) for i in range(3))
    speed, deep, own_deep = given
    level = index(c.shape, 0).astype(jnp.float32)
    is_open = level < jnp.minimum(deep, own_deep)
    flux = face_flux(c, c_one, c_next, c_two, speed, is_open)
    jump = jnp.where(is_open, h - h_one, 0.0)
    carried = speed * jump
    total = 7.0 * carried + diffusivity * jump
    below = tuple(rows_of(lower, i) for i in range(4))
    for item, value in enumerate(below + (c, flux, total, carried, carried_next)):
        edge[item * levels : (item + 1) * levels, :] = value


def edges_x(before, after, own_last, speeds, depths):
    c_before, h_before = before
    c_after, h_after = after
    c_own, h_own = own_last
    speed_before, speed_after = speeds
    deep_before, deep_after, deep_own = depths
    shape = c_before.shape
    place = lax.rem(index(shape, 1), slot)
    level = lax.div(index(shape, 1), slot).astype(jnp.float32)
    inner = place < 2
    c = jnp.where(inner, turned(c_own, -2, 1), c_after)
    h = jnp.where(inner, turned(h_own, -2, 1), h_after)
    deep = jnp.where(inner, turned(deep_own, -2, 1), deep_after)
    is_open = level < jnp.minimum(deep, turned(deep, 1, 1))
    flux = face_flux(c, turned(c, 1, 1), turned(c, -1, 1), turned(c, 2, 1), speed_after, is_open)
    jump = jnp.where(is_open, h - turned(h, 1, 1), 0.0)
    carried = speed_after * jump
    total = 7.0 * carried + diffusivity * jump
    is_open = level < jnp.minimum(deep_before, turned(deep_before, 1, 1))
    carried_before = jnp.where(is_open, speed_before * (h_before - turned(h_before, 1, 1)), 0.0)
    start = place < 4
    return (
        jnp.where(start, turned(c_before, -2, 1), turned(c, -3, 1)),
        jnp.where(start, turned(c_before, -3, 1), turned(flux, -3, 1)),
        jnp.where(start, turned(h_before, -3, 1), turned(total, -3, 1)),
        jnp.where(start, turned(carried_before, -3, 1), turned(carried, -4, 1)),
    )


def step_levels(first, levels, c, h, east_part, north_part, shallow, edge, packed):
    count, rows, columns = c.shape
    shallow_x, shallow_y = shallow
    inside = range(first, first + count)
    level = index((count, rows, columns), 0) + first

    lead = [jnp.stack([turned(tile, -slot * k, 1) for k in inside]) for tile in packed]
    speeds = split(east_part * (1.0 / 12.0), 2)
    opens = split(level < shallow_x[None], 2)
    forward = explicit_flux(split(c, 2), speeds, opens, 2, (lead[1], lead[0], lead[0], lead[1]))
    backward = reverse_flux(split(h, 2), speeds, opens, 2, (lead[2], lead[2], lead[3], lead[3]))

    def line(item):
        at = item * levels
        return jnp.stack([jnp.broadcast_to(edge[at + k : at + k + 1, :], (sublanes, columns)) for k in inside])

    row = index((count, sublanes, columns), 1)
    speeds = split(north_part * (1.0 / 12.0), 1)
    opens = split(level < shallow_y[None], 1)
    one = line(1)
    edges = (one, jnp.where(row == 0, line(0), one), line(4), line(5))
    forward = forward + explicit_flux(split(c, 1), speeds, opens, 1, edges)
    edges = (line(2), line(6), line(3), jnp.where(row == sublanes - 2, line(7), line(8)))
    backward = backward + reverse_flux(split(h, 1), speeds, opens, 1, edges)
    return forward, h + backward


def shallow_faces(deep, deep_before, deep_lower):
    rows, columns = deep.shape
    previous = turned(deep, 1, 1)
    head = jnp.where(index((rows, lanes), 1) == 0, turned(deep_before, -3, 1), previous[:, :lanes])
    previous_x = jnp.concatenate([head, previous[:, lanes:]], axis=1)
    previous = turned(deep, 1, 0)
    head = jnp.where(index((sublanes, columns), 0) == 0, deep_lower, previous[:sublanes])
    previous_y = jnp.concatenate([head, previous[sublanes:]], axis=0)
    return jnp.minimum(deep, previous_x).astype(jnp.int32), jnp.minimum(deep, previous_y).astype(jnp.int32)


def item_of(value, item):
    return value[:, item * lanes : (item + 1) * lanes]


def take(flag, first, second):
    a, b = first[...], second[...]
    return jnp.where(flag, b, a), jnp.where(flag, a, b)


def first_kernel(
    tracer, east, north, mixing, depth, inverse, weight, own_up, sent_chip, sent_core,
    got_even, got_odd, got_chip, got_core,
    state, weight_next, pay_even, pay_odd, pay_chip, pay_core, up, own_last,
    passed, linear, lower, upper, edge, down,
):
    levels, rows, columns = tracer.shape
    even_y, even_x = parities()
    choose(even_y, got_odd, got_even, lower)
    choose(even_y, got_even, got_odd, upper)
    before, after = take(even_x, got_core, got_chip)
    own = jnp.where(even_x, sent_core[...], sent_chip[...])
    deep = depth[...]
    at = 5 * levels
    depth_float = deep.astype(jnp.float32)
    shallow = shallow_faces(depth_float, item_of(before, 3), lower[at : at + sublanes, :])
    speed = upper[4 * levels : at, :]
    edges_y(levels, lower, upper, own_up, (speed, upper[at : at + 1, :], depth_float[rows - 1 :]), edge)
    pairs_of = lambda value: (item_of(value, 0), item_of(value, 1))
    packed = edges_x(
        pairs_of(before),
        pairs_of(after),
        pairs_of(own),
        (item_of(before, 2), item_of(after, 2)),
        (item_of(before, 3), item_of(after, 3), item_of(own, 3)),
    )
    current = jnp.zeros((rows, columns), jnp.float32)
    above = current
    for k in range(0, levels, group_size):
        part = slice(k, min(k + group_size, levels))
        c, h = tracer[part], weight[part]
        forward, back = step_levels(k, levels, c, h, east[part], north[part], shallow, edge, packed)
        linear[part] = back
        passed[part] = c + forward - uptake * c * c
    for k in range(levels):
        current = (jnp.where(k < deep, passed[k], 0.0) + above * current) * inverse[k]
        passed[k] = current
        if k < levels - 1:
            above = jnp.where(k + 1 < deep, mixing[k], 0.0)
    state[levels - 1] = current
    for k in range(levels - 2, -1, -1):
        current = passed[k] + (jnp.where(k + 1 < deep, mixing[k], 0.0) * inverse[k]) * current
        state[k] = current
    current = jnp.zeros((rows, columns), jnp.float32)
    for k in range(levels):
        right = linear[k] - (2.0 * uptake) * state[k] * weight[k]
        if k > 0:
            right = right + jnp.where(k < deep, mixing[k - 1], 0.0) * current
        current = right * inverse[k]
        passed[k] = current
    last = [jnp.zeros((rows, lanes), jnp.float32)] * 2
    first = last
    shallow_y = shallow[1]
    for k in range(levels - 1, -1, -1):
        if k < levels - 1:
            current = passed[k] + (jnp.where(k + 1 < deep, mixing[k], 0.0) * inverse[k]) * current
        h = jnp.where(k < deep, current, 0.0)
        weight_next[k] = h
        c = state[k]
        items = (c, h)
        last = [pack_last(k, item[:, -lanes:], packed) for item, packed in zip(items, last)]
        first = [pack_first(k, item[:, :lanes], packed) for item, packed in zip(items, first)]
        pack_rows(k, levels, c, h, north[k] * (1.0 / 12.0), k < shallow_y, up, down)
    choose(even_y, up, down, pay_even)
    choose(even_y, down, up, pay_odd)
    last, first = jnp.concatenate(last, axis=1), jnp.concatenate(first, axis=1)
    own_last[...] = last
    pay_chip[...] = jnp.where(even_x, first, last)
    pay_core[...] = jnp.where(even_x, last, first)


def second_kernel(
    tracer, east, north, mixing, depth, inverse, state, weight, own_up, own_last, sent_chip, sent_core,
    got1_even, got1_odd, got1_chip, got1_core, got_even, got_odd, got_chip, got_core,
    final_far, adjoint_far,
    final, adjoint, passed, lower, upper, edge, sent,
):
    copies = []

    def send(near, far, part):
        copy = pltpu.make_async_copy(near.at[part], far.at[part], sent.at[len(copies)])
        copy.start()
        copies.append(copy)

    levels, rows, columns = tracer.shape
    even_y, even_x = parities()
    choose(even_y, got_odd, got_even, lower)
    choose(even_y, got_even, got_odd, upper)
    before1, after1 = take(even_x, got1_core, got1_chip)
    before, after = take(even_x, got_core, got_chip)
    own1 = jnp.where(even_x, sent_core[...], sent_chip[...])
    deep = depth[...]
    depth_float = deep.astype(jnp.float32)
    at = 5 * levels
    lower_deep = jnp.where(even_y, got1_odd[at : at + sublanes, :], got1_even[at : at + sublanes, :])
    upper_deep = jnp.where(even_y, got1_even[at : at + 1, :], got1_odd[at : at + 1, :])
    speed = jnp.where(even_y, got1_even[4 * levels : at, :], got1_odd[4 * levels : at, :])
    shallow = shallow_faces(depth_float, item_of(before1, 3), lower_deep)
    edges_y(levels, lower, upper, own_up, (speed, upper_deep, depth_float[rows - 1 :]), edge)
    pairs_of = lambda value: (item_of(value, 0), item_of(value, 1))
    packed = edges_x(
        pairs_of(before),
        pairs_of(after),
        pairs_of(own_last[...]),
        (item_of(before1, 2), item_of(after1, 2)),
        (item_of(before1, 3), item_of(after1, 3), item_of(own1, 3)),
    )
    current = jnp.zeros((rows, columns), jnp.float32)
    above = current
    for k in range(0, levels, group_size):
        part = slice(k, min(k + group_size, levels))
        c, h = state[part], weight[part]
        forward, back = step_levels(k, levels, c, h, east[part], north[part], shallow, edge, packed)
        adjoint[part] = back - (2.0 * uptake) * tracer[part] * h
        send(adjoint, adjoint_far, part)
        passed[part] = c + forward - uptake * c * c
    for k in range(levels):
        current = (jnp.where(k < deep, passed[k], 0.0) + above * current) * inverse[k]
        passed[k] = current
        if k < levels - 1:
            above = jnp.where(k + 1 < deep, mixing[k], 0.0)
    final[levels - 1] = current
    for k in range(levels - 2, -1, -1):
        current = passed[k] + (jnp.where(k + 1 < deep, mixing[k], 0.0) * inverse[k]) * current
        final[k] = current
        if k % group_size == 0:
            send(final, final_far, slice(k, min(k + group_size, levels)))
    for copy in copies:
        copy.wait()


def pairs(axis, parity):
    devices = lax.axis_size(axis)
    swaps = []
    for i in range(parity, devices - 1, 2):
        swaps += [(i, i + 1), (i + 1, i)]
    return swaps


def exchange(pay_even, pay_odd, pay_chip, pay_core):
    got_even = lax.ppermute(pay_even, "group", pairs("group", 0))
    got_odd = lax.ppermute(pay_odd, "group", pairs("group", 1))
    got_chip = lax.ppermute(pay_chip, "tile", pairs("tile", 1))
    got_core = lax.ppermute(pay_core, "tile", pairs("tile", 0))
    return got_even, got_odd, got_chip, got_core


def shards(tracer, east_speed, north_speed, mixing, depth_levels, sensitivity):
    levels, rows, columns = tracer.shape
    assert levels * slot == lanes and rows % sublanes == 0 and columns % lanes == 0
    f32 = jnp.float32
    field = jax.ShapeDtypeStruct((levels, rows, columns), f32)
    first_size = 5 * levels + sublanes
    second_size = 4 * levels
    edge_size = 9 * levels
    block = pltpu.VMEM((levels, rows, columns), f32)
    params = pltpu.CompilerParams(vmem_limit_bytes=32 * 1024 * 1024)
    far = pl.BlockSpec(memory_space=pl.ANY)

    def lines(size):
        return jax.ShapeDtypeStruct((size, columns), f32)

    def space(size):
        return pltpu.VMEM((size, columns), f32)

    def tiles(count):
        return jax.ShapeDtypeStruct((rows, count * lanes), f32)

    given = (tracer, east_speed, north_speed, mixing, depth_levels)
    near = tuple(jax.ShapeDtypeStruct(array.shape, array.dtype) for array in given)
    distant = [pltpu.with_memory_space_constraint(array, pltpu.HBM) for array in given + (sensitivity,)]
    outcome = pl.pallas_call(
        factor_kernel,
        in_specs=[far] * 6,
        out_shape=near
        + (field, field, lines(first_size), lines(first_size), tiles(4), tiles(4), lines(first_size)),
        scratch_shapes=[block, block, space(first_size), pltpu.SemaphoreType.DMA((6,))],
        compiler_params=params,
    )(*distant)
    given = outcome[:5]
    inverse, weight, *messages, up = outcome[5:]
    got1 = exchange(*messages)
    sent1 = messages[2:]
    state, weight_next, *messages, up2, last2 = pl.pallas_call(
        first_kernel,
        out_shape=(field, field, lines(second_size), lines(second_size), tiles(2), tiles(2), lines(second_size), tiles(2)),
        scratch_shapes=[
            block, block, space(first_size), space(first_size), space(edge_size), space(second_size),
        ],
        compiler_params=params,
    )(*given, inverse, weight, up, *sent1, *got1)
    got2 = exchange(*messages)
    sends = pltpu.SemaphoreType.DMA((2 * -(-levels // group_size),))
    final, adjoint = pl.pallas_call(
        second_kernel,
        out_specs=[far] * 2,
        out_shape=(field, field),
        scratch_shapes=[block, block, block, space(second_size), space(second_size), space(edge_size), sends],
        compiler_params=params,
    )(*given, inverse, state, weight_next, up2, last2, *sent1, *got1, *got2)
    return final, adjoint


def solution(mesh):
    block = P(None, "group", "tile")
    in_specs = (block, block, block, block, P("group", "tile"), block)
    return jax.shard_map(shards, mesh=mesh, in_specs=in_specs, out_specs=(block, block), check_vma=False)
```

time: 27.7 us -> 25.5 us (0.921)
  Pallas kernels: 7.63 us -> 5.57 us
  waiting for transfers between devices: 3.51 us -> 3.17 us
    ppermute x2, starting transfers between devices: 6.39 us -> 8.09 us  [exchange(): got_chip = lax.ppermute(pay_chip, 'tile', pairs('tile', 1))]
    ppermute x2, starting transfers between devices: 1.67 us -> 0.14 us  [exchange(): got_core = lax.ppermute(pay_core, 'tile', pairs('tile', 0))]
    pallas_call x1, Pallas kernels: 2.85 us -> 1.67 us  [shards(): pl.pallas_call(first_kernel, out_shape=(field, field, lines(second_size),...]
    pallas_call x1, Pallas kernels: 2.3 us -> 1.8 us  [shards(): pl.pallas_call(factor_kernel, in_specs=[far] * 6, out_shape=near + (field...]
    pallas_call x1, Pallas kernels: 2.48 us -> 2.1 us  [shards(): pl.pallas_call(second_kernel, out_specs=[far] * 2, out_shape=(field, fiel...]
    ppermute x2, waiting for transfers between devices: 3.49 us -> 3.15 us  [exchange(): got_chip = lax.ppermute(pay_chip, 'tile', pairs('tile', 1))]
where the time goes in v3:
time: 25.5 us; the launch traced here: 25.2 us
  starting transfers between devices  15.7 us (62%)
  Pallas kernels  5.57 us (22%)
  waiting for transfers between devices  3.17 us (12%)
  between operations  0.71 us (3%)
    ppermute x2, starting transfers between devices, exchange(): got_chip = lax.ppermute(pay_chip, 'tile', pairs('tile', 1))  8.09 us
    ppermute x2, starting transfers between devices, exchange(): got_odd = lax.ppermute(pay_odd, 'group', pairs('group', 1))  6.17 us
    ppermute x2, waiting for transfers between devices, exchange(): got_chip = lax.ppermute(pay_chip, 'tile', pairs('tile', 1))  3.15 us
    pallas_call x1, Pallas kernels, shards(): pl.pallas_call(second_kernel, out_specs=[far] * 2, out_shape=(field, fiel...  2.1 us
    pallas_call x1, Pallas kernels, shards(): pl.pallas_call(factor_kernel, in_specs=[far] * 6, out_shape=near + (field...  1.8 us
    pallas_call x1, Pallas kernels, shards(): pl.pallas_call(first_kernel, out_shape=(field, field, lines(second_size),...  1.67 us
    ppermute x2, starting transfers between devices, exchange(): got_even = lax.ppermute(pay_even, 'group', pairs('group', 0))  1.35 us
  transfers between devices with their start and end apart: 8, of which 2 were waited for; matrix products, arithmetic and copies ran while one was open for 0% of the time, Pallas kernels for 0%

profile of v3, /device:TPU:13, one launch (start us, length us, event | category | flops | bytes accessed | tf_op | source)
XLA Modules:
  0.0 25.2 jit_solution(14317394638489270775)
XLA Ops:
  0.6 1.8 %shard_map.77 = (f32[16,16,256]{2,1,0:T(8,128)S(1)}, f32[16,16,256]{2,1,0:T(8,128)S(1)}, f32[16,16,256]{2,1,0:T(8,128)S(1)}, f32[15,16,256]{2,1,0:T(8,128)S(1)},...) custom-call(f32[16,16,256]{2,1,0:T(8,128)} %tracer_far.1, ...), custom_call_target="tpu_custom_call" | custom-call | tf_op jit(solution)/shard_map/pallas_call | solution.py:438
  2.4 1.3 %collective-permute-start = (f32[88,256]{1,0:T(8,128)S(1)}, f32[88,256]{1,0:T(8,128)S(1)}, u32[]{:S(2)}, u32[]{:S(2)}) collective-permute-start(f32[88,256]{1,0:T(8,128)S(1)} %get-tuple-element.32), channel_id=1, source_target_pairs={{0,8},{8,0},{16,24},{24,16},{1,9},{9,1},{17,25},{25,17},{2,10},{10... | collective-permute-start | bytes 270344 | tf_op jit(solution)/shard_map/ppermute | solution.py:407
  3.7 2.1 %collective-permute-start.1 = (f32[88,256]{1,0:T(8,128)S(1)}, f32[88,256]{1,0:T(8,128)S(1)}, u32[]{:S(2)}, u32[]{:S(2)}) collective-permute-start(f32[88,256]{1,0:T(8,128)S(1)} %get-tuple-element.33), channel_id=1, source_target_pairs={{8,16},{16,8},{9,17},{17,9},{10,18},{18,10},{11,19},{19,11},{12,20... | collective-permute-start | bytes 270344 | tf_op jit(solution)/shard_map/ppermute | solution.py:408
  5.8 4.3 %collective-permute-start.2 = (f32[16,512]{1,0:T(8,128)S(1)}, f32[16,512]{1,0:T(8,128)S(1)}, u32[]{:S(2)}, u32[]{:S(2)}) collective-permute-start(f32[16,512]{1,0:T(8,128)S(1)} %get-tuple-element.30.sent_chip), channel_id=1, source_target_pairs={{1,2},{2,1},{3,4},{4,3},{5,6},{6,5},{9,10},{10,9},{11,12},{12,11},... | collective-permute-start | bytes 98312 | tf_op jit(solution)/shard_map/ppermute | solution.py:409
  10.1 0.1 collective-permute-start.3
  10.2 1.7 %collective-permute-done.2.got_chip.got1_chip = f32[16,512]{1,0:T(8,128)S(1)} collective-permute-done((f32[16,512]{1,0:T(8,128)S(1)}, f32[16,512]{1,0:T(8,128)S(1)}, u32[]{:S(2)}, u32[]{:S(2)}) %collective-permute-start.2) | collective-permute-done | bytes 32800 | tf_op jit(solution)/shard_map/ppermute | solution.py:409
  11.9 0.0 collective-permute-done.3.got_core.got1_core
  11.9 0.0 collective-permute-done.got_even.got1_even
  11.9 0.0 collective-permute-done.1.got_odd.got1_odd
  11.9 1.7 %shard_map.78 = (f32[16,16,256]{2,1,0:T(8,128)S(1)}, f32[16,16,256]{2,1,0:T(8,128)S(1)}, f32[64,256]{1,0:T(8,128)S(1)}, f32[64,256]{1,0:T(8,128)S(1)}, f32[16,25...) custom-call(f32[16,16,256]{2,1,0:T(8,128)S(1)} %get-tuple-element.22.tracer, ...), custom_call_target="tpu_custom_call" | custom-call | tf_op jit(solution)/shard_map/pallas_call | solution.py:450
  13.6 0.1 collective-permute-start.4
  13.7 4.1 %collective-permute-start.5 = (f32[64,256]{1,0:T(8,128)S(1)}, f32[64,256]{1,0:T(8,128)S(1)}, u32[]{:S(2)}, u32[]{:S(2)}) collective-permute-start(f32[64,256]{1,0:T(8,128)S(1)} %get-tuple-element.39), channel_id=1, source_target_pairs={{8,16},{16,8},{9,17},{17,9},{10,18},{18,10},{11,19},{19,11},{12,20... | collective-permute-start | bytes 196616 | tf_op jit(solution)/shard_map/ppermute | solution.py:408
  17.7 3.8 %collective-permute-start.6 = (f32[16,256]{1,0:T(8,128)S(1)}, f32[16,256]{1,0:T(8,128)S(1)}, u32[]{:S(2)}, u32[]{:S(2)}) collective-permute-start(f32[16,256]{1,0:T(8,128)S(1)} %get-tuple-element.40), channel_id=1, source_target_pairs={{1,2},{2,1},{3,4},{4,3},{5,6},{6,5},{9,10},{10,9},{11,12},{12,11},... | collective-permute-start | bytes 49160 | tf_op jit(solution)/shard_map/ppermute | solution.py:409
  21.5 0.1 collective-permute-start.7
  21.6 1.5 %collective-permute-done.6.got_chip = f32[16,256]{1,0:T(8,128)S(1)} collective-permute-done((f32[16,256]{1,0:T(8,128)S(1)}, f32[16,256]{1,0:T(8,128)S(1)}, u32[]{:S(2)}, u32[]{:S(2)}) %collective-permute-start.6) | collective-permute-done | bytes 16416 | tf_op jit(solution)/shard_map/ppermute | solution.py:409
  23.1 0.0 collective-permute-done.7.got_core
  23.1 0.0 collective-permute-done.4.got_even
  23.1 0.0 collective-permute-done.5.got_odd
  23.1 2.1 %shard_map.79 = (f32[16,16,256]{2,1,0:T(8,128)}, f32[16,16,256]{2,1,0:T(8,128)}) custom-call(f32[16,16,256]{2,1,0:T(8,128)S(1)} %get-tuple-element.22.tracer, f32[16,16,256]{2,1,0:T(8,128)S(1)} %get-tuple-element.23.east, f32[16,16,256]{2,1,0:T(8,128)S(1)} %get-tuple-element.24.north, f32[15,16,256]{2,1,0:T(8,128)S(1)} %get-tuple-element.25.mixing, ...), custom_call_target="tpu_custom_call" | custom-call | tf_op jit(solution)/shard_map/pallas_call | solution.py:460
Async XLA Ops:
  2.4 9.5 %collective-permute-start = (f32[88,256]{1,0:T(8,128)S(1)}, f32[88,256]{1,0:T(8,128)S(1)}, u32[]{:S(2)}, u32[]{:S(2)}) collective-permute-start(f32[88,256]{1,0:T(8,128)S(1)} %get-tuple-element.32), channel_id=1, source_target_pairs={{0,8},{8,0},{16,24},{24,16},{1,9},{9,1},{17,25},{25,17},{2,10},{10... | collective-permute-start | bytes 270344 | tf_op jit(solution)/shard_map/ppermute | solution.py:407
  3.7 8.2 %collective-permute-start.1 = (f32[88,256]{1,0:T(8,128)S(1)}, f32[88,256]{1,0:T(8,128)S(1)}, u32[]{:S(2)}, u32[]{:S(2)}) collective-permute-start(f32[88,256]{1,0:T(8,128)S(1)} %get-tuple-element.33), channel_id=1, source_target_pairs={{8,16},{16,8},{9,17},{17,9},{10,18},{18,10},{11,19},{19,11},{12,20... | collective-permute-start | bytes 270344 | tf_op jit(solution)/shard_map/ppermute | solution.py:408
  5.8 6.1 %collective-permute-start.2 = (f32[16,512]{1,0:T(8,128)S(1)}, f32[16,512]{1,0:T(8,128)S(1)}, u32[]{:S(2)}, u32[]{:S(2)}) collective-permute-start(f32[16,512]{1,0:T(8,128)S(1)} %get-tuple-element.30.sent_chip), channel_id=1, source_target_pairs={{1,2},{2,1},{3,4},{4,3},{5,6},{6,5},{9,10},{10,9},{11,12},{12,11},... | collective-permute-start | bytes 98312 | tf_op jit(solution)/shard_map/ppermute | solution.py:409
  10.1 1.7 %collective-permute-start.3 = (f32[16,512]{1,0:T(8,128)S(1)}, f32[16,512]{1,0:T(8,128)S(1)}, u32[]{:S(2)}, u32[]{:S(2)}) collective-permute-start(f32[16,512]{1,0:T(8,128)S(1)} %get-tuple-element.31.sent_core), channel_id=1, source_target_pairs={{0,1},{1,0},{2,3},{3,2},{4,5},{5,4},{6,7},{7,6},{8,9},{9,8},{10,11... | collective-permute-start | bytes 98312 | tf_op jit(solution)/shard_map/ppermute | solution.py:410
  13.6 9.5 %collective-permute-start.4 = (f32[64,256]{1,0:T(8,128)S(1)}, f32[64,256]{1,0:T(8,128)S(1)}, u32[]{:S(2)}, u32[]{:S(2)}) collective-permute-start(f32[64,256]{1,0:T(8,128)S(1)} %get-tuple-element.38), channel_id=1, source_target_pairs={{0,8},{8,0},{16,24},{24,16},{1,9},{9,1},{17,25},{25,17},{2,10},{10... | collective-permute-start | bytes 196616 | tf_op jit(solution)/shard_map/ppermute | solution.py:407
  13.7 9.4 %collective-permute-start.5 = (f32[64,256]{1,0:T(8,128)S(1)}, f32[64,256]{1,0:T(8,128)S(1)}, u32[]{:S(2)}, u32[]{:S(2)}) collective-permute-start(f32[64,256]{1,0:T(8,128)S(1)} %get-tuple-element.39), channel_id=1, source_target_pairs={{8,16},{16,8},{9,17},{17,9},{10,18},{18,10},{11,19},{19,11},{12,20... | collective-permute-start | bytes 196616 | tf_op jit(solution)/shard_map/ppermute | solution.py:408
  17.7 5.3 %collective-permute-start.6 = (f32[16,256]{1,0:T(8,128)S(1)}, f32[16,256]{1,0:T(8,128)S(1)}, u32[]{:S(2)}, u32[]{:S(2)}) collective-permute-start(f32[16,256]{1,0:T(8,128)S(1)} %get-tuple-element.40), channel_id=1, source_target_pairs={{1,2},{2,1},{3,4},{4,3},{5,6},{6,5},{9,10},{10,9},{11,12},{12,11},... | collective-permute-start | bytes 49160 | tf_op jit(solution)/shard_map/ppermute | solution.py:409
  21.5 1.6 %collective-permute-start.7 = (f32[16,256]{1,0:T(8,128)S(1)}, f32[16,256]{1,0:T(8,128)S(1)}, u32[]{:S(2)}, u32[]{:S(2)}) collective-permute-start(f32[16,256]{1,0:T(8,128)S(1)} %get-tuple-element.41), channel_id=1, source_target_pairs={{0,1},{1,0},{2,3},{3,2},{4,5},{5,4},{6,7},{7,6},{8,9},{9,8},{10,11... | collective-permute-start | bytes 49160 | tf_op jit(solution)/shard_map/ppermute | solution.py:410

commit v4 on v3

--- a/solution.py
+++ b/solution.py
@@ -143,6 +143,7 @@
         copy.wait()
     last = [jnp.zeros((rows, lanes), jnp.float32)] * 3
     first = last
+    side = [last[0]] * 2
     for k in range(levels - 1, -1, -1):
         if k < levels - 1:
             share = jnp.where(k + 1 < deep, mixing[k], 0.0) * inverse[k]
@@ -155,6 +156,11 @@
         items = (c, h, speed_x)
         last = [pack_last(k, item[:, -lanes:], packed) for item, packed in zip(items, last)]
         first = [pack_first(k, item[:, :lanes], packed) for item, packed in zip(items, first)]
+        items = (speed_y, mixing[k]) if k < levels - 1 else (speed_y,)
+        for i, item in enumerate(items):
+            tile = jnp.where(even_x, item[:, :lanes], item[:, -lanes:])
+            lane = index(tile.shape, 1) - slot * k
+            side[i] = jnp.where((lane >= 0) & (lane < 4), turned(tile, slot * k + 2, 1), side[i])
         pack_rows(k, levels, c, h, speed_y, k < shallow_y, up, down)
         at = 4 * levels + k
         down[at : at + 1, :] = speed_y[0:1]
@@ -168,7 +174,11 @@
     last.append(repeated(turned(depth_float[:, -lanes:], 4, 1)))
     first.append(repeated(turned(depth_float[:, :lanes], 2, 1)))
     last, first = jnp.concatenate(last, axis=1), jnp.concatenate(first, axis=1)
-    pay_chip[...] = jnp.where(even_x, first, last)
+    speed_y, mixed = side
+    speed_y = jnp.where(even_x, speed_y, turned(speed_y, 2, 1))
+    mixed = jnp.where(even_x, turned(mixed, 4, 1), turned(mixed, 6, 1))
+    side = jnp.where(lax.rem(index(mixed.shape, 1), slot) < 4, speed_y, mixed)
+    pay_chip[...] = jnp.concatenate([jnp.where(even_x, first, last), side], axis=1)
     pay_core[...] = jnp.where(even_x, last, first)
 
 
@@ -259,23 +269,143 @@
     return value[:, item * lanes : (item + 1) * lanes]
 
 
-def take(flag, first, second):
-    a, b = first[...], second[...]
-    return jnp.where(flag, b, a), jnp.where(flag, a, b)
+def take(flag, core, chip):
+    return jnp.where(flag, chip, core), jnp.where(flag, core, chip)
+
+
+def common(ref):
+    return ref[:, : 4 * lanes]
+
+
+def strip_rows(levels, message, up, down):
+    c, h, _, deep, side = (item_of(message, i) for i in range(5))
+    size = c.shape[0]
+    level = lax.div(index(c.shape, 1), slot).astype(jnp.float32)
+    is_open = level < jnp.minimum(deep, turned(deep, 1, 0))
+    carried = jnp.where(is_open, side * (h - turned(h, 1, 0)), 0.0)
+    at = 4 * levels
+    for ref in (up, down):
+        ref[at : at + sublanes, :] = jnp.zeros((sublanes, ref.shape[1]), jnp.float32)
+    end = size - 1
+    above = (c[end - 1 : end], c[end:], h[end:], carried[end:], deep[end:])
+    below = (c[0:1], c[1:2], h[0:1], carried[1:2], deep[0:1], side[0:1])
+    for ref, lines in ((up, above), (down, below)):
+        for i, line in enumerate(lines):
+            ref[at + i : at + i + 1, :lanes] = line
+
+
+def strip_states(levels, message, own, lower, upper, even):
+    c, h, speed, deep, side = (item_of(message, i) for i in range(5))
+    shape = c.shape
+    place = lax.rem(index(shape, 1), slot)
+    level = lax.div(index(shape, 1), slot).astype(jnp.float32)
+    from_own = place - jnp.where(even, 4, 0)
+    from_own = (from_own == 0) | (from_own == 1)
+
+    def joined(item, value):
+        mine = item_of(own, item)
+        return jnp.where(from_own, jnp.where(even, turned(mine, 2, 1), turned(mine, -2, 1)), value)
+
+    c, h, speed, deep = (joined(i, value) for i, value in enumerate((c, h, speed, deep)))
+    is_open = level < jnp.minimum(deep, turned(deep, 1, 1))
+    flux = face_flux(c, turned(c, 1, 1), turned(c, -1, 1), turned(c, 2, 1), speed, is_open)
+    jump = jnp.where(is_open, h - turned(h, 1, 1), 0.0)
+    carried = speed * jump
+    plus = 7.0 * carried + diffusivity * jump
+    minus = 7.0 * carried - diffusivity * jump
+    forward = flux - turned(flux, -1, 1)
+    backward = minus + turned(plus, -1, 1) - turned(carried, 1, 1) - turned(carried, -2, 1)
+
+    def line(ref, item):
+        at = 4 * levels + item
+        return jnp.broadcast_to(ref[at : at + 1, :lanes], (sublanes, lanes))
+
+    def row_of(value, at):
+        return jnp.broadcast_to(value[at : at + 1], (sublanes, lanes))
+
+    rows = shape[0]
+    row = index((sublanes, lanes), 0)
+    tile_level = level[:sublanes]
+    previous = turned(deep, 1, 0)
+    previous = jnp.concatenate([jnp.where(row == 0, line(lower, 4), previous[:sublanes]), previous[sublanes:]], axis=0)
+    opens = split(level < jnp.minimum(deep, previous), 0)
+    speeds = split(side, 0)
+    is_open = tile_level < jnp.minimum(line(upper, 4), row_of(deep, rows - 1))
+    speed_end = line(upper, 5)
+    c_one, c_two = row_of(c, rows - 1), row_of(c, rows - 2)
+    flux = face_flux(line(upper, 0), c_one, line(upper, 1), c_two, speed_end, is_open)
+    jump = jnp.where(is_open, line(upper, 2) - row_of(h, rows - 1), 0.0)
+    carried = speed_end * jump
+    plus = 7.0 * carried + diffusivity * jump
+    edges = (line(lower, 1), jnp.where(row == 0, line(lower, 0), line(lower, 1)), line(upper, 0), flux)
+    forward = forward + explicit_flux(split(c, 0), speeds, opens, 0, edges)
+    edges = (line(lower, 2), plus, line(lower, 3), jnp.where(row == sublanes - 2, carried, line(upper, 3)))
+    backward = backward + reverse_flux(split(h, 0), speeds, opens, 0, edges)
+    right = jnp.where(level < deep, c + forward - uptake * c * c, 0.0)
+    linear = h + backward
+    kept = (place == 2) | (place == 3)
+    links = jnp.where(kept & (level + 1.0 < deep), turned(side, -4, 1), 0.0)
+
+    def ready(value):
+        return jnp.where(even, turned(value, -4, 1), turned(value, -2, 1))
+
+    def levels_of(value):
+        value = ready(value)
+        return [turned(value, -slot * k, 1) for k in range(levels)]
+
+    right, linear, links, weights = (levels_of(value) for value in (right, linear, links, h))
+    deep = ready(deep)
+    inverse, passed = [], []
+    above = jnp.zeros(shape, jnp.float32)
+    share = above
+    current = above
+    for k in range(levels):
+        inv = 1.0 / (1.0 + links[k] + (above - above * share))
+        current = (right[k] + above * current) * inv
+        share = links[k] * inv
+        above = links[k]
+        inverse.append(inv)
+        passed.append(current)
+    state = [current]
+    for k in range(levels - 2, -1, -1):
+        current = passed[k] + (links[k] * inverse[k]) * current
+        state.insert(0, current)
+    passed = []
+    current = jnp.zeros(shape, jnp.float32)
+    for k in range(levels):
+        value = linear[k] - (2.0 * uptake) * state[k] * weights[k]
+        if k > 0:
+            value = value + links[k - 1] * current
+        current = value * inverse[k]
+        passed.append(current)
+    weight = [current]
+    for k in range(levels - 2, -1, -1):
+        current = passed[k] + (links[k] * inverse[k]) * current
+        weight.insert(0, current)
+    lane = index(shape, 1)
+    packed_state = jnp.zeros(shape, jnp.float32)
+    packed_weight = packed_state
+    for k in range(levels):
+        here = lax.rem(lane + (lanes + 2 - slot * k), lanes) < 4
+        packed_state = jnp.where(here, turned(state[k], slot * k, 1), packed_state)
+        value = jnp.where(k < deep, weight[k], 0.0)
+        packed_weight = jnp.where(here, turned(value, slot * k, 1), packed_weight)
+    back = lambda value: jnp.where(even, turned(value, 4, 1), turned(value, 2, 1))
+    return back(packed_state), back(packed_weight)
 
 
 def first_kernel(
     tracer, east, north, mixing, depth, inverse, weight, own_up, sent_chip, sent_core,
     got_even, got_odd, got_chip, got_core,
-    state, weight_next, pay_even, pay_odd, pay_chip, pay_core, up, own_last,
+    state, weight_next, pay_even, pay_odd, pay_core, up, own_last,
     passed, linear, lower, upper, edge, down,
 ):
     levels, rows, columns = tracer.shape
     even_y, even_x = parities()
     choose(even_y, got_odd, got_even, lower)
     choose(even_y, got_even, got_odd, upper)
-    before, after = take(even_x, got_core, got_chip)
-    own = jnp.where(even_x, sent_core[...], sent_chip[...])
+    before, after = take(even_x, got_core[...], common(got_chip))
+    own = jnp.where(even_x, sent_core[...], common(sent_chip))
     deep = depth[...]
     at = 5 * levels
     depth_float = deep.astype(jnp.float32)
@@ -327,17 +457,17 @@
         last = [pack_last(k, item[:, -lanes:], packed) for item, packed in zip(items, last)]
         first = [pack_first(k, item[:, :lanes], packed) for item, packed in zip(items, first)]
         pack_rows(k, levels, c, h, north[k] * (1.0 / 12.0), k < shallow_y, up, down)
+    strip_rows(levels, got_chip[...], up, down)
     choose(even_y, up, down, pay_even)
     choose(even_y, down, up, pay_odd)
     last, first = jnp.concatenate(last, axis=1), jnp.concatenate(first, axis=1)
     own_last[...] = last
-    pay_chip[...] = jnp.where(even_x, first, last)
     pay_core[...] = jnp.where(even_x, last, first)
 
 
 def second_kernel(
     tracer, east, north, mixing, depth, inverse, state, weight, own_up, own_last, sent_chip, sent_core,
-    got1_even, got1_odd, got1_chip, got1_core, got_even, got_odd, got_chip, got_core,
+    got1_even, got1_odd, got1_chip, got1_core, got_even, got_odd, got_core,
     final_far, adjoint_far,
     final, adjoint, passed, lower, upper, edge, sent,
 ):
@@ -352,9 +482,10 @@
     even_y, even_x = parities()
     choose(even_y, got_odd, got_even, lower)
     choose(even_y, got_even, got_odd, upper)
-    before1, after1 = take(even_x, got1_core, got1_chip)
-    before, after = take(even_x, got_core, got_chip)
-    own1 = jnp.where(even_x, sent_core[...], sent_chip[...])
+    before1, after1 = take(even_x, got1_core[...], common(got1_chip))
+    strip = strip_states(levels, got1_chip[...], sent_chip[...], lower, upper, even_x)
+    before, after = take(even_x, got_core[...], jnp.concatenate(strip, axis=1))
+    own1 = jnp.where(even_x, sent_core[...], common(sent_chip))
     deep = depth[...]
     depth_float = deep.astype(jnp.float32)
     at = 5 * levels
@@ -403,12 +534,11 @@
     return swaps
 
 
-def exchange(pay_even, pay_odd, pay_chip, pay_core):
+def exchange(pay_even, pay_odd, *pay):
     got_even = lax.ppermute(pay_even, "group", pairs("group", 0))
     got_odd = lax.ppermute(pay_odd, "group", pairs("group", 1))
-    got_chip = lax.ppermute(pay_chip, "tile", pairs("tile", 1))
-    got_core = lax.ppermute(pay_core, "tile", pairs("tile", 0))
-    return got_even, got_odd, got_chip, got_core
+    got = [lax.ppermute(each, "tile", pairs("tile", len(pay) - 1 - i)) for i, each in enumerate(pay)]
+    return got_even, got_odd, *got
 
 
 def shards(tracer, east_speed, north_speed, mixing, depth_levels, sensitivity):
@@ -417,7 +547,7 @@
     f32 = jnp.float32
     field = jax.ShapeDtypeStruct((levels, rows, columns), f32)
     first_size = 5 * levels + sublanes
-    second_size = 4 * levels
+    second_size = 4 * levels + sublanes
     edge_size = 9 * levels
     block = pltpu.VMEM((levels, rows, columns), f32)
     params = pltpu.CompilerParams(vmem_limit_bytes=32 * 1024 * 1024)
@@ -439,7 +569,7 @@
         factor_kernel,
         in_specs=[far] * 6,
         out_shape=near
-        + (field, field, lines(first_size), lines(first_size), tiles(4), tiles(4), lines(first_size)),
+        + (field, field, lines(first_size), lines(first_size), tiles(5), tiles(4), lines(first_size)),
         scratch_shapes=[block, block, space(first_size), pltpu.SemaphoreType.DMA((6,))],
         compiler_params=params,
     )(*distant)
@@ -449,7 +579,7 @@
     sent1 = messages[2:]
     state, weight_next, *messages, up2, last2 = pl.pallas_call(
         first_kernel,
-        out_shape=(field, field, lines(second_size), lines(second_size), tiles(2), tiles(2), lines(second_size), tiles(2)),
+        out_shape=(field, field, lines(second_size), lines(second_size), tiles(2), lines(second_size), tiles(2)),
         scratch_shapes=[
             block, block, space(first_size), space(first_size), space(edge_size), space(second_size),
         ],

time: 25.5 us -> 24.5 us (0.961)
  the two profiles are of different devices: /device:TPU:13 before, /device:TPU:10 now
where the time goes in v4:
time: 24.5 us; the launch traced here: 24.3 us
  starting transfers between devices  11.1 us (45%)
  waiting for transfers between devices  6.32 us (26%)
  Pallas kernels  6.1 us (25%)
  between operations  0.69 us (3%)
    ppermute x2, starting transfers between devices, exchange(): got_odd = lax.ppermute(pay_odd, 'group', pairs('group', 1))  6.73 us
    ppermute x3, starting transfers between devices, exchange(): lax.ppermute(each, 'tile', pairs('tile', len(pay) - 1 - i))  3.74 us
    ppermute x3, waiting for transfers between devices, exchange(): lax.ppermute(each, 'tile', pairs('tile', len(pay) - 1 - i))  2.82 us
    ppermute x2, waiting for transfers between devices, exchange(): got_odd = lax.ppermute(pay_odd, 'group', pairs('group', 1))  2.81 us
    pallas_call x1, Pallas kernels, shards(): pl.pallas_call(second_kernel, out_specs=[far] * 2, out_shape=(field, fiel...  2.6 us
    pallas_call x1, Pallas kernels, shards(): pl.pallas_call(factor_kernel, in_specs=[far] * 6, out_shape=near + (field...  1.89 us
    pallas_call x1, Pallas kernels, shards(): pl.pallas_call(first_kernel, out_shape=(field, field, lines(second_size),...  1.61 us
    ppermute x2, waiting for transfers between devices, exchange(): got_even = lax.ppermute(pay_even, 'group', pairs('group', 0))  0.7 us
  transfers between devices with their start and end apart: 7, of which 5 were waited for; matrix products, arithmetic and copies ran while one was open for 0% of the time, Pallas kernels for 0%

profile of v4, /device:TPU:10, one launch (start us, length us, event | category | flops | bytes accessed | tf_op | source)
XLA Modules:
  0.0 24.3 jit_solution(17452192398320765600)
XLA Ops:
  0.6 1.9 %shard_map.77 = (f32[16,16,256]{2,1,0:T(8,128)S(1)}, f32[16,16,256]{2,1,0:T(8,128)S(1)}, f32[16,16,256]{2,1,0:T(8,128)S(1)}, f32[15,16,256]{2,1,0:T(8,128)S(1)},...) custom-call(f32[16,16,256]{2,1,0:T(8,128)} %tracer_far.1, ...), custom_call_target="tpu_custom_call" | custom-call | tf_op jit(solution)/shard_map/pallas_call | solution.py:568
  2.5 0.6 %collective-permute-start = (f32[88,256]{1,0:T(8,128)S(1)}, f32[88,256]{1,0:T(8,128)S(1)}, u32[]{:S(2)}, u32[]{:S(2)}) collective-permute-start(f32[88,256]{1,0:T(8,128)S(1)} %get-tuple-element.31), channel_id=1, source_target_pairs={{0,8},{8,0},{16,24},{24,16},{1,9},{9,1},{17,25},{25,17},{2,10},{10... | collective-permute-start | bytes 270344 | tf_op jit(solution)/shard_map/ppermute | solution.py:538
  3.1 4.3 %collective-permute-start.1 = (f32[88,256]{1,0:T(8,128)S(1)}, f32[88,256]{1,0:T(8,128)S(1)}, u32[]{:S(2)}, u32[]{:S(2)}) collective-permute-start(f32[88,256]{1,0:T(8,128)S(1)} %get-tuple-element.32), channel_id=1, source_target_pairs={{8,16},{16,8},{9,17},{17,9},{10,18},{18,10},{11,19},{19,11},{12,20... | collective-permute-start | bytes 270344 | tf_op jit(solution)/shard_map/ppermute | solution.py:539
  7.5 1.9 %collective-permute-start.2 = (f32[16,640]{1,0:T(8,128)S(1)}, f32[16,640]{1,0:T(8,128)S(1)}, u32[]{:S(2)}, u32[]{:S(2)}) collective-permute-start(f32[16,640]{1,0:T(8,128)S(1)} %get-tuple-element.29.sent_chip), channel_id=1, source_target_pairs={{1,2},{2,1},{3,4},{4,3},{5,6},{6,5},{9,10},{10,9},{11,12},{12,11},... | collective-permute-start | bytes 122888 | tf_op jit(solution)/shard_map/ppermute | solution.py:540
  9.4 1.7 %collective-permute-start.3 = (f32[16,512]{1,0:T(8,128)S(1)}, f32[16,512]{1,0:T(8,128)S(1)}, u32[]{:S(2)}, u32[]{:S(2)}) collective-permute-start(f32[16,512]{1,0:T(8,128)S(1)} %get-tuple-element.30.sent_core), channel_id=1, source_target_pairs={{0,1},{1,0},{2,3},{3,2},{4,5},{5,4},{6,7},{7,6},{8,9},{9,8},{10,11... | collective-permute-start | bytes 98312 | tf_op jit(solution)/shard_map/ppermute | solution.py:540
  11.2 0.9 %collective-permute-done.3.got_core.got1_core = f32[16,512]{1,0:T(8,128)S(1)} collective-permute-done((f32[16,512]{1,0:T(8,128)S(1)}, f32[16,512]{1,0:T(8,128)S(1)}, u32[]{:S(2)}, u32[]{:S(2)}) %collective-permute-start.3) | collective-permute-done | bytes 32800 | tf_op jit(solution)/shard_map/ppermute | solution.py:540
  12.0 0.8 %collective-permute-done.2.got_chip.got1_chip = f32[16,640]{1,0:T(8,128)S(1)} collective-permute-done((f32[16,640]{1,0:T(8,128)S(1)}, f32[16,640]{1,0:T(8,128)S(1)}, u32[]{:S(2)}, u32[]{:S(2)}) %collective-permute-start.2) | collective-permute-done | bytes 40992 | tf_op jit(solution)/shard_map/ppermute | solution.py:540
  12.8 0.0 collective-permute-done.got_even.got1_even
  12.8 0.0 collective-permute-done.1.got_odd.got1_odd
  12.8 1.6 %shard_map.78 = (f32[16,16,256]{2,1,0:T(8,128)S(1)}, f32[16,16,256]{2,1,0:T(8,128)S(1)}, f32[72,256]{1,0:T(8,128)S(1)}, f32[72,256]{1,0:T(8,128)S(1)}, f32[16,25...) custom-call(f32[16,16,256]{2,1,0:T(8,128)S(1)} %get-tuple-element.21.tracer, ...), custom_call_target="tpu_custom_call" | custom-call | tf_op jit(solution)/shard_map/pallas_call | solution.py:580
  14.4 0.1 collective-permute-start.4
  14.5 2.4 %collective-permute-start.5 = (f32[72,256]{1,0:T(8,128)S(1)}, f32[72,256]{1,0:T(8,128)S(1)}, u32[]{:S(2)}, u32[]{:S(2)}) collective-permute-start(f32[72,256]{1,0:T(8,128)S(1)} %get-tuple-element.38), channel_id=1, source_target_pairs={{8,16},{16,8},{9,17},{17,9},{10,18},{18,10},{11,19},{19,11},{12,20... | collective-permute-start | bytes 221192 | tf_op jit(solution)/shard_map/ppermute | solution.py:539
  16.9 0.1 collective-permute-start.6
  17.0 1.2 %collective-permute-done.6.got_core = f32[16,256]{1,0:T(8,128)S(1)} collective-permute-done((f32[16,256]{1,0:T(8,128)S(1)}, f32[16,256]{1,0:T(8,128)S(1)}, u32[]{:S(2)}, u32[]{:S(2)}) %collective-permute-start.6) | collective-permute-done | bytes 16416 | tf_op jit(solution)/shard_map/ppermute | solution.py:540
  18.2 0.7 %collective-permute-done.4.got_even = f32[72,256]{1,0:T(8,128)S(1)} collective-permute-done((f32[72,256]{1,0:T(8,128)S(1)}, f32[72,256]{1,0:T(8,128)S(1)}, u32[]{:S(2)}, u32[]{:S(2)}) %collective-permute-start.4) | collective-permute-done | bytes 73760 | tf_op jit(solution)/shard_map/ppermute | solution.py:538
  18.8 2.8 %collective-permute-done.5.got_odd = f32[72,256]{1,0:T(8,128)S(1)} collective-permute-done((f32[72,256]{1,0:T(8,128)S(1)}, f32[72,256]{1,0:T(8,128)S(1)}, u32[]{:S(2)}, u32[]{:S(2)}) %collective-permute-start.5) | collective-permute-done | bytes 73760 | tf_op jit(solution)/shard_map/ppermute | solution.py:539
  21.7 2.6 %shard_map.79 = (f32[16,16,256]{2,1,0:T(8,128)}, f32[16,16,256]{2,1,0:T(8,128)}) custom-call(f32[16,16,256]{2,1,0:T(8,128)S(1)} %get-tuple-element.21.tracer, f32[16,16,256]{2,1,0:T(8,128)S(1)} %get-tuple-element.22.east, f32[16,16,256]{2,1,0:T(8,128)S(1)} %get-tuple-element.23.north, f32[15,16,256]{2,1,0:T(8,128)S(1)} %get-tuple-element.24.mixing, ...), custom_call_target="tpu_custom_call" | custom-call | tf_op jit(solution)/shard_map/pallas_call | solution.py:590
Async XLA Ops:
  2.5 10.3 %collective-permute-start = (f32[88,256]{1,0:T(8,128)S(1)}, f32[88,256]{1,0:T(8,128)S(1)}, u32[]{:S(2)}, u32[]{:S(2)}) collective-permute-start(f32[88,256]{1,0:T(8,128)S(1)} %get-tuple-element.31), channel_id=1, source_target_pairs={{0,8},{8,0},{16,24},{24,16},{1,9},{9,1},{17,25},{25,17},{2,10},{10... | collective-permute-start | bytes 270344 | tf_op jit(solution)/shard_map/ppermute | solution.py:538
  3.1 9.7 %collective-permute-start.1 = (f32[88,256]{1,0:T(8,128)S(1)}, f32[88,256]{1,0:T(8,128)S(1)}, u32[]{:S(2)}, u32[]{:S(2)}) collective-permute-start(f32[88,256]{1,0:T(8,128)S(1)} %get-tuple-element.32), channel_id=1, source_target_pairs={{8,16},{16,8},{9,17},{17,9},{10,18},{18,10},{11,19},{19,11},{12,20... | collective-permute-start | bytes 270344 | tf_op jit(solution)/shard_map/ppermute | solution.py:539
  7.5 5.3 %collective-permute-start.2 = (f32[16,640]{1,0:T(8,128)S(1)}, f32[16,640]{1,0:T(8,128)S(1)}, u32[]{:S(2)}, u32[]{:S(2)}) collective-permute-start(f32[16,640]{1,0:T(8,128)S(1)} %get-tuple-element.29.sent_chip), channel_id=1, source_target_pairs={{1,2},{2,1},{3,4},{4,3},{5,6},{6,5},{9,10},{10,9},{11,12},{12,11},... | collective-permute-start | bytes 122888 | tf_op jit(solution)/shard_map/ppermute | solution.py:540
  9.4 2.6 %collective-permute-start.3 = (f32[16,512]{1,0:T(8,128)S(1)}, f32[16,512]{1,0:T(8,128)S(1)}, u32[]{:S(2)}, u32[]{:S(2)}) collective-permute-start(f32[16,512]{1,0:T(8,128)S(1)} %get-tuple-element.30.sent_core), channel_id=1, source_target_pairs={{0,1},{1,0},{2,3},{3,2},{4,5},{5,4},{6,7},{7,6},{8,9},{9,8},{10,11... | collective-permute-start | bytes 98312 | tf_op jit(solution)/shard_map/ppermute | solution.py:540
  14.4 4.4 %collective-permute-start.4 = (f32[72,256]{1,0:T(8,128)S(1)}, f32[72,256]{1,0:T(8,128)S(1)}, u32[]{:S(2)}, u32[]{:S(2)}) collective-permute-start(f32[72,256]{1,0:T(8,128)S(1)} %get-tuple-element.37), channel_id=1, source_target_pairs={{0,8},{8,0},{16,24},{24,16},{1,9},{9,1},{17,25},{25,17},{2,10},{10... | collective-permute-start | bytes 221192 | tf_op jit(solution)/shard_map/ppermute | solution.py:538
  14.5 7.1 %collective-permute-start.5 = (f32[72,256]{1,0:T(8,128)S(1)}, f32[72,256]{1,0:T(8,128)S(1)}, u32[]{:S(2)}, u32[]{:S(2)}) collective-permute-start(f32[72,256]{1,0:T(8,128)S(1)} %get-tuple-element.38), channel_id=1, source_target_pairs={{8,16},{16,8},{9,17},{17,9},{10,18},{18,10},{11,19},{19,11},{12,20... | collective-permute-start | bytes 221192 | tf_op jit(solution)/shard_map/ppermute | solution.py:539
  16.9 1.2 %collective-permute-start.6 = (f32[16,256]{1,0:T(8,128)S(1)}, f32[16,256]{1,0:T(8,128)S(1)}, u32[]{:S(2)}, u32[]{:S(2)}) collective-permute-start(f32[16,256]{1,0:T(8,128)S(1)} %get-tuple-element.39), channel_id=1, source_target_pairs={{0,1},{1,0},{2,3},{3,2},{4,5},{5,4},{6,7},{7,6},{8,9},{9,8},{10,11... | collective-permute-start | bytes 49160 | tf_op jit(solution)/shard_map/ppermute | solution.py:540

commit v5 on v4

--- a/solution.py
+++ b/solution.py
@@ -108,8 +108,8 @@
 
 def factor_kernel(
     tracer_far, east_far, north_far, mixing_far, depth_far, sensitivity_far,
-    tracer, east, north, mixing, depth, inverse, weight, pay_even, pay_odd, pay_chip, pay_core, up,
-    sensitivity, passed, down, arrived,
+    tracer, east, north, mixing, depth, inverse, weight, pay_even, pay_odd, pay_chip, pay_core, up, down, beside,
+    sensitivity, passed, arrived,
 ):
     order = (
         (depth_far, depth),
@@ -164,9 +164,10 @@
         pack_rows(k, levels, c, h, speed_y, k < shallow_y, up, down)
         at = 4 * levels + k
         down[at : at + 1, :] = speed_y[0:1]
+        up[at : at + 1, :] = speed_y[rows - 1 :]
+        beside[k : k + 1, :] = speed_y[1:2]
     depth_float = deep.astype(jnp.float32)
     at = 5 * levels
-    up[4 * levels : at, :] = jnp.zeros((levels, columns), jnp.float32)
     up[at : at + sublanes, :] = jnp.broadcast_to(depth_float[rows - 1 :], (sublanes, columns))
     down[at : at + sublanes, :] = jnp.broadcast_to(depth_float[0:1], (sublanes, columns))
     choose(even_y, up, down, pay_even)
@@ -182,87 +183,127 @@
     pay_core[...] = jnp.where(even_x, last, first)
 
 
-def edges_y(levels, lower, upper, own, given, edge):
-    rows_of = lambda ref, item: ref[item * levels : (item + 1) * levels, :]
-    c, c_next, h, carried_next = (rows_of(upper, i) for i in range(4))
-    c_two, c_one, h_one = (rows_of(own, i) for i in range(3))
-    speed, deep, own_deep = given
-    level = index(c.shape, 0).astype(jnp.float32)
-    is_open = level < jnp.minimum(deep, own_deep)
-    flux = face_flux(c, c_one, c_next, c_two, speed, is_open)
-    jump = jnp.where(is_open, h - h_one, 0.0)
-    carried = speed * jump
-    total = 7.0 * carried + diffusivity * jump
-    below = tuple(rows_of(lower, i) for i in range(4))
-    for item, value in enumerate(below + (c, flux, total, carried, carried_next)):
-        edge[item * levels : (item + 1) * levels, :] = value
-
-
-def edges_x(before, after, own_last, speeds, depths):
-    c_before, h_before = before
-    c_after, h_after = after
-    c_own, h_own = own_last
-    speed_before, speed_after = speeds
-    deep_before, deep_after, deep_own = depths
-    shape = c_before.shape
+def rows_of(ref, item, levels):
+    return ref[item * levels : (item + 1) * levels, :]
+
+
+def borders_y(levels, lower, upper, up, down, speeds, deep, deeps, border):
+    c_far, c_near, h_near, g_near = (rows_of(lower, i, levels) for i in range(4))
+    c_next, c_over, h_next, g_over = (rows_of(upper, i, levels) for i in range(4))
+    c_two, c_one, h_one = (rows_of(up, i, levels) for i in range(3))
+    c_zero, c_first, h_zero = (rows_of(down, i, levels) for i in range(3))
+    speed_start, speed_first, speed_last, speed_end = speeds
+    deep_before, deep_after = deeps
+    end = deep.shape[0] - 1
+    level = index(c_next.shape, 0).astype(jnp.float32)
+    start_open = level < jnp.minimum(deep_before, deep[0:1])
+    first_open = level < jnp.minimum(deep[0:1], deep[1:2])
+    last_open = level < jnp.minimum(deep[end - 1 : end], deep[end:])
+    end_open = level < jnp.minimum(deep[end:], deep_after)
+    start = face_flux(c_zero, c_near, c_first, c_far, speed_start, start_open)
+    first = jnp.where(first_open, -speed_first * c_near, 0.0)
+    last = jnp.where(last_open, -speed_last * c_next, 0.0)
+    finish = face_flux(c_next, c_one, c_over, c_two, speed_end, end_open)
+    start_jump = jnp.where(start_open, h_zero - h_near, 0.0)
+    end_jump = jnp.where(end_open, h_next - h_one, 0.0)
+    start_carried = speed_start * start_jump
+    end_carried = speed_end * end_jump
+    values = (
+        start - first,
+        first,
+        -last,
+        last - finish,
+        7.0 * start_carried - diffusivity * start_jump - g_near,
+        -start_carried,
+        -end_carried,
+        7.0 * end_carried + diffusivity * end_jump - g_over,
+    )
+    for item, value in enumerate(values):
+        border[item * levels : (item + 1) * levels, :] = value
+
+
+def borders_x(before, after, first, last):
+    shape = before[0].shape
     place = lax.rem(index(shape, 1), slot)
     level = lax.div(index(shape, 1), slot).astype(jnp.float32)
-    inner = place < 2
-    c = jnp.where(inner, turned(c_own, -2, 1), c_after)
-    h = jnp.where(inner, turned(h_own, -2, 1), h_after)
-    deep = jnp.where(inner, turned(deep_own, -2, 1), deep_after)
-    is_open = level < jnp.minimum(deep, turned(deep, 1, 1))
-    flux = face_flux(c, turned(c, 1, 1), turned(c, -1, 1), turned(c, 2, 1), speed_after, is_open)
-    jump = jnp.where(is_open, h - turned(h, 1, 1), 0.0)
-    carried = speed_after * jump
-    total = 7.0 * carried + diffusivity * jump
-    is_open = level < jnp.minimum(deep_before, turned(deep_before, 1, 1))
-    carried_before = jnp.where(is_open, speed_before * (h_before - turned(h_before, 1, 1)), 0.0)
-    start = place < 4
+
+    def faces(items):
+        c, h, speed, deep = items
+        is_open = level < jnp.minimum(deep, turned(deep, 1, 1))
+        flux = face_flux(c, turned(c, 1, 1), turned(c, -1, 1), turned(c, 2, 1), speed, is_open)
+        jump = jnp.where(is_open, h - turned(h, 1, 1), 0.0)
+        return is_open, flux, jump, speed * jump
+
+    c, _, speed, _ = items = [jnp.where(place < 4, a, turned(b, 2, 1)) for a, b in zip(before, first)]
+    is_open, flux, jump, carried = faces(items)
+    inner = jnp.where((place == 5) & is_open, -speed * turned(c, 2, 1), 0.0)
+    forward = jnp.where(place == 4, flux, inner) - turned(inner, -1, 1)
+    backward = jnp.where(place == 4, 7.0 * carried - diffusivity * jump, 0.0) - turned(carried, 1, 1)
+    c, _, speed, _ = items = [jnp.where(place < 2, turned(b, -2, 1), a) for a, b in zip(after, last)]
+    is_open, flux, jump, carried = faces(items)
+    inner = jnp.where((place == 1) & is_open, -speed * turned(c, -1, 1), 0.0)
+    forward_end = inner - turned(jnp.where(place == 2, flux, inner), -1, 1)
+    total = turned(7.0 * carried + diffusivity * jump, -1, 1)
+    backward_end = jnp.where(place == 1, total, 0.0) - turned(carried, -2, 1)
+    start = place < 2
     return (
-        jnp.where(start, turned(c_before, -2, 1), turned(c, -3, 1)),
-        jnp.where(start, turned(c_before, -3, 1), turned(flux, -3, 1)),
-        jnp.where(start, turned(h_before, -3, 1), turned(total, -3, 1)),
-        jnp.where(start, turned(carried_before, -3, 1), turned(carried, -4, 1)),
+        jnp.where(start, turned(forward, -4, 1), turned(forward_end, -2, 1)),
+        jnp.where(start, turned(backward, -4, 1), turned(backward_end, -2, 1)),
     )
 
 
-def step_levels(first, levels, c, h, east_part, north_part, shallow, edge, packed):
+def bordered(k, levels, value, border, item, packed):
+    rows, columns = value.shape
+    row = index((sublanes, columns), 0)
+
+    def line(which):
+        at = (item + which) * levels + k
+        return jnp.broadcast_to(border[at : at + 1, :], (sublanes, columns))
+
+    tiles = split(value, 0)
+    tiles[0] = tiles[0] + jnp.where(row == 0, line(0), jnp.where(row == 1, line(1), 0.0))
+    added = jnp.where(row == sublanes - 2, line(2), jnp.where(row == sublanes - 1, line(3), 0.0))
+    tiles[-1] = tiles[-1] + added
+    value = jnp.concatenate(tiles, axis=0)
+    lead = turned(packed, -slot * k, 1)
+    lane = index(lead.shape, 1)
+    tiles = [value[:, i : i + lanes] for i in range(0, columns, lanes)]
+    tiles[0] = tiles[0] + jnp.where(lane < 2, lead, 0.0)
+    tiles[-1] = tiles[-1] + jnp.where(lane >= lanes - 2, lead, 0.0)
+    return jnp.concatenate(tiles, axis=1)
+
+
+def step_levels(first, c, h, east_part, north_part, shallow):
     count, rows, columns = c.shape
     shallow_x, shallow_y = shallow
-    inside = range(first, first + count)
     level = index((count, rows, columns), 0) + first
-
-    lead = [jnp.stack([turned(tile, -slot * k, 1) for k in inside]) for tile in packed]
+    none = (0.0, 0.0, 0.0, 0.0)
     speeds = split(east_part * (1.0 / 12.0), 2)
     opens = split(level < shallow_x[None], 2)
-    forward = explicit_flux(split(c, 2), speeds, opens, 2, (lead[1], lead[0], lead[0], lead[1]))
-    backward = reverse_flux(split(h, 2), speeds, opens, 2, (lead[2], lead[2], lead[3], lead[3]))
-
-    def line(item):
-        at = item * levels
-        return jnp.stack([jnp.broadcast_to(edge[at + k : at + k + 1, :], (sublanes, columns)) for k in inside])
-
-    row = index((count, sublanes, columns), 1)
+    forward = explicit_flux(split(c, 2), speeds, opens, 2, none)
+    backward = reverse_flux(split(h, 2), speeds, opens, 2, none)
     speeds = split(north_part * (1.0 / 12.0), 1)
     opens = split(level < shallow_y[None], 1)
-    one = line(1)
-    edges = (one, jnp.where(row == 0, line(0), one), line(4), line(5))
-    forward = forward + explicit_flux(split(c, 1), speeds, opens, 1, edges)
-    edges = (line(2), line(6), line(3), jnp.where(row == sublanes - 2, line(7), line(8)))
-    backward = backward + reverse_flux(split(h, 1), speeds, opens, 1, edges)
+    forward = forward + explicit_flux(split(c, 1), speeds, opens, 1, none)
+    backward = backward + reverse_flux(split(h, 1), speeds, opens, 1, none)
     return forward, h + backward
 
 
-def shallow_faces(deep, deep_before, deep_lower):
-    rows, columns = deep.shape
-    previous = turned(deep, 1, 1)
-    head = jnp.where(index((rows, lanes), 1) == 0, turned(deep_before, -3, 1), previous[:, :lanes])
-    previous_x = jnp.concatenate([head, previous[:, lanes:]], axis=1)
-    previous = turned(deep, 1, 0)
-    head = jnp.where(index((sublanes, columns), 0) == 0, deep_lower, previous[:sublanes])
-    previous_y = jnp.concatenate([head, previous[sublanes:]], axis=0)
-    return jnp.minimum(deep, previous_x).astype(jnp.int32), jnp.minimum(deep, previous_y).astype(jnp.int32)
+def inner_kernel(c_ref, h_ref, east, north, depth, *rest):
+    *tracer, forward, linear = rest
+    levels, rows, columns = c_ref.shape
+    deep = depth[...]
+    lane, row = index(deep.shape, 1), index(deep.shape, 0)
+    shallow_x = jnp.where(lane == 0, 0, jnp.minimum(deep, turned(deep, 1, 1)))
+    shallow_y = jnp.where(row == 0, 0, jnp.minimum(deep, turned(deep, 1, 0)))
+    for k in range(0, levels, group_size):
+        part = slice(k, min(k + group_size, levels))
+        c, h = c_ref[part], h_ref[part]
+        ahead, back = step_levels(k, c, h, east[part], north[part], (shallow_x, shallow_y))
+        if tracer:
+            back = back - (2.0 * uptake) * tracer[0][part] * h
+        linear[part] = back
+        forward[part] = c + ahead - uptake * c * c
 
 
 def item_of(value, item):
@@ -395,41 +436,30 @@
 
 
 def first_kernel(
-    tracer, east, north, mixing, depth, inverse, weight, own_up, sent_chip, sent_core,
+    north, mixing, depth, inverse, weight, forward, linear, own_up, own_down, beside, sent_chip, sent_core,
     got_even, got_odd, got_chip, got_core,
-    state, weight_next, pay_even, pay_odd, pay_core, up, own_last,
-    passed, linear, lower, upper, edge, down,
+    state, weight_next, pay_even, pay_odd, pay_core, up, down, own_first, own_last,
+    passed, lower, upper, border,
 ):
-    levels, rows, columns = tracer.shape
+    levels, rows, columns = weight.shape
     even_y, even_x = parities()
     choose(even_y, got_odd, got_even, lower)
     choose(even_y, got_even, got_odd, upper)
     before, after = take(even_x, got_core[...], common(got_chip))
-    own = jnp.where(even_x, sent_core[...], common(sent_chip))
+    last, first = take(even_x, common(sent_chip), sent_core[...])
     deep = depth[...]
+    depth_float = deep.astype(jnp.float32)
     at = 5 * levels
-    depth_float = deep.astype(jnp.float32)
-    shallow = shallow_faces(depth_float, item_of(before, 3), lower[at : at + sublanes, :])
-    speed = upper[4 * levels : at, :]
-    edges_y(levels, lower, upper, own_up, (speed, upper[at : at + 1, :], depth_float[rows - 1 :]), edge)
-    pairs_of = lambda value: (item_of(value, 0), item_of(value, 1))
-    packed = edges_x(
-        pairs_of(before),
-        pairs_of(after),
-        pairs_of(own),
-        (item_of(before, 2), item_of(after, 2)),
-        (item_of(before, 3), item_of(after, 3), item_of(own, 3)),
-    )
+    speeds = (rows_of(own_down, 4, levels), beside[...], rows_of(own_up, 4, levels), rows_of(upper, 4, levels))
+    deeps = (lower[at : at + 1, :], upper[at : at + 1, :])
+    borders_y(levels, lower, upper, own_up, own_down, speeds, depth_float, deeps, border)
+    four = lambda value: [item_of(value, i) for i in range(4)]
+    packed = borders_x(four(before), four(after), four(first), four(last))
     current = jnp.zeros((rows, columns), jnp.float32)
     above = current
-    for k in range(0, levels, group_size):
-        part = slice(k, min(k + group_size, levels))
-        c, h = tracer[part], weight[part]
-        forward, back = step_levels(k, levels, c, h, east[part], north[part], shallow, edge, packed)
-        linear[part] = back
-        passed[part] = c + forward - uptake * c * c
     for k in range(levels):
-        current = (jnp.where(k < deep, passed[k], 0.0) + above * current) * inverse[k]
+        right = bordered(k, levels, forward[k], border, 0, packed[0])
+        current = (jnp.where(k < deep, right, 0.0) + above * current) * inverse[k]
         passed[k] = current
         if k < levels - 1:
             above = jnp.where(k + 1 < deep, mixing[k], 0.0)
@@ -439,14 +469,14 @@
         state[k] = current
     current = jnp.zeros((rows, columns), jnp.float32)
     for k in range(levels):
-        right = linear[k] - (2.0 * uptake) * state[k] * weight[k]
+        right = bordered(k, levels, linear[k], border, 4, packed[1]) - (2.0 * uptake) * state[k] * weight[k]
         if k > 0:
             right = right + jnp.where(k < deep, mixing[k - 1], 0.0) * current
         current = right * inverse[k]
         passed[k] = current
     last = [jnp.zeros((rows, lanes), jnp.float32)] * 2
     first = last
-    shallow_y = shallow[1]
+    shallow_y = jnp.minimum(deep, turned(deep, 1, 0))
     for k in range(levels - 1, -1, -1):
         if k < levels - 1:
             current = passed[k] + (jnp.where(k + 1 < deep, mixing[k], 0.0) * inverse[k]) * current
@@ -461,15 +491,17 @@
     choose(even_y, up, down, pay_even)
     choose(even_y, down, up, pay_odd)
     last, first = jnp.concatenate(last, axis=1), jnp.concatenate(first, axis=1)
+    own_first[...] = first
     own_last[...] = last
     pay_core[...] = jnp.where(even_x, last, first)
 
 
 def second_kernel(
-    tracer, east, north, mixing, depth, inverse, state, weight, own_up, own_last, sent_chip, sent_core,
+    mixing, depth, inverse, forward, linear, own_up, own_down, own_first, own_last,
+    first_up, first_down, beside, sent_chip, sent_core,
     got1_even, got1_odd, got1_chip, got1_core, got_even, got_odd, got_core,
     final_far, adjoint_far,
-    final, adjoint, passed, lower, upper, edge, sent,
+    final, adjoint, passed, lower, upper, border, sent,
 ):
     copies = []
 
@@ -478,44 +510,41 @@
         copy.start()
         copies.append(copy)
 
-    levels, rows, columns = tracer.shape
+    levels, rows, columns = forward.shape
     even_y, even_x = parities()
     choose(even_y, got_odd, got_even, lower)
     choose(even_y, got_even, got_odd, upper)
     before1, after1 = take(even_x, got1_core[...], common(got1_chip))
+    last1, first1 = take(even_x, common(sent_chip), sent_core[...])
     strip = strip_states(levels, got1_chip[...], sent_chip[...], lower, upper, even_x)
     before, after = take(even_x, got_core[...], jnp.concatenate(strip, axis=1))
-    own1 = jnp.where(even_x, sent_core[...], common(sent_chip))
     deep = depth[...]
     depth_float = deep.astype(jnp.float32)
     at = 5 * levels
-    lower_deep = jnp.where(even_y, got1_odd[at : at + sublanes, :], got1_even[at : at + sublanes, :])
-    upper_deep = jnp.where(even_y, got1_even[at : at + 1, :], got1_odd[at : at + 1, :])
-    speed = jnp.where(even_y, got1_even[4 * levels : at, :], got1_odd[4 * levels : at, :])
-    shallow = shallow_faces(depth_float, item_of(before1, 3), lower_deep)
-    edges_y(levels, lower, upper, own_up, (speed, upper_deep, depth_float[rows - 1 :]), edge)
-    pairs_of = lambda value: (item_of(value, 0), item_of(value, 1))
-    packed = edges_x(
-        pairs_of(before),
-        pairs_of(after),
-        pairs_of(own_last[...]),
-        (item_of(before1, 2), item_of(after1, 2)),
-        (item_of(before1, 3), item_of(after1, 3), item_of(own1, 3)),
+    deeps = (
+        jnp.where(even_y, got1_odd[at : at + 1, :], got1_even[at : at + 1, :]),
+        jnp.where(even_y, got1_even[at : at + 1, :], got1_odd[at : at + 1, :]),
     )
+    speed = jnp.where(even_y, rows_of(got1_even, 4, levels), rows_of(got1_odd, 4, levels))
+    speeds = (rows_of(first_down, 4, levels), beside[...], rows_of(first_up, 4, levels), speed)
+    borders_y(levels, lower, upper, own_up, own_down, speeds, depth_float, deeps, border)
+
+    def four(value, fixed):
+        return [item_of(value, 0), item_of(value, 1), item_of(fixed, 2), item_of(fixed, 3)]
+
+    sides = ((before, before1), (after, after1), (own_first, first1), (own_last, last1))
+    packed = borders_x(*(four(*side) for side in sides))
     current = jnp.zeros((rows, columns), jnp.float32)
     above = current
-    for k in range(0, levels, group_size):
-        part = slice(k, min(k + group_size, levels))
-        c, h = state[part], weight[part]
-        forward, back = step_levels(k, levels, c, h, east[part], north[part], shallow, edge, packed)
-        adjoint[part] = back - (2.0 * uptake) * tracer[part] * h
-        send(adjoint, adjoint_far, part)
-        passed[part] = c + forward - uptake * c * c
     for k in range(levels):
-        current = (jnp.where(k < deep, passed[k], 0.0) + above * current) * inverse[k]
+        adjoint[k] = bordered(k, levels, linear[k], border, 4, packed[1])
+        right = bordered(k, levels, forward[k], border, 0, packed[0])
+        current = (jnp.where(k < deep, right, 0.0) + above * current) * inverse[k]
         passed[k] = current
         if k < levels - 1:
             above = jnp.where(k + 1 < deep, mixing[k], 0.0)
+        if (k + 1) % group_size == 0 or k == levels - 1:
+            send(adjoint, adjoint_far, slice(k // group_size * group_size, k + 1))
     final[levels - 1] = current
     for k in range(levels - 2, -1, -1):
         current = passed[k] + (jnp.where(k + 1 < deep, mixing[k], 0.0) * inverse[k]) * current
@@ -548,7 +577,7 @@
     field = jax.ShapeDtypeStruct((levels, rows, columns), f32)
     first_size = 5 * levels + sublanes
     second_size = 4 * levels + sublanes
-    edge_size = 9 * levels
+    border_size = 8 * levels
     block = pltpu.VMEM((levels, rows, columns), f32)
     params = pltpu.CompilerParams(vmem_limit_bytes=32 * 1024 * 1024)
     far = pl.BlockSpec(memory_space=pl.ANY)
@@ -569,31 +598,39 @@
         factor_kernel,
         in_specs=[far] * 6,
         out_shape=near
-        + (field, field, lines(first_size), lines(first_size), tiles(5), tiles(4), lines(first_size)),
-        scratch_shapes=[block, block, space(first_size), pltpu.SemaphoreType.DMA((6,))],
+        + (field, field, lines(first_size), lines(first_size), tiles(5), tiles(4), lines(first_size), lines(first_size), lines(levels)),
+        scratch_shapes=[block, block, pltpu.SemaphoreType.DMA((6,))],
         compiler_params=params,
     )(*distant)
-    given = outcome[:5]
-    inverse, weight, *messages, up = outcome[5:]
+    tracer, east_speed, north_speed, mixing, depth_levels, inverse, weight, *messages, up, down, beside = outcome
+    cells = levels * rows * columns
+    inner = pl.CostEstimate(flops=80 * cells, bytes_accessed=24 * cells, transcendentals=0)
+
+    def inside(c, h, *more):
+        return pl.pallas_call(inner_kernel, out_shape=(field, field), compiler_params=params, cost_estimate=inner)(
+            c, h, east_speed, north_speed, depth_levels, *more
+        )
+
     got1 = exchange(*messages)
     sent1 = messages[2:]
-    state, weight_next, *messages, up2, last2 = pl.pallas_call(
+    parts = inside(tracer, weight)
+    state, weight_next, *messages, up2, down2, first2, last2 = pl.pallas_call(
         first_kernel,
-        out_shape=(field, field, lines(second_size), lines(second_size), tiles(2), lines(second_size), tiles(2)),
-        scratch_shapes=[
-            block, block, space(first_size), space(first_size), space(edge_size), space(second_size),
-        ],
+        out_shape=(field, field, lines(second_size), lines(second_size), tiles(2))
+        + (lines(second_size), lines(second_size), tiles(2), tiles(2)),
+        scratch_shapes=[block, space(first_size), space(first_size), space(border_size)],
         compiler_params=params,
-    )(*given, inverse, weight, up, *sent1, *got1)
+    )(north_speed, mixing, depth_levels, inverse, weight, *parts, up, down, beside, *sent1, *got1)
     got2 = exchange(*messages)
+    parts = inside(state, weight_next, tracer)
     sends = pltpu.SemaphoreType.DMA((2 * -(-levels // group_size),))
     final, adjoint = pl.pallas_call(
         second_kernel,
         out_specs=[far] * 2,
         out_shape=(field, field),
-        scratch_shapes=[block, block, block, space(second_size), space(second_size), space(edge_size), sends],
+        scratch_shapes=[block, block, block, space(second_size), space(second_size), space(border_size), sends],
         compiler_params=params,
-    )(*given, inverse, state, weight_next, up2, last2, *sent1, *got1, *got2)
+    )(mixing, depth_levels, inverse, *parts, up2, down2, first2, last2, up, down, beside, *sent1, *got1, *got2)
     return final, adjoint
 
 

time: 24.5 us -> 23.3 us (0.951)
  waiting for transfers between devices: 6.32 us -> 4.28 us
  Pallas kernels: 6.1 us -> 6.91 us
    ppermute x3, waiting for transfers between devices: 2.82 us -> 0.77 us  [exchange(): lax.ppermute(each, 'tile', pairs('tile', len(pay) - 1 - i))]
    pallas_call x0 -> x2, Pallas kernels: none -> 2.02 us  [inside(): pl.pallas_call(inner_kernel, out_shape=(field, field), compiler_params=pa...]
    pallas_call x1, Pallas kernels: 1.61 us -> 0.99 us  [shards(): pl.pallas_call(first_kernel, out_shape=(field, field, lines(second_size),...]
    pallas_call x1, Pallas kernels: 2.6 us -> 2 us  [shards(): pl.pallas_call(second_kernel, out_specs=[far] * 2, out_shape=(field, fiel...]
  transfers between devices with their start and end apart: 7 -> 7, of which waited for: 5 -> 4; matrix products, arithmetic and copies ran while one was open for 0% -> 0% of each run, Pallas kernels for 0% -> 9%
where the time goes in v5:
time: 23.3 us; the launch traced here: 23 us
  starting transfers between devices  11.1 us (48%)
  Pallas kernels  6.91 us (30%)
  waiting for transfers between devices  4.28 us (18%)
  between operations  0.71 us (3%)
    ppermute x2, starting transfers between devices, exchange(): got_odd = lax.ppermute(pay_odd, 'group', pairs('group', 1))  6.73 us
    ppermute x3, starting transfers between devices, exchange(): lax.ppermute(each, 'tile', pairs('tile', len(pay) - 1 - i))  3.74 us
    ppermute x2, waiting for transfers between devices, exchange(): got_odd = lax.ppermute(pay_odd, 'group', pairs('group', 1))  2.81 us
    pallas_call x2, Pallas kernels, inside(): pl.pallas_call(inner_kernel, out_shape=(field, field), compiler_params=pa...  2.02 us
    pallas_call x1, Pallas kernels, shards(): pl.pallas_call(second_kernel, out_specs=[far] * 2, out_shape=(field, fiel...  2 us
    pallas_call x1, Pallas kernels, shards(): pl.pallas_call(factor_kernel, in_specs=[far] * 6, out_shape=near + (field...  1.9 us
    pallas_call x1, Pallas kernels, shards(): pl.pallas_call(first_kernel, out_shape=(field, field, lines(second_size),...  0.99 us
    ppermute x3, waiting for transfers between devices, exchange(): lax.ppermute(each, 'tile', pairs('tile', len(pay) - 1 - i))  0.77 us
  transfers between devices with their start and end apart: 7, of which 4 were waited for; matrix products, arithmetic and copies ran while one was open for 0% of the time, Pallas kernels for 9%

profile of v5, /device:TPU:10, one launch (start us, length us, event | category | flops | bytes accessed | tf_op | source)
XLA Modules:
  0.0 23.0 jit_solution(4417667383201452295)
XLA Ops:
  0.6 1.9 %shard_map.77 = (f32[16,16,256]{2,1,0:T(8,128)S(1)}, f32[16,16,256]{2,1,0:T(8,128)S(1)}, f32[16,16,256]{2,1,0:T(8,128)S(1)}, f32[15,16,256]{2,1,0:T(8,128)S(1)},...) custom-call(f32[16,16,256]{2,1,0:T(8,128)} %tracer_far.1, ...), custom_call_target="tpu_custom_call" | custom-call | tf_op jit(solution)/shard_map/pallas_call | solution.py:597
  2.5 0.6 %collective-permute-start = (f32[88,256]{1,0:T(8,128)S(1)}, f32[88,256]{1,0:T(8,128)S(1)}, u32[]{:S(2)}, u32[]{:S(2)}) collective-permute-start(f32[88,256]{1,0:T(8,128)S(1)} %get-tuple-element.43), channel_id=1, source_target_pairs={{0,8},{8,0},{16,24},{24,16},{1,9},{9,1},{17,25},{25,17},{2,10},{10... | collective-permute-start | bytes 270344 | tf_op jit(solution)/shard_map/ppermute | solution.py:567
  3.1 4.3 %collective-permute-start.1 = (f32[88,256]{1,0:T(8,128)S(1)}, f32[88,256]{1,0:T(8,128)S(1)}, u32[]{:S(2)}, u32[]{:S(2)}) collective-permute-start(f32[88,256]{1,0:T(8,128)S(1)} %get-tuple-element.44), channel_id=1, source_target_pairs={{8,16},{16,8},{9,17},{17,9},{10,18},{18,10},{11,19},{19,11},{12,20... | collective-permute-start | bytes 270344 | tf_op jit(solution)/shard_map/ppermute | solution.py:568
  7.5 1.9 %collective-permute-start.2 = (f32[16,640]{1,0:T(8,128)S(1)}, f32[16,640]{1,0:T(8,128)S(1)}, u32[]{:S(2)}, u32[]{:S(2)}) collective-permute-start(f32[16,640]{1,0:T(8,128)S(1)} %get-tuple-element.41.sent_chip), channel_id=1, source_target_pairs={{1,2},{2,1},{3,4},{4,3},{5,6},{6,5},{9,10},{10,9},{11,12},{12,11},... | collective-permute-start | bytes 122888 | tf_op jit(solution)/shard_map/ppermute | solution.py:569
  9.4 1.7 %collective-permute-start.3 = (f32[16,512]{1,0:T(8,128)S(1)}, f32[16,512]{1,0:T(8,128)S(1)}, u32[]{:S(2)}, u32[]{:S(2)}) collective-permute-start(f32[16,512]{1,0:T(8,128)S(1)} %get-tuple-element.42.sent_core), channel_id=1, source_target_pairs={{0,1},{1,0},{2,3},{3,2},{4,5},{5,4},{6,7},{7,6},{8,9},{9,8},{10,11... | collective-permute-start | bytes 98312 | tf_op jit(solution)/shard_map/ppermute | solution.py:569
  11.2 1.0 %shard_map.78 = (f32[16,16,256]{2,1,0:T(8,128)S(1)}, f32[16,16,256]{2,1,0:T(8,128)S(1)}) custom-call(f32[16,16,256]{2,1,0:T(8,128)S(1)} %get-tuple-element.34.c_ref.rest_0_, f32[16,16,256]{2,1,0:T(8,128)S(1)} %get-tuple-element.33.h_ref.weight, f32[16,16,256]{2,1,0:T(8,128)S(1)} %get-tuple-element.35.east, f32[16,16,256]{2,1,0:T(8,128)S(1)} %get-tuple-element.32.north, ...), custom_call_target="tpu_custom_call" | custom-call | flops 5242880 | bytes 1572864 | tf_op jit(solution)/shard_map/pallas_call | solution.py:610
  12.2 0.0 collective-permute-done.3.got_core.got1_core
  12.2 0.6 %collective-permute-done.2.got_chip.got1_chip = f32[16,640]{1,0:T(8,128)S(1)} collective-permute-done((f32[16,640]{1,0:T(8,128)S(1)}, f32[16,640]{1,0:T(8,128)S(1)}, u32[]{:S(2)}, u32[]{:S(2)}) %collective-permute-start.2) | collective-permute-done | bytes 40992 | tf_op jit(solution)/shard_map/ppermute | solution.py:569
  12.8 0.0 collective-permute-done.got_even.got1_even
  12.8 0.0 collective-permute-done.1.got_odd.got1_odd
  12.8 1.0 %shard_map.79 = (f32[16,16,256]{2,1,0:T(8,128)S(1)}, f32[16,16,256]{2,1,0:T(8,128)S(1)}, f32[72,256]{1,0:T(8,128)S(1)}, f32[72,256]{1,0:T(8,128)S(1)}, f32[16,25...) custom-call(f32[16,16,256]{2,1,0:T(8,128)S(1)} %get-tuple-element.32, ...), custom_call_target="tpu_custom_call" | custom-call | tf_op jit(solution)/shard_map/pallas_call | solution.py:617
  13.8 0.1 collective-permute-start.4
  13.9 2.4 %collective-permute-start.5 = (f32[72,256]{1,0:T(8,128)S(1)}, f32[72,256]{1,0:T(8,128)S(1)}, u32[]{:S(2)}, u32[]{:S(2)}) collective-permute-start(f32[72,256]{1,0:T(8,128)S(1)} %get-tuple-element.54), channel_id=1, source_target_pairs={{8,16},{16,8},{9,17},{17,9},{10,18},{18,10},{11,19},{19,11},{12,20... | collective-permute-start | bytes 221192 | tf_op jit(solution)/shard_map/ppermute | solution.py:568
  16.3 0.1 collective-permute-start.6
  16.4 1.0 %shard_map.80 = (f32[16,16,256]{2,1,0:T(8,128)S(1)}, f32[16,16,256]{2,1,0:T(8,128)S(1)}) custom-call(f32[16,16,256]{2,1,0:T(8,128)S(1)} %get-tuple-element.45.c_ref, f32[16,16,256]{2,1,0:T(8,128)S(1)} %get-tuple-element.46.h_ref, f32[16,16,256]{2,1,0:T(8,128)S(1)} %get-tuple-element.35.east, f32[16,16,256]{2,1,0:T(8,128)S(1)} %get-tuple-element.32.north, ...), custom_call_target="tpu_custom_call" | custom-call | flops 5242880 | bytes 1572864 | tf_op jit(solution)/shard_map/pallas_call | solution.py:610
  17.4 0.1 collective-permute-done.6.got_core
  17.5 0.7 %collective-permute-done.4.got_even = f32[72,256]{1,0:T(8,128)S(1)} collective-permute-done((f32[72,256]{1,0:T(8,128)S(1)}, f32[72,256]{1,0:T(8,128)S(1)}, u32[]{:S(2)}, u32[]{:S(2)}) %collective-permute-start.4) | collective-permute-done | bytes 73760 | tf_op jit(solution)/shard_map/ppermute | solution.py:567
  18.2 2.8 %collective-permute-done.5.got_odd = f32[72,256]{1,0:T(8,128)S(1)} collective-permute-done((f32[72,256]{1,0:T(8,128)S(1)}, f32[72,256]{1,0:T(8,128)S(1)}, u32[]{:S(2)}, u32[]{:S(2)}) %collective-permute-start.5) | collective-permute-done | bytes 73760 | tf_op jit(solution)/shard_map/ppermute | solution.py:568
  21.0 2.0 %shard_map.81 = (f32[16,16,256]{2,1,0:T(8,128)}, f32[16,16,256]{2,1,0:T(8,128)}) custom-call(f32[15,16,256]{2,1,0:T(8,128)S(1)} %get-tuple-element.29.mixing, s32[16,256]{1,0:T(8,128)S(1)} %get-tuple-element.30.depth, f32[16,16,256]{2,1,0:T(8,128)S(1)} %get-tuple-element.31.inverse, f32[16,16,256]{2,1,0:T(8,128)S(1)} %get-tuple-element.47.forward, ...), custom_call_target="tpu_custom_call" | custom-call | tf_op jit(solution)/shard_map/pallas_call | solution.py:627
Async XLA Ops:
  2.5 10.3 %collective-permute-start = (f32[88,256]{1,0:T(8,128)S(1)}, f32[88,256]{1,0:T(8,128)S(1)}, u32[]{:S(2)}, u32[]{:S(2)}) collective-permute-start(f32[88,256]{1,0:T(8,128)S(1)} %get-tuple-element.43), channel_id=1, source_target_pairs={{0,8},{8,0},{16,24},{24,16},{1,9},{9,1},{17,25},{25,17},{2,10},{10... | collective-permute-start | bytes 270344 | tf_op jit(solution)/shard_map/ppermute | solution.py:567
  3.1 9.7 %collective-permute-start.1 = (f32[88,256]{1,0:T(8,128)S(1)}, f32[88,256]{1,0:T(8,128)S(1)}, u32[]{:S(2)}, u32[]{:S(2)}) collective-permute-start(f32[88,256]{1,0:T(8,128)S(1)} %get-tuple-element.44), channel_id=1, source_target_pairs={{8,16},{16,8},{9,17},{17,9},{10,18},{18,10},{11,19},{19,11},{12,20... | collective-permute-start | bytes 270344 | tf_op jit(solution)/shard_map/ppermute | solution.py:568
  7.5 5.3 %collective-permute-start.2 = (f32[16,640]{1,0:T(8,128)S(1)}, f32[16,640]{1,0:T(8,128)S(1)}, u32[]{:S(2)}, u32[]{:S(2)}) collective-permute-start(f32[16,640]{1,0:T(8,128)S(1)} %get-tuple-element.41.sent_chip), channel_id=1, source_target_pairs={{1,2},{2,1},{3,4},{4,3},{5,6},{6,5},{9,10},{10,9},{11,12},{12,11},... | collective-permute-start | bytes 122888 | tf_op jit(solution)/shard_map/ppermute | solution.py:569
  9.4 2.8 %collective-permute-start.3 = (f32[16,512]{1,0:T(8,128)S(1)}, f32[16,512]{1,0:T(8,128)S(1)}, u32[]{:S(2)}, u32[]{:S(2)}) collective-permute-start(f32[16,512]{1,0:T(8,128)S(1)} %get-tuple-element.42.sent_core), channel_id=1, source_target_pairs={{0,1},{1,0},{2,3},{3,2},{4,5},{5,4},{6,7},{7,6},{8,9},{9,8},{10,11... | collective-permute-start | bytes 98312 | tf_op jit(solution)/shard_map/ppermute | solution.py:569
  13.8 4.4 %collective-permute-start.4 = (f32[72,256]{1,0:T(8,128)S(1)}, f32[72,256]{1,0:T(8,128)S(1)}, u32[]{:S(2)}, u32[]{:S(2)}) collective-permute-start(f32[72,256]{1,0:T(8,128)S(1)} %get-tuple-element.53), channel_id=1, source_target_pairs={{0,8},{8,0},{16,24},{24,16},{1,9},{9,1},{17,25},{25,17},{2,10},{10... | collective-permute-start | bytes 221192 | tf_op jit(solution)/shard_map/ppermute | solution.py:567
  13.9 7.1 %collective-permute-start.5 = (f32[72,256]{1,0:T(8,128)S(1)}, f32[72,256]{1,0:T(8,128)S(1)}, u32[]{:S(2)}, u32[]{:S(2)}) collective-permute-start(f32[72,256]{1,0:T(8,128)S(1)} %get-tuple-element.54), channel_id=1, source_target_pairs={{8,16},{16,8},{9,17},{17,9},{10,18},{18,10},{11,19},{19,11},{12,20... | collective-permute-start | bytes 221192 | tf_op jit(solution)/shard_map/ppermute | solution.py:568
  16.3 1.2 %collective-permute-start.6 = (f32[16,256]{1,0:T(8,128)S(1)}, f32[16,256]{1,0:T(8,128)S(1)}, u32[]{:S(2)}, u32[]{:S(2)}) collective-permute-start(f32[16,256]{1,0:T(8,128)S(1)} %get-tuple-element.55), channel_id=1, source_target_pairs={{0,1},{1,0},{2,3},{3,2},{4,5},{5,4},{6,7},{7,6},{8,9},{9,8},{10,11... | collective-permute-start | bytes 49160 | tf_op jit(solution)/shard_map/ppermute | solution.py:569

commit v6 on v5

v6 whole, which is shorter than its diff:
```python
import jax
import jax.numpy as jnp
from jax import lax
from jax.experimental import pallas as pl
from jax.experimental.pallas import tpu as pltpu
from jax.sharding import PartitionSpec as P

diffusivity = 0.1
uptake = 0.2
lanes = 128
sublanes = 8
group_size = 8

slot = 8


def turned(value, shift, axis):
    return pltpu.roll(value, shift % value.shape[axis], axis)


def index(shape, axis):
    return lax.broadcasted_iota(jnp.int32, shape, axis)


def parities():
    return lax.rem(lax.axis_index("group"), 2) == 0, lax.rem(lax.axis_index("tile"), 2) == 0


def split(value, axis):
    step = lanes if axis == 2 else sublanes
    return [lax.slice_in_dim(value, i, i + step, axis=axis) for i in range(0, value.shape[axis], step)]


def shifted(tiles, shift, axis, edge):
    span = tiles[0].shape[axis]
    moved = [turned(tile, shift, axis) for tile in tiles]
    place = index(tiles[0].shape, axis)
    if shift > 0:
        return [jnp.where(place < shift, a, b) for a, b in zip([edge] + moved[:-1], moved)]
    return [jnp.where(place >= span + shift, a, b) for a, b in zip(moved[1:] + [edge], moved)]


def face_flux(c, behind, ahead, far, speed, is_open):
    flux = speed * (7.0 * (c + behind) - (ahead + far)) - diffusivity * (c - behind)
    return jnp.where(is_open, flux, 0.0)


def explicit_flux(tiles, speeds, opens, axis, edges):
    edge_behind, edge_far, edge_ahead, edge_flux = edges
    behind = shifted(tiles, 1, axis, edge_behind)
    ahead = shifted(tiles, -1, axis, edge_ahead)
    far = shifted(tiles, 2, axis, edge_far)
    flux = [face_flux(*each) for each in zip(tiles, behind, ahead, far, speeds, opens)]
    following = shifted(flux, -1, axis, edge_flux)
    return jnp.concatenate([g - n for g, n in zip(flux, following)], axis=axis)


def reverse_flux(tiles, speeds, opens, axis, edges):
    edge_behind, edge_sum, edge_carried, edge_far = edges
    behind = shifted(tiles, 1, axis, edge_behind)
    jump = [jnp.where(o, h - b, 0.0) for h, b, o in zip(tiles, behind, opens)]
    carried = [s * j for s, j in zip(speeds, jump)]
    seven = [7.0 * g for g in carried]
    spread = [diffusivity * j for j in jump]
    ahead = shifted([a + b for a, b in zip(seven, spread)], -1, axis, edge_sum)
    back = shifted(carried, 1, axis, edge_carried)
    far = shifted(carried, -2, axis, edge_far)
    parts = zip(seven, spread, ahead, back, far)
    return jnp.concatenate([(a - b) + c - d - e for a, b, c, d, e in parts], axis=axis)


def level_of(lane):
    return lax.div(lax.rem(lane + slot // 2, lanes), slot)


def pack_columns(k, item, packed):
    lane = index(packed.shape, 1)
    tile = jnp.where(lane < lanes // 2, item[:, :lanes], item[:, -lanes:])
    return jnp.where(level_of(lane) == k, turned(tile, slot * k, 1), packed)


def repeated(value):
    lane = index((value.shape[0], lanes), 1)
    value = jnp.where(lane < lanes // 2, value[:, :lanes], value[:, -lanes:])
    value = jnp.where(level_of(lane) == 0, value, 0.0)
    width = slot
    while width < lanes:
        value = value + turned(value, width, 1)
        width *= 2
    return value


def pack_rows(k, levels, c, h, speed, open_y, up, down):
    size = c.shape[0]
    last = slice(size - sublanes, size)
    first = slice(0, sublanes)
    g_last = jnp.where(open_y[last], speed[last] * (h[last] - turned(h[last], 1, 0)), 0.0)
    g_first = jnp.where(open_y[first], speed[first] * (h[first] - turned(h[first], 1, 0)), 0.0)
    above = (c[size - 2 : size - 1], c[size - 1 :], h[size - 1 :], g_last[sublanes - 1 :])
    below = (c[0:1], c[1:2], h[0:1], g_first[1:2])
    for item in range(4):
        at = item * levels + k
        up[at : at + 1, :] = above[item]
        down[at : at + 1, :] = below[item]


def inward(levels, scaled, links, inverse, joint, passed):
    middle = levels // 2
    top = bottom = None
    for i in range(levels - middle):
        k = levels - 1 - i
        bottom = scaled(k) if i == 0 else scaled(k) + (links[k] * inverse[k]) * bottom
        passed[k] = bottom
        if i < middle:
            top = scaled(i) if i == 0 else scaled(i) + (links[i - 1] * inverse[i]) * top
            passed[i] = top
    link = links[middle - 1]
    top = (top + (link * inverse[middle - 1]) * bottom) * joint
    return top, bottom + (link * inverse[middle]) * top


def outward(levels, ends, links, inverse, passed):
    middle = levels // 2
    top, bottom = ends
    yield middle - 1, top
    yield middle, bottom
    for i in range(1, levels - middle):
        k = middle + i
        bottom = passed[k] + (links[k - 1] * inverse[k]) * bottom
        yield k, bottom
        k = middle - 1 - i
        if k >= 0:
            top = passed[k] + (links[k] * inverse[k]) * top
            yield k, top


def factorized(levels, links, inverse):
    middle = levels // 2

    def pivots(order, near, far):
        share = None
        for k in order:
            pivot = 1.0
            if 0 <= far(k) < levels - 1:
                pivot = pivot + links[far(k)]
            if share is not None:
                pivot = pivot + (links[near(k)] - links[near(k)] * share)
            inverse[k] = 1.0 / pivot
            if 0 <= far(k) < levels - 1:
                share = links[far(k)] * inverse[k]
            yield

    down = pivots(range(middle), lambda k: k - 1, lambda k: k)
    up = pivots(range(levels - 1, middle - 1, -1), lambda k: k, lambda k: k - 1)
    for _ in range(levels - middle):
        next(up)
        next(down, None)
    link = links[middle - 1]
    return 1.0 / (1.0 - (link * inverse[middle - 1]) * (link * inverse[middle]))


def choose(flag, ref_true, ref_false, into):
    into[...] = jnp.where(flag, ref_true[...], ref_false[...])


def factor_kernel(
    tracer_far, east_far, north_far, mixing_far, depth_far, sensitivity_far,
    tracer, east, north, depth, links, inverse, joint, weight, pay_even, pay_odd, outer, pay_core, up, down, beside,
    mixing, sensitivity, passed, arrived,
):
    order = (
        (depth_far, depth),
        (mixing_far, mixing),
        (sensitivity_far, sensitivity),
        (tracer_far, tracer),
        (east_far, east),
        (north_far, north),
    )
    copies = [pltpu.make_async_copy(far, near, arrived.at[i]) for i, (far, near) in enumerate(order)]
    for copy in copies:
        copy.start()
    levels, rows, columns = tracer.shape
    even_y, _ = parities()
    copies[0].wait()
    deep = depth[...]
    depth_float = deep.astype(jnp.float32)
    outer[:, 3 * lanes : 4 * lanes] = repeated(depth_float)
    for copy in copies[1:3]:
        copy.wait()
    shallow_y = jnp.minimum(deep, turned(deep, 1, 0))
    for k in range(levels - 1):
        links[k] = jnp.where(k + 1 < deep, mixing[k], 0.0)
    joint[...] = factorized(levels, links, inverse)
    ends = inward(levels, lambda k: sensitivity[k] * inverse[k], links, inverse, joint[...], passed)
    for copy in copies[3:]:
        copy.wait()
    packed = [jnp.zeros((rows, lanes), jnp.float32)] * 5
    for k, current in outward(levels, ends, links, inverse, passed):
        h = jnp.where(k < deep, current, 0.0)
        weight[k] = h
        c = tracer[k]
        speed_x = east[k] * (1.0 / 12.0)
        speed_y = north[k] * (1.0 / 12.0)
        items = (c, h, speed_x, speed_y) + ((mixing[k],) if k < levels - 1 else ())
        packed[: len(items)] = [pack_columns(k, *each) for each in zip(items, packed)]
        pack_rows(k, levels, c, h, speed_y, k < shallow_y, up, down)
        at = 4 * levels + k
        down[at : at + 1, :] = speed_y[0:1]
        up[at : at + 1, :] = speed_y[rows - 1 :]
        beside[k : k + 1, :] = speed_y[1:2]
    for place, value in zip((0, 1, 2, 4, 5), packed):
        outer[:, place * lanes : (place + 1) * lanes] = value
    pay_core[...] = common(outer)
    at = 5 * levels
    up[at : at + sublanes, :] = jnp.broadcast_to(depth_float[rows - 1 :], (sublanes, columns))
    down[at : at + sublanes, :] = jnp.broadcast_to(depth_float[0:1], (sublanes, columns))
    choose(even_y, up, down, pay_even)
    choose(even_y, down, up, pay_odd)


def rows_of(ref, item, levels):
    return ref[item * levels : (item + 1) * levels, :]


def border_rows(level, lower, upper, up, down, speeds, deeps):
    c_far, c_near, h_near, g_near = lower
    c_next, c_over, h_next, g_over = upper
    c_two, c_one, h_one = up
    c_zero, c_first, h_zero = down
    speed_start, speed_first, speed_last, speed_end = speeds
    before, zero, one, two_last, last, after = deeps
    start_open = level < jnp.minimum(before, zero)
    first_open = level < jnp.minimum(zero, one)
    last_open = level < jnp.minimum(two_last, last)
    end_open = level < jnp.minimum(last, after)
    start = face_flux(c_zero, c_near, c_first, c_far, speed_start, start_open)
    first = jnp.where(first_open, -speed_first * c_near, 0.0)
    final = jnp.where(last_open, -speed_last * c_next, 0.0)
    finish = face_flux(c_next, c_one, c_over, c_two, speed_end, end_open)
    start_jump = jnp.where(start_open, h_zero - h_near, 0.0)
    end_jump = jnp.where(end_open, h_next - h_one, 0.0)
    start_carried = speed_start * start_jump
    end_carried = speed_end * end_jump
    return (
        start - first,
        first,
        -final,
        final - finish,
        7.0 * start_carried - diffusivity * start_jump - g_near,
        -start_carried,
        -end_carried,
        7.0 * end_carried + diffusivity * end_jump - g_over,
    )


def borders_y(levels, lower, upper, up, down, speeds, deep, deeps, border):
    end = deep.shape[0] - 1
    deeps = (deeps[0], deep[0:1], deep[1:2], deep[end - 1 : end], deep[end:], deeps[1])
    several = lambda ref, count: [rows_of(ref, i, levels) for i in range(count)]
    level = index((levels, deep.shape[1]), 0).astype(jnp.float32)
    values = border_rows(level, several(lower, 4), several(upper, 4), several(up, 3), several(down, 3), speeds, deeps)
    for item, value in enumerate(values):
        border[item * levels : (item + 1) * levels, :] = value


def placed(shape):
    lane = index(shape, 1)
    return lax.rem(lane, slot), level_of(lane).astype(jnp.float32)


def borders_x(before, after, own):
    place, level = placed(own[0].shape)
    start = place < slot // 2
    at = lambda value, distance: turned(value, -distance, 1)
    c, h, speed, deep = (jnp.where(start, mine, other) for mine, other in zip(own, before))
    deep_back = at(deep, -1)
    is_open = level < jnp.minimum(deep, deep_back)
    next_open = level < jnp.minimum(deep, at(deep, 1))
    back_open = level < jnp.minimum(deep_back, at(deep, -2))
    behind, far = at(c, -1), at(c, -2)
    flux = face_flux(c, behind, at(c, 1), far, speed, is_open) + jnp.where(next_open, at(speed, 1) * behind, 0.0)
    forward = jnp.where(place == 0, flux, jnp.where(is_open, -speed * far, 0.0))
    h_back = at(h, -1)
    jump = jnp.where(is_open, h - h_back, 0.0)
    back = jnp.where(back_open, at(speed, -1) * (h_back - at(h, -2)), 0.0)
    backward = jnp.where(place == 0, 7.0 * (speed * jump) - diffusivity * jump, 0.0) - back
    c, h, speed, deep = (jnp.where(start, other, mine) for mine, other in zip(own, after))
    deep_next = at(deep, 1)
    is_open = level < jnp.minimum(deep, at(deep, -1))
    next_open = level < jnp.minimum(deep, deep_next)
    over_open = level < jnp.minimum(deep_next, at(deep, 2))
    c_next, c_over, speed_next = at(c, 1), at(c, 2), at(speed, 1)
    flux = face_flux(c_next, c, c_over, at(c, -1), speed_next, next_open) + jnp.where(is_open, speed * c_next, 0.0)
    forward_end = jnp.where(place == slot - 1, -flux, jnp.where(next_open, speed_next * c_over, 0.0))
    h_next = at(h, 1)
    jump = jnp.where(next_open, h_next - h, 0.0)
    over = jnp.where(over_open, at(speed, 2) * (at(h, 2) - h_next), 0.0)
    total = 7.0 * (speed_next * jump) + diffusivity * jump
    backward_end = jnp.where(place == slot - 1, total, 0.0) - over
    return jnp.where(start, forward, forward_end), jnp.where(start, backward, backward_end)


def with_rows(k, levels, value, border, item):
    rows, columns = value.shape
    row = index((sublanes, columns), 0)

    def line(which):
        at = (item + which) * levels + k
        return jnp.broadcast_to(border[at : at + 1, :], (sublanes, columns))

    tiles = split(value, 0)
    tiles[0] = tiles[0] + jnp.where(row == 0, line(0), jnp.where(row == 1, line(1), 0.0))
    added = jnp.where(row == sublanes - 2, line(2), jnp.where(row == sublanes - 1, line(3), 0.0))
    tiles[-1] = tiles[-1] + added
    return jnp.concatenate(tiles, axis=0)


def with_columns(k, value, packed):
    lead = turned(packed, -slot * k, 1)
    lane = index(lead.shape, 1)
    tiles = [value[:, i : i + lanes] for i in range(0, value.shape[1], lanes)]
    tiles[0] = tiles[0] + jnp.where(lane < 2, lead, 0.0)
    tiles[-1] = tiles[-1] + jnp.where(lane >= lanes - 2, lead, 0.0)
    return jnp.concatenate(tiles, axis=1)


def step_levels(first, c, h, east_part, north_part, shallow):
    count, rows, columns = c.shape
    shallow_x, shallow_y = shallow
    level = index((count, rows, columns), 0) + first
    none = (0.0, 0.0, 0.0, 0.0)
    speeds = split(east_part * (1.0 / 12.0), 2)
    opens = split(level < shallow_x[None], 2)
    forward = explicit_flux(split(c, 2), speeds, opens, 2, none)
    backward = reverse_flux(split(h, 2), speeds, opens, 2, none)
    speeds = split(north_part * (1.0 / 12.0), 1)
    opens = split(level < shallow_y[None], 1)
    forward = forward + explicit_flux(split(c, 1), speeds, opens, 1, none)
    backward = backward + reverse_flux(split(h, 1), speeds, opens, 1, none)
    return forward, h + backward


def inner_kernel(c_ref, h_ref, east, north, depth, *rest):
    *tracer, forward, linear = rest
    levels, rows, columns = c_ref.shape
    deep = depth[...]
    lane, row = index(deep.shape, 1), index(deep.shape, 0)
    shallow_x = jnp.where(lane == 0, 0, jnp.minimum(deep, turned(deep, 1, 1)))
    shallow_y = jnp.where(row == 0, 0, jnp.minimum(deep, turned(deep, 1, 0)))
    for k in range(0, levels, group_size):
        part = slice(k, min(k + group_size, levels))
        c, h = c_ref[part], h_ref[part]
        ahead, back = step_levels(k, c, h, east[part], north[part], (shallow_x, shallow_y))
        if tracer:
            back = back - (2.0 * uptake) * tracer[0][part] * h
        linear[part] = back
        forward[part] = c + ahead - uptake * c * c


def item_of(value, item):
    return value[:, item * lanes : (item + 1) * lanes]


def take(flag, core, chip):
    return jnp.where(flag, chip, core), jnp.where(flag, core, chip)


def common(ref):
    return ref[:, : 4 * lanes]


def strip_rows(levels, message, up, down):
    c, h, deep, side = (item_of(message, i) for i in (0, 1, 3, 4))
    size = c.shape[0]
    _, level = placed(c.shape)
    is_open = level < jnp.minimum(deep, turned(deep, 1, 0))
    carried = jnp.where(is_open, side * (h - turned(h, 1, 0)), 0.0)
    at = 4 * levels
    for ref in (up, down):
        ref[at : at + sublanes, :] = jnp.zeros((sublanes, ref.shape[1]), jnp.float32)
    end = size - 1
    above = (c[end - 1 : end], c[end:], h[end:], carried[end:], deep[end:])
    below = (c[0:1], c[1:2], h[0:1], carried[1:2], deep[0:1], side[0:1])
    for ref, lines in ((up, above), (down, below)):
        for i, line in enumerate(lines):
            ref[at + i : at + i + 1, :lanes] = line


def second_inner_kernel(
    c_ref, h_ref, east, north, depth, tracer, outer, got_chip,
    forward, linear, base, strip_links, strip_inverse, strip_joint, strip_weight,
):
    inner_kernel(c_ref, h_ref, east, north, depth, tracer, forward, linear)
    levels = c_ref.shape[0]
    _, even = parities()
    place, level = placed((outer.shape[0], lanes))
    ours = (place < slot // 2) == even
    c, h, speed, deep = (jnp.where(ours, item_of(outer, i), item_of(got_chip, i)) for i in range(4))
    side, mixed = item_of(got_chip, 4), item_of(got_chip, 5)
    is_open = level < jnp.minimum(deep, turned(deep, 1, 1))
    flux = face_flux(c, turned(c, 1, 1), turned(c, -1, 1), turned(c, 2, 1), speed, is_open)
    jump = jnp.where(is_open, h - turned(h, 1, 1), 0.0)
    carried = speed * jump
    plus = 7.0 * carried + diffusivity * jump
    minus = 7.0 * carried - diffusivity * jump
    step = c + (flux - turned(flux, -1, 1)) - uptake * c * c
    reverse = h + minus + turned(plus, -1, 1) - turned(carried, 1, 1) - turned(carried, -2, 1)
    previous = jnp.where(index(deep.shape, 0) == 0, 0.0, turned(deep, 1, 0))
    opens = split(level < jnp.minimum(deep, previous), 0)
    none = (0.0, 0.0, 0.0, 0.0)
    base[:, :lanes] = step + explicit_flux(split(c, 0), split(side, 0), opens, 0, none)
    base[:, lanes:] = reverse + reverse_flux(split(h, 0), split(side, 0), opens, 0, none)
    ours = (place == 0) | (place == 1) | (place == slot - 2) | (place == slot - 1)
    mixed = jnp.where(ours & (level + 1.0 < deep), mixed, 0.0)
    for k in range(levels):
        strip_weight[k] = turned(h, -slot * k, 1)
        if k < levels - 1:
            strip_links[k] = turned(mixed, -slot * k, 1)
    strip_joint[...] = factorized(levels, strip_links, strip_inverse)


def strip_states(levels, message, base, factors, weights, lower, upper):
    links, inverse, joint = factors
    c, h, deep, side = (item_of(message, i) for i in (0, 1, 3, 4))
    place, level = placed(c.shape)
    end = c.shape[0] - 1

    def line(ref, item):
        at = 4 * levels + item
        return jnp.broadcast_to(ref[at : at + 1, :lanes], (sublanes, lanes))

    def row_of(value, at):
        return jnp.broadcast_to(value[at : at + 1], (sublanes, lanes))

    values = border_rows(
        level[:sublanes],
        [line(lower, i) for i in range(4)],
        [line(upper, i) for i in range(4)],
        (row_of(c, end - 1), row_of(c, end), row_of(h, end)),
        (row_of(c, 0), row_of(c, 1), row_of(h, 0)),
        (row_of(side, 0), row_of(side, 1), row_of(side, end), line(upper, 5)),
        (line(lower, 4), row_of(deep, 0), row_of(deep, 1), row_of(deep, end - 1), row_of(deep, end), line(upper, 4)),
    )
    row = index((sublanes, lanes), 0)

    def bordered(value, rows):
        tiles = split(value, 0)
        tiles[0] = tiles[0] + jnp.where(row == 0, rows[0], jnp.where(row == 1, rows[1], 0.0))
        tiles[-1] = tiles[-1] + jnp.where(row == sublanes - 2, rows[2], jnp.where(row == sublanes - 1, rows[3], 0.0))
        return jnp.concatenate(tiles, axis=0)

    right = jnp.where(level < deep, bordered(base[:, :lanes], values[:4]), 0.0)
    linear = bordered(base[:, lanes:], values[4:])
    right, linear = ([turned(value, -slot * k, 1) for k in range(levels)] for value in (right, linear))
    passed = [None] * levels
    ends = inward(levels, lambda k: right[k] * inverse[k], links, inverse, joint, passed)
    state = dict(outward(levels, ends, links, inverse, passed))

    def scaled(k):
        return (linear[k] - (2.0 * uptake) * state[k] * weights[k]) * inverse[k]

    ends = inward(levels, scaled, links, inverse, joint, passed)
    weight = dict(outward(levels, ends, links, inverse, passed))
    packed_state = packed_weight = jnp.zeros(c.shape, jnp.float32)
    for k in range(levels):
        here = level == float(k)
        packed_state = jnp.where(here, turned(state[k], slot * k, 1), packed_state)
        value = jnp.where(k < deep, weight[k], 0.0)
        packed_weight = jnp.where(here, turned(value, slot * k, 1), packed_weight)
    return packed_state, packed_weight


def first_kernel(
    north, depth, links, inverse, joint, weight, forward, linear, own_up, own_down, beside, own,
    got_even, got_odd, got_chip, got_core,
    state, weight_next, pay_even, pay_odd, outer, up, down,
    passed, scaled, lower, upper, border,
):
    levels, rows, columns = weight.shape
    even_y, even_x = parities()
    choose(even_y, got_odd, got_even, lower)
    choose(even_y, got_even, got_odd, upper)
    before, after = take(even_x, got_core[...], common(got_chip))
    deep = depth[...]
    depth_float = deep.astype(jnp.float32)
    at = 5 * levels
    speeds = (rows_of(own_down, 4, levels), beside[...], rows_of(own_up, 4, levels), rows_of(upper, 4, levels))
    deeps = (lower[at : at + 1, :], upper[at : at + 1, :])
    borders_y(levels, lower, upper, own_up, own_down, speeds, depth_float, deeps, border)
    four = lambda value: [item_of(value, i) for i in range(4)]
    packed = borders_x(four(before), four(after), four(own))
    for k in range(levels):
        scaled[k] = with_rows(k, levels, forward[k], border, 0)
        state[k] = with_rows(k, levels, linear[k], border, 4)
    for k in range(levels):
        scaled[k] = jnp.where(k < deep, with_columns(k, scaled[k], packed[0]), 0.0) * inverse[k]
        state[k] = with_columns(k, state[k], packed[1])
    ends = inward(levels, lambda k: scaled[k], links, inverse, joint[...], passed)
    for k, current in outward(levels, ends, links, inverse, passed):
        scaled[k] = (state[k] - (2.0 * uptake) * current * weight[k]) * inverse[k]
        state[k] = current
    ends = inward(levels, lambda k: scaled[k], links, inverse, joint[...], passed)
    packed = [jnp.zeros((rows, lanes), jnp.float32)] * 2
    shallow_y = jnp.minimum(deep, turned(deep, 1, 0))
    for k, current in outward(levels, ends, links, inverse, passed):
        h = jnp.where(k < deep, current, 0.0)
        weight_next[k] = h
        c = state[k]
        packed = [pack_columns(k, *each) for each in zip((c, h), packed)]
        pack_rows(k, levels, c, h, north[k] * (1.0 / 12.0), k < shallow_y, up, down)
    strip_rows(levels, got_chip[...], up, down)
    choose(even_y, up, down, pay_even)
    choose(even_y, down, up, pay_odd)
    outer[...] = jnp.concatenate(packed, axis=1)


def second_kernel(
    depth, links, inverse, joint, forward, linear, base, strip_links, strip_inverse, strip_joint, strip_weight,
    own_up, own_down, own, first_up, first_down, beside, first_own,
    got1_even, got1_odd, got1_chip, got1_core, got_even, got_odd, got_core,
    final_far, adjoint_far,
    final, adjoint, passed, scaled, lower, upper, border, sent,
):
    copies = []

    def send(near, far, part):
        copy = pltpu.make_async_copy(near.at[part], far.at[part], sent.at[len(copies)])
        copy.start()
        copies.append(copy)

    levels, rows, columns = forward.shape
    even_y, even_x = parities()
    choose(even_y, got_odd, got_even, lower)
    choose(even_y, got_even, got_odd, upper)
    before1, after1 = take(even_x, got1_core[...], common(got1_chip))
    factors = (strip_links, strip_inverse, strip_joint[...])
    strip = strip_states(levels, got1_chip, base, factors, strip_weight, lower, upper)
    before, after = take(even_x, got_core[...], jnp.concatenate(strip, axis=1))
    deep = depth[...]
    depth_float = deep.astype(jnp.float32)
    at = 5 * levels
    deeps = (
        jnp.where(even_y, got1_odd[at : at + 1, :], got1_even[at : at + 1, :]),
        jnp.where(even_y, got1_even[at : at + 1, :], got1_odd[at : at + 1, :]),
    )
    speed = jnp.where(even_y, rows_of(got1_even, 4, levels), rows_of(got1_odd, 4, levels))
    speeds = (rows_of(first_down, 4, levels), beside[...], rows_of(first_up, 4, levels), speed)
    borders_y(levels, lower, upper, own_up, own_down, speeds, depth_float, deeps, border)

    def four(value, fixed):
        return [item_of(value, 0), item_of(value, 1), item_of(fixed, 2), item_of(fixed, 3)]

    sides = ((before, before1), (after, after1), (own, first_own))
    packed = borders_x(*(four(*side) for side in sides))
    for k in range(levels):
        adjoint[k] = with_rows(k, levels, linear[k], border, 4)
        scaled[k] = with_rows(k, levels, forward[k], border, 0)
    for k in range(levels):
        scaled[k] = jnp.where(k < deep, with_columns(k, scaled[k], packed[0]), 0.0) * inverse[k]
    for k in range(levels):
        adjoint[k] = with_columns(k, adjoint[k], packed[1])
    send(adjoint, adjoint_far, slice(0, levels))
    ends = inward(levels, lambda k: scaled[k], links, inverse, joint[...], passed)
    middle = levels // 2
    quarter = middle // 2
    for k, current in outward(levels, ends, links, inverse, passed):
        final[k] = current
        if k == middle - quarter:
            send(final, final_far, slice(middle - quarter, middle + quarter))
    send(final, final_far, slice(0, middle - quarter))
    send(final, final_far, slice(middle + quarter, levels))
    for copy in copies:
        copy.wait()


def pairs(axis, parity):
    devices = lax.axis_size(axis)
    swaps = []
    for i in range(parity, devices - 1, 2):
        swaps += [(i, i + 1), (i + 1, i)]
    return swaps


def exchange(pay_even, pay_odd, *pay):
    got_even = lax.ppermute(pay_even, "group", pairs("group", 0))
    got_odd = lax.ppermute(pay_odd, "group", pairs("group", 1))
    got = [lax.ppermute(each, "tile", pairs("tile", len(pay) - 1 - i)) for i, each in enumerate(pay)]
    return got_even, got_odd, *got


def shards(tracer, east_speed, north_speed, mixing, depth_levels, sensitivity):
    levels, rows, columns = tracer.shape
    assert levels * slot == lanes and rows % sublanes == 0 and columns % lanes == 0
    f32 = jnp.float32
    field = jax.ShapeDtypeStruct((levels, rows, columns), f32)
    first_size = 5 * levels + sublanes
    second_size = 4 * levels + sublanes
    border_size = 8 * levels
    block = pltpu.VMEM((levels, rows, columns), f32)
    params = pltpu.CompilerParams(vmem_limit_bytes=32 * 1024 * 1024)
    far = pl.BlockSpec(memory_space=pl.ANY)

    def lines(size):
        return jax.ShapeDtypeStruct((size, columns), f32)

    def space(size):
        return pltpu.VMEM((size, columns), f32)

    def tiles(count):
        return jax.ShapeDtypeStruct((rows, count * lanes), f32)

    given = (tracer, east_speed, north_speed, mixing, depth_levels)
    near = tuple(jax.ShapeDtypeStruct(given[i].shape, given[i].dtype) for i in (0, 1, 2, 4))
    links = jax.ShapeDtypeStruct(mixing.shape, f32)
    plane = jax.ShapeDtypeStruct((rows, columns), f32)
    distant = [pltpu.with_memory_space_constraint(array, pltpu.HBM) for array in given + (sensitivity,)]
    outcome = pl.pallas_call(
        factor_kernel,
        in_specs=[far] * 6,
        out_shape=near
        + (links, field, plane, field, lines(first_size), lines(first_size), tiles(6), tiles(4), lines(first_size), lines(first_size), lines(levels)),
        scratch_shapes=[pltpu.VMEM(mixing.shape, f32), block, block, pltpu.SemaphoreType.DMA((6,))],
        compiler_params=params,
    )(*distant)
    tracer, east_speed, north_speed, depth_levels, *factors, weight = outcome[:8]
    pay_even, pay_odd, outer, pay_core, up, down, beside = outcome[8:]
    cells = levels * rows * columns
    inner = pl.CostEstimate(flops=80 * cells, bytes_accessed=24 * cells, transcendentals=0)

    got1 = exchange(pay_even, pay_odd, outer, pay_core)
    parts = pl.pallas_call(inner_kernel, out_shape=(field, field), compiler_params=params, cost_estimate=inner)(
        tracer, weight, east_speed, north_speed, depth_levels
    )
    state, weight_next, pay_even, pay_odd, outer2, up2, down2 = pl.pallas_call(
        first_kernel,
        out_shape=(field, field, lines(second_size), lines(second_size), tiles(2), lines(second_size), lines(second_size)),
        scratch_shapes=[block, block, space(first_size), space(first_size), space(border_size)],
        compiler_params=params,
    )(north_speed, depth_levels, *factors, weight, *parts, up, down, beside, outer, *got1)
    got2 = exchange(pay_even, pay_odd, outer2)

    def strips(count):
        return jax.ShapeDtypeStruct((count, rows, lanes), f32)

    parts = pl.pallas_call(
        second_inner_kernel,
        out_shape=(field, field, tiles(2), strips(levels - 1), strips(levels), tiles(1), strips(levels)),
        compiler_params=params,
        cost_estimate=inner,
    )(state, weight_next, east_speed, north_speed, depth_levels, tracer, outer, got1[2])
    sends = pltpu.SemaphoreType.DMA((4,))
    final, adjoint = pl.pallas_call(
        second_kernel,
        out_specs=[far] * 2,
        out_shape=(field, field),
        scratch_shapes=[block] * 4 + [space(second_size), space(second_size), space(border_size), sends],
        compiler_params=params,
    )(depth_levels, *factors, *parts, up2, down2, outer2, up, down, beside, outer, *got1, *got2)
    return final, adjoint


def solution(mesh):
    block = P(None, "group", "tile")
    in_specs = (block, block, block, block, P("group", "tile"), block)
    return jax.shard_map(shards, mesh=mesh, in_specs=in_specs, out_specs=(block, block), check_vma=False)
```

time: 23.3 us -> 22.1 us (0.948)
  Pallas kernels: 6.91 us -> 5.77 us
    pallas_call x1, Pallas kernels: 2 us -> 1.37 us  [shards(): pl.pallas_call(second_kernel, out_specs=[far] * 2, out_shape=(field, fiel...]
    pallas_call x1, Pallas kernels: 0.99 us -> 0.6 us  [shards(): pl.pallas_call(first_kernel, out_shape=(field, field, lines(second_size),...]
  transfers between devices with their start and end apart: 7 -> 7, of which waited for: 4 -> 3; matrix products, arithmetic and copies ran while one was open for 0% -> 0% of each run, Pallas kernels for 9% -> 10%
where the time goes in v6:
time: 22.1 us; the launch traced here: 21.9 us
  starting transfers between devices  11.1 us (50%)
  Pallas kernels  5.77 us (26%)
  waiting for transfers between devices  4.26 us (19%)
  between operations  0.71 us (3%)
    ppermute x2, starting transfers between devices, exchange(): got_odd = lax.ppermute(pay_odd, 'group', pairs('group', 1))  6.73 us
    ppermute x3, starting transfers between devices, exchange(): lax.ppermute(each, 'tile', pairs('tile', len(pay) - 1 - i))  3.74 us
    ppermute x2, waiting for transfers between devices, exchange(): got_odd = lax.ppermute(pay_odd, 'group', pairs('group', 1))  2.81 us
    pallas_call x1, Pallas kernels, shards(): pl.pallas_call(factor_kernel, in_specs=[far] * 6, out_shape=near + (links...  1.67 us
    pallas_call x1, Pallas kernels, shards(): pl.pallas_call(second_kernel, out_specs=[far] * 2, out_shape=(field, fiel...  1.37 us
    pallas_call x1, Pallas kernels, shards(): pl.pallas_call(second_inner_kernel, out_shape=(field, field, tiles(2), st...  1.14 us
    pallas_call x1, Pallas kernels, shards(): pl.pallas_call(inner_kernel, out_shape=(field, field), compiler_params=pa...  1 us
    ppermute x3, waiting for transfers between devices, exchange(): lax.ppermute(each, 'tile', pairs('tile', len(pay) - 1 - i))  0.75 us
  transfers between devices with their start and end apart: 7, of which 3 were waited for; matrix products, arithmetic and copies ran while one was open for 0% of the time, Pallas kernels for 10%

profile of v6, /device:TPU:10, one launch (start us, length us, event | category | flops | bytes accessed | tf_op | source)
XLA Modules:
  0.0 21.9 jit_solution(13331401363785950391)
XLA Ops:
  0.6 1.7 %shard_map.77 = (f32[16,16,256]{2,1,0:T(8,128)S(1)}, f32[16,16,256]{2,1,0:T(8,128)S(1)}, f32[16,16,256]{2,1,0:T(8,128)S(1)}, s32[16,256]{1,0:T(8,128)S(1)}, f32[...) custom-call(f32[16,16,256]{2,1,0:T(8,128)} %tracer_far.1, ...), custom_call_target="tpu_custom_call" | custom-call | tf_op jit(solution)/shard_map/pallas_call | solution.py:617
  2.3 0.6 %collective-permute-start = (f32[88,256]{1,0:T(8,128)S(1)}, f32[88,256]{1,0:T(8,128)S(1)}, u32[]{:S(2)}, u32[]{:S(2)}) collective-permute-start(f32[88,256]{1,0:T(8,128)S(1)} %get-tuple-element.47), channel_id=1, source_target_pairs={{0,8},{8,0},{16,24},{24,16},{1,9},{9,1},{17,25},{25,17},{2,10},{10... | collective-permute-start | bytes 270344 | tf_op jit(solution)/shard_map/ppermute | solution.py:585
  2.9 4.3 %collective-permute-start.1 = (f32[88,256]{1,0:T(8,128)S(1)}, f32[88,256]{1,0:T(8,128)S(1)}, u32[]{:S(2)}, u32[]{:S(2)}) collective-permute-start(f32[88,256]{1,0:T(8,128)S(1)} %get-tuple-element.48), channel_id=1, source_target_pairs={{8,16},{16,8},{9,17},{17,9},{10,18},{18,10},{11,19},{19,11},{12,20... | collective-permute-start | bytes 270344 | tf_op jit(solution)/shard_map/ppermute | solution.py:586
  7.3 1.9 %collective-permute-start.2 = (f32[16,768]{1,0:T(8,128)S(1)}, f32[16,768]{1,0:T(8,128)S(1)}, u32[]{:S(2)}, u32[]{:S(2)}) collective-permute-start(f32[16,768]{1,0:T(8,128)S(1)} %get-tuple-element.46.own.outer.first_own), channel_id=1, source_target_pairs={{1,2},{2,1},{3,4},{4,3},{5,6},{6,5},{9,10},{10,9},{11,12},{12,11},... | collective-permute-start | bytes 147464 | tf_op jit(solution)/shard_map/ppermute | solution.py:587
  9.2 1.7 %collective-permute-start.3 = (f32[16,512]{1,0:T(8,128)S(1)}, f32[16,512]{1,0:T(8,128)S(1)}, u32[]{:S(2)}, u32[]{:S(2)}) collective-permute-start(f32[16,512]{1,0:T(8,128)S(1)} %get-tuple-element.49), channel_id=1, source_target_pairs={{0,1},{1,0},{2,3},{3,2},{4,5},{5,4},{6,7},{7,6},{8,9},{9,8},{10,11... | collective-permute-start | bytes 98312 | tf_op jit(solution)/shard_map/ppermute | solution.py:587
  10.9 1.0 %shard_map.78 = (f32[16,16,256]{2,1,0:T(8,128)S(1)}, f32[16,16,256]{2,1,0:T(8,128)S(1)}) custom-call(f32[16,16,256]{2,1,0:T(8,128)S(1)} %get-tuple-element.39.c_ref.tracer, f32[16,16,256]{2,1,0:T(8,128)S(1)} %get-tuple-element.38.h_ref.weight, f32[16,16,256]{2,1,0:T(8,128)S(1)} %get-tuple-element.40.east, f32[16,16,256]{2,1,0:T(8,128)S(1)} %get-tuple-element.37.north, ...), custom_call_target="tpu_custom_call" | custom-call | flops 5242880 | bytes 1572864 | tf_op jit(solution)/shard_map/pallas_call | solution.py:631
  11.9 0.0 collective-permute-done.3.got_core.got1_core
  11.9 0.7 %collective-permute-done.2.got_chip.got1_chip = f32[16,768]{1,0:T(8,128)S(1)} collective-permute-done((f32[16,768]{1,0:T(8,128)S(1)}, f32[16,768]{1,0:T(8,128)S(1)}, u32[]{:S(2)}, u32[]{:S(2)}) %collective-permute-start.2) | collective-permute-done | bytes 49184 | tf_op jit(solution)/shard_map/ppermute | solution.py:587
  12.7 0.0 collective-permute-done.got_even.got1_even
  12.7 0.0 collective-permute-done.1.got_odd.got1_odd
  12.7 0.6 %shard_map.79 = (f32[16,16,256]{2,1,0:T(8,128)S(1)}, f32[16,16,256]{2,1,0:T(8,128)S(1)}, f32[72,256]{1,0:T(8,128)S(1)}, f32[72,256]{1,0:T(8,128)S(1)}, f32[16,25...) custom-call(f32[16,16,256]{2,1,0:T(8,128)S(1)} %get-tuple-element.37.north, ...), custom_call_target="tpu_custom_call" | custom-call | tf_op jit(solution)/shard_map/pallas_call | solution.py:634
  13.3 0.1 collective-permute-start.4
  13.4 2.4 %collective-permute-start.5 = (f32[72,256]{1,0:T(8,128)S(1)}, f32[72,256]{1,0:T(8,128)S(1)}, u32[]{:S(2)}, u32[]{:S(2)}) collective-permute-start(f32[72,256]{1,0:T(8,128)S(1)} %get-tuple-element.63), channel_id=1, source_target_pairs={{8,16},{16,8},{9,17},{17,9},{10,18},{18,10},{11,19},{19,11},{12,20... | collective-permute-start | bytes 221192 | tf_op jit(solution)/shard_map/ppermute | solution.py:586
  15.8 0.1 collective-permute-start.6
  15.8 1.1 %shard_map.80 = (f32[16,16,256]{2,1,0:T(8,128)S(1)}, f32[16,16,256]{2,1,0:T(8,128)S(1)}, f32[16,256]{1,0:T(8,128)S(1)}, f32[15,16,128]{2,1,0:T(8,128)S(1)}, f32[...) custom-call(f32[16,16,256]{2,1,0:T(8,128)S(1)} %get-tuple-element.50.c_ref, ...), custom_call_target="tpu_custom_call" | custom-call | flops 5242880 | bytes 1572864 | tf_op jit(solution)/shard_map/pallas_call | solution.py:645
  17.0 0.0 collective-permute-done.6.got_core
  17.0 0.7 %collective-permute-done.4.got_even = f32[72,256]{1,0:T(8,128)S(1)} collective-permute-done((f32[72,256]{1,0:T(8,128)S(1)}, f32[72,256]{1,0:T(8,128)S(1)}, u32[]{:S(2)}, u32[]{:S(2)}) %collective-permute-start.4) | collective-permute-done | bytes 73760 | tf_op jit(solution)/shard_map/ppermute | solution.py:585
  17.7 2.8 %collective-permute-done.5.got_odd = f32[72,256]{1,0:T(8,128)S(1)} collective-permute-done((f32[72,256]{1,0:T(8,128)S(1)}, f32[72,256]{1,0:T(8,128)S(1)}, u32[]{:S(2)}, u32[]{:S(2)}) %collective-permute-start.5) | collective-permute-done | bytes 73760 | tf_op jit(solution)/shard_map/ppermute | solution.py:586
  20.5 1.4 %shard_map.81 = (f32[16,16,256]{2,1,0:T(8,128)}, f32[16,16,256]{2,1,0:T(8,128)}) custom-call(s32[16,256]{1,0:T(8,128)S(1)} %get-tuple-element.33.depth, f32[15,16,256]{2,1,0:T(8,128)S(1)} %get-tuple-element.34.links, f32[16,16,256]{2,1,0:T(8,128)S(1)} %get-tuple-element.35.inverse, f32[16,256]{1,0:T(8,128)S(1)} %get-tuple-element.36.joint, ...), custom_call_target="tpu_custom_call" | custom-call | tf_op jit(solution)/shard_map/pallas_call | solution.py:652
Async XLA Ops:
  2.3 10.4 %collective-permute-start = (f32[88,256]{1,0:T(8,128)S(1)}, f32[88,256]{1,0:T(8,128)S(1)}, u32[]{:S(2)}, u32[]{:S(2)}) collective-permute-start(f32[88,256]{1,0:T(8,128)S(1)} %get-tuple-element.47), channel_id=1, source_target_pairs={{0,8},{8,0},{16,24},{24,16},{1,9},{9,1},{17,25},{25,17},{2,10},{10... | collective-permute-start | bytes 270344 | tf_op jit(solution)/shard_map/ppermute | solution.py:585
  2.9 9.8 %collective-permute-start.1 = (f32[88,256]{1,0:T(8,128)S(1)}, f32[88,256]{1,0:T(8,128)S(1)}, u32[]{:S(2)}, u32[]{:S(2)}) collective-permute-start(f32[88,256]{1,0:T(8,128)S(1)} %get-tuple-element.48), channel_id=1, source_target_pairs={{8,16},{16,8},{9,17},{17,9},{10,18},{18,10},{11,19},{19,11},{12,20... | collective-permute-start | bytes 270344 | tf_op jit(solution)/shard_map/ppermute | solution.py:586
  7.3 5.4 %collective-permute-start.2 = (f32[16,768]{1,0:T(8,128)S(1)}, f32[16,768]{1,0:T(8,128)S(1)}, u32[]{:S(2)}, u32[]{:S(2)}) collective-permute-start(f32[16,768]{1,0:T(8,128)S(1)} %get-tuple-element.46.own.outer.first_own), channel_id=1, source_target_pairs={{1,2},{2,1},{3,4},{4,3},{5,6},{6,5},{9,10},{10,9},{11,12},{12,11},... | collective-permute-start | bytes 147464 | tf_op jit(solution)/shard_map/ppermute | solution.py:587
  9.2 2.8 %collective-permute-start.3 = (f32[16,512]{1,0:T(8,128)S(1)}, f32[16,512]{1,0:T(8,128)S(1)}, u32[]{:S(2)}, u32[]{:S(2)}) collective-permute-start(f32[16,512]{1,0:T(8,128)S(1)} %get-tuple-element.49), channel_id=1, source_target_pairs={{0,1},{1,0},{2,3},{3,2},{4,5},{5,4},{6,7},{7,6},{8,9},{9,8},{10,11... | collective-permute-start | bytes 98312 | tf_op jit(solution)/shard_map/ppermute | solution.py:587
  13.3 4.4 %collective-permute-start.4 = (f32[72,256]{1,0:T(8,128)S(1)}, f32[72,256]{1,0:T(8,128)S(1)}, u32[]{:S(2)}, u32[]{:S(2)}) collective-permute-start(f32[72,256]{1,0:T(8,128)S(1)} %get-tuple-element.62), channel_id=1, source_target_pairs={{0,8},{8,0},{16,24},{24,16},{1,9},{9,1},{17,25},{25,17},{2,10},{10... | collective-permute-start | bytes 221192 | tf_op jit(solution)/shard_map/ppermute | solution.py:585
  13.4 7.1 %collective-permute-start.5 = (f32[72,256]{1,0:T(8,128)S(1)}, f32[72,256]{1,0:T(8,128)S(1)}, u32[]{:S(2)}, u32[]{:S(2)}) collective-permute-start(f32[72,256]{1,0:T(8,128)S(1)} %get-tuple-element.63), channel_id=1, source_target_pairs={{8,16},{16,8},{9,17},{17,9},{10,18},{18,10},{11,19},{19,11},{12,20... | collective-permute-start | bytes 221192 | tf_op jit(solution)/shard_map/ppermute | solution.py:586
  15.8 1.2 %collective-permute-start.6 = (f32[16,256]{1,0:T(8,128)S(1)}, f32[16,256]{1,0:T(8,128)S(1)}, u32[]{:S(2)}, u32[]{:S(2)}) collective-permute-start(f32[16,256]{1,0:T(8,128)S(1)} %get-tuple-element.61.own), channel_id=1, source_target_pairs={{0,1},{1,0},{2,3},{3,2},{4,5},{5,4},{6,7},{7,6},{8,9},{9,8},{10,11... | collective-permute-start | bytes 49160 | tf_op jit(solution)/shard_map/ppermute | solution.py:587

commit v7 on v6

--- a/solution.py
+++ b/solution.py
@@ -73,10 +73,14 @@
     return lax.div(lax.rem(lane + slot // 2, lanes), slot)
 
 
-def pack_columns(k, item, packed):
+def pack_columns(k, item, packed, ahead=0):
     lane = index(packed.shape, 1)
     tile = jnp.where(lane < lanes // 2, item[:, :lanes], item[:, -lanes:])
-    return jnp.where(level_of(lane) == k, turned(tile, slot * k, 1), packed)
+    return jnp.where(level_of(lane + (lanes - ahead)) == k, turned(tile, slot * k + ahead, 1), packed)
+
+
+def second_item(tile):
+    return turned(tile, -(slot // 2), 1)
 
 
 def repeated(value):
@@ -165,7 +169,7 @@
 
 def factor_kernel(
     tracer_far, east_far, north_far, mixing_far, depth_far, sensitivity_far,
-    tracer, east, north, depth, links, inverse, joint, weight, pay_even, pay_odd, outer, pay_core, up, down, beside,
+    tracer, east, north, depth, links, inverse, joint, weight, pay_even, pay_odd, outer, pay_chip, pay_core, up, down, beside,
     mixing, sensitivity, passed, arrived,
 ):
     order = (
@@ -180,11 +184,11 @@
     for copy in copies:
         copy.start()
     levels, rows, columns = tracer.shape
-    even_y, _ = parities()
+    even_y, even_x = parities()
     copies[0].wait()
     deep = depth[...]
     depth_float = deep.astype(jnp.float32)
-    outer[:, 3 * lanes : 4 * lanes] = repeated(depth_float)
+    packed_depth = repeated(depth_float)
     for copy in copies[1:3]:
         copy.wait()
     shallow_y = jnp.minimum(deep, turned(deep, 1, 0))
@@ -202,15 +206,20 @@
         speed_x = east[k] * (1.0 / 12.0)
         speed_y = north[k] * (1.0 / 12.0)
         items = (c, h, speed_x, speed_y) + ((mixing[k],) if k < levels - 1 else ())
-        packed[: len(items)] = [pack_columns(k, *each) for each in zip(items, packed)]
+        ahead = (0, slot // 2, 0, slot // 2, slot // 2)
+        packed[: len(items)] = [pack_columns(k, *each) for each in zip(items, packed, ahead)]
         pack_rows(k, levels, c, h, speed_y, k < shallow_y, up, down)
         at = 4 * levels + k
         down[at : at + 1, :] = speed_y[0:1]
         up[at : at + 1, :] = speed_y[rows - 1 :]
         beside[k : k + 1, :] = speed_y[1:2]
-    for place, value in zip((0, 1, 2, 4, 5), packed):
-        outer[:, place * lanes : (place + 1) * lanes] = value
-    pay_core[...] = common(outer)
+    start = lax.rem(index((rows, lanes), 1), slot) < slot // 2
+    twice = ((packed[0], packed[1]), (packed[2], packed[3]), (packed_depth, packed[4]))
+    first = jnp.concatenate([jnp.where(start, a, b) for a, b in twice], axis=1)
+    last = jnp.concatenate([jnp.where(start, b, a) for a, b in twice], axis=1)
+    pay_chip[...] = jnp.where(even_x, first, last)
+    pay_core[...] = jnp.where(even_x, last, first)
+    outer[...] = jnp.concatenate([packed[0], packed[1], packed[2], packed_depth], axis=1)
     at = 5 * levels
     up[at : at + sublanes, :] = jnp.broadcast_to(depth_float[rows - 1 :], (sublanes, columns))
     down[at : at + sublanes, :] = jnp.broadcast_to(depth_float[0:1], (sublanes, columns))
@@ -365,12 +374,19 @@
     return jnp.where(flag, chip, core), jnp.where(flag, core, chip)
 
 
-def common(ref):
-    return ref[:, : 4 * lanes]
+def four_items(message):
+    values, speeds, depths = (item_of(message, i) for i in range(3))
+    return [values, second_item(values), speeds, depths]
+
+
+def own_items(outer):
+    values, shifted_values, speeds, depths = (item_of(outer, i) for i in range(4))
+    return [values, second_item(shifted_values), speeds, depths]
 
 
 def strip_rows(levels, message, up, down):
-    c, h, deep, side = (item_of(message, i) for i in (0, 1, 3, 4))
+    c, h, speeds, deep = four_items(message)
+    side = second_item(speeds)
     size = c.shape[0]
     _, level = placed(c.shape)
     is_open = level < jnp.minimum(deep, turned(deep, 1, 0))
@@ -388,15 +404,21 @@
 
 def second_inner_kernel(
     c_ref, h_ref, east, north, depth, tracer, outer, got_chip,
-    forward, linear, base, strip_links, strip_inverse, strip_joint, strip_weight,
+    forward, linear, base, strip_links, strip_inverse, strip_joint, strip_weight, strip_values, outer_next,
 ):
+    levels = c_ref.shape[0]
+    packed = [jnp.zeros((outer.shape[0], lanes), jnp.float32)] * 2
+    for k in range(levels):
+        packed = [pack_columns(k, *each) for each in zip((c_ref[k], h_ref[k]), packed)]
+    outer_next[...] = jnp.concatenate(packed, axis=1)
     inner_kernel(c_ref, h_ref, east, north, depth, tracer, forward, linear)
-    levels = c_ref.shape[0]
     _, even = parities()
     place, level = placed((outer.shape[0], lanes))
     ours = (place < slot // 2) == even
-    c, h, speed, deep = (jnp.where(ours, item_of(outer, i), item_of(got_chip, i)) for i in range(4))
-    side, mixed = item_of(got_chip, 4), item_of(got_chip, 5)
+    items = four_items(got_chip)
+    side, mixed = second_item(items[2]), second_item(items[3])
+    strip_values[...] = jnp.concatenate([items[0], items[1], items[3], side], axis=1)
+    c, h, speed, deep = (jnp.where(ours, mine, item) for mine, item in zip(own_items(outer), items))
     is_open = level < jnp.minimum(deep, turned(deep, 1, 1))
     flux = face_flux(c, turned(c, 1, 1), turned(c, -1, 1), turned(c, 2, 1), speed, is_open)
     jump = jnp.where(is_open, h - turned(h, 1, 1), 0.0)
@@ -419,9 +441,9 @@
     strip_joint[...] = factorized(levels, strip_links, strip_inverse)
 
 
-def strip_states(levels, message, base, factors, weights, lower, upper):
+def strip_states(levels, values, base, factors, weights, lower, upper):
     links, inverse, joint = factors
-    c, h, deep, side = (item_of(message, i) for i in (0, 1, 3, 4))
+    c, h, deep, side = (item_of(values, i) for i in range(4))
     place, level = placed(c.shape)
     end = c.shape[0] - 1
 
@@ -432,7 +454,7 @@
     def row_of(value, at):
         return jnp.broadcast_to(value[at : at + 1], (sublanes, lanes))
 
-    values = border_rows(
+    added = border_rows(
         level[:sublanes],
         [line(lower, i) for i in range(4)],
         [line(upper, i) for i in range(4)],
@@ -449,8 +471,8 @@
         tiles[-1] = tiles[-1] + jnp.where(row == sublanes - 2, rows[2], jnp.where(row == sublanes - 1, rows[3], 0.0))
         return jnp.concatenate(tiles, axis=0)
 
-    right = jnp.where(level < deep, bordered(base[:, :lanes], values[:4]), 0.0)
-    linear = bordered(base[:, lanes:], values[4:])
+    right = jnp.where(level < deep, bordered(base[:, :lanes], added[:4]), 0.0)
+    linear = bordered(base[:, lanes:], added[4:])
     right, linear = ([turned(value, -slot * k, 1) for k in range(levels)] for value in (right, linear))
     passed = [None] * levels
     ends = inward(levels, lambda k: right[k] * inverse[k], links, inverse, joint, passed)
@@ -473,22 +495,21 @@
 def first_kernel(
     north, depth, links, inverse, joint, weight, forward, linear, own_up, own_down, beside, own,
     got_even, got_odd, got_chip, got_core,
-    state, weight_next, pay_even, pay_odd, outer, up, down,
+    state, weight_next, pay_even, pay_odd, up, down,
     passed, scaled, lower, upper, border,
 ):
     levels, rows, columns = weight.shape
     even_y, even_x = parities()
     choose(even_y, got_odd, got_even, lower)
     choose(even_y, got_even, got_odd, upper)
-    before, after = take(even_x, got_core[...], common(got_chip))
+    before, after = take(even_x, got_core[...], got_chip[...])
     deep = depth[...]
     depth_float = deep.astype(jnp.float32)
     at = 5 * levels
     speeds = (rows_of(own_down, 4, levels), beside[...], rows_of(own_up, 4, levels), rows_of(upper, 4, levels))
     deeps = (lower[at : at + 1, :], upper[at : at + 1, :])
     borders_y(levels, lower, upper, own_up, own_down, speeds, depth_float, deeps, border)
-    four = lambda value: [item_of(value, i) for i in range(4)]
-    packed = borders_x(four(before), four(after), four(own))
+    packed = borders_x(four_items(before), four_items(after), own_items(own))
     for k in range(levels):
         scaled[k] = with_rows(k, levels, forward[k], border, 0)
         state[k] = with_rows(k, levels, linear[k], border, 4)
@@ -500,22 +521,19 @@
         scaled[k] = (state[k] - (2.0 * uptake) * current * weight[k]) * inverse[k]
         state[k] = current
     ends = inward(levels, lambda k: scaled[k], links, inverse, joint[...], passed)
-    packed = [jnp.zeros((rows, lanes), jnp.float32)] * 2
     shallow_y = jnp.minimum(deep, turned(deep, 1, 0))
     for k, current in outward(levels, ends, links, inverse, passed):
         h = jnp.where(k < deep, current, 0.0)
         weight_next[k] = h
         c = state[k]
-        packed = [pack_columns(k, *each) for each in zip((c, h), packed)]
         pack_rows(k, levels, c, h, north[k] * (1.0 / 12.0), k < shallow_y, up, down)
     strip_rows(levels, got_chip[...], up, down)
     choose(even_y, up, down, pay_even)
     choose(even_y, down, up, pay_odd)
-    outer[...] = jnp.concatenate(packed, axis=1)
 
 
 def second_kernel(
-    depth, links, inverse, joint, forward, linear, base, strip_links, strip_inverse, strip_joint, strip_weight,
+    depth, links, inverse, joint, forward, linear, base, strip_links, strip_inverse, strip_joint, strip_weight, strip_values,
     own_up, own_down, own, first_up, first_down, beside, first_own,
     got1_even, got1_odd, got1_chip, got1_core, got_even, got_odd, got_core,
     final_far, adjoint_far,
@@ -532,9 +550,9 @@
     even_y, even_x = parities()
     choose(even_y, got_odd, got_even, lower)
     choose(even_y, got_even, got_odd, upper)
-    before1, after1 = take(even_x, got1_core[...], common(got1_chip))
+    before1, after1 = take(even_x, got1_core[...], got1_chip[...])
     factors = (strip_links, strip_inverse, strip_joint[...])
-    strip = strip_states(levels, got1_chip, base, factors, strip_weight, lower, upper)
+    strip = strip_states(levels, strip_values, base, factors, strip_weight, lower, upper)
     before, after = take(even_x, got_core[...], jnp.concatenate(strip, axis=1))
     deep = depth[...]
     depth_float = deep.astype(jnp.float32)
@@ -547,11 +565,10 @@
     speeds = (rows_of(first_down, 4, levels), beside[...], rows_of(first_up, 4, levels), speed)
     borders_y(levels, lower, upper, own_up, own_down, speeds, depth_float, deeps, border)
 
-    def four(value, fixed):
-        return [item_of(value, 0), item_of(value, 1), item_of(fixed, 2), item_of(fixed, 3)]
-
-    sides = ((before, before1), (after, after1), (own, first_own))
-    packed = borders_x(*(four(*side) for side in sides))
+    pair = lambda value: [item_of(value, 0), item_of(value, 1)]
+    ends = (pair(before) + four_items(before1)[2:], pair(after) + four_items(after1)[2:])
+    mine = pair(own) + [item_of(first_own, 2), item_of(first_own, 3)]
+    packed = borders_x(*ends, mine)
     for k in range(levels):
         adjoint[k] = with_rows(k, levels, linear[k], border, 4)
         scaled[k] = with_rows(k, levels, forward[k], border, 0)
@@ -618,36 +635,37 @@
         factor_kernel,
         in_specs=[far] * 6,
         out_shape=near
-        + (links, field, plane, field, lines(first_size), lines(first_size), tiles(6), tiles(4), lines(first_size), lines(first_size), lines(levels)),
+        + (links, field, plane, field, lines(first_size), lines(first_size), tiles(4), tiles(3), tiles(3), lines(first_size), lines(first_size), lines(levels)),
         scratch_shapes=[pltpu.VMEM(mixing.shape, f32), block, block, pltpu.SemaphoreType.DMA((6,))],
         compiler_params=params,
     )(*distant)
     tracer, east_speed, north_speed, depth_levels, *factors, weight = outcome[:8]
-    pay_even, pay_odd, outer, pay_core, up, down, beside = outcome[8:]
+    *messages, up, down, beside = outcome[8:]
+    pay_even, pay_odd, outer, pay_chip, pay_core = messages
     cells = levels * rows * columns
     inner = pl.CostEstimate(flops=80 * cells, bytes_accessed=24 * cells, transcendentals=0)
 
-    got1 = exchange(pay_even, pay_odd, outer, pay_core)
+    got1 = exchange(pay_even, pay_odd, pay_chip, pay_core)
     parts = pl.pallas_call(inner_kernel, out_shape=(field, field), compiler_params=params, cost_estimate=inner)(
         tracer, weight, east_speed, north_speed, depth_levels
     )
-    state, weight_next, pay_even, pay_odd, outer2, up2, down2 = pl.pallas_call(
+    state, weight_next, pay_even, pay_odd, up2, down2 = pl.pallas_call(
         first_kernel,
-        out_shape=(field, field, lines(second_size), lines(second_size), tiles(2), lines(second_size), lines(second_size)),
+        out_shape=(field, field) + (lines(second_size),) * 4,
         scratch_shapes=[block, block, space(first_size), space(first_size), space(border_size)],
         compiler_params=params,
     )(north_speed, depth_levels, *factors, weight, *parts, up, down, beside, outer, *got1)
-    got2 = exchange(pay_even, pay_odd, outer2)
 
     def strips(count):
         return jax.ShapeDtypeStruct((count, rows, lanes), f32)
 
-    parts = pl.pallas_call(
+    *parts, outer2 = pl.pallas_call(
         second_inner_kernel,
-        out_shape=(field, field, tiles(2), strips(levels - 1), strips(levels), tiles(1), strips(levels)),
+        out_shape=(field, field, tiles(2), strips(levels - 1), strips(levels), tiles(1), strips(levels), tiles(4), tiles(2)),
         compiler_params=params,
         cost_estimate=inner,
     )(state, weight_next, east_speed, north_speed, depth_levels, tracer, outer, got1[2])
+    got2 = exchange(pay_even, pay_odd, outer2)
     sends = pltpu.SemaphoreType.DMA((4,))
     final, adjoint = pl.pallas_call(
         second_kernel,

time: 22.1 us -> 21.9 us (level)
  waiting for transfers between devices: 4.26 us -> 3.89 us
    ppermute x3, waiting for transfers between devices: 0.75 us -> 1.64 us  [exchange(): lax.ppermute(each, 'tile', pairs('tile', len(pay) - 1 - i))]
    ppermute x2, waiting for transfers between devices: 0.7 us -> 0.01 us  [exchange(): got_even = lax.ppermute(pay_even, 'group', pairs('group', 0))]
    ppermute x2, waiting for transfers between devices: 2.81 us -> 2.24 us  [exchange(): got_odd = lax.ppermute(pay_odd, 'group', pairs('group', 1))]
where the time goes in v7:
time: 21.9 us; the launch traced here: 21.6 us
  starting transfers between devices  11.1 us (51%)
  Pallas kernels  5.89 us (27%)
  waiting for transfers between devices  3.89 us (18%)
  between operations  0.71 us (3%)
    ppermute x2, starting transfers between devices, exchange(): got_odd = lax.ppermute(pay_odd, 'group', pairs('group', 1))  6.73 us
    ppermute x3, starting transfers between devices, exchange(): lax.ppermute(each, 'tile', pairs('tile', len(pay) - 1 - i))  3.74 us
    ppermute x2, waiting for transfers between devices, exchange(): got_odd = lax.ppermute(pay_odd, 'group', pairs('group', 1))  2.24 us
    pallas_call x1, Pallas kernels, shards(): pl.pallas_call(factor_kernel, in_specs=[far] * 6, out_shape=near + (links...  1.69 us
    ppermute x3, waiting for transfers between devices, exchange(): lax.ppermute(each, 'tile', pairs('tile', len(pay) - 1 - i))  1.64 us
    pallas_call x1, Pallas kernels, shards(): pl.pallas_call(second_kernel, out_specs=[far] * 2, out_shape=(field, fiel...  1.38 us
    pallas_call x1, Pallas kernels, shards(): pl.pallas_call(second_inner_kernel, out_shape=(field, field, tiles(2), st...  1.26 us
    pallas_call x1, Pallas kernels, shards(): pl.pallas_call(inner_kernel, out_shape=(field, field), compiler_params=pa...  1 us
  transfers between devices with their start and end apart: 7, of which 3 were waited for; matrix products, arithmetic and copies ran while one was open for 0% of the time, Pallas kernels for 10%

profile of v7, /device:TPU:10, one launch (start us, length us, event | category | flops | bytes accessed | tf_op | source)
XLA Modules:
  0.0 21.6 jit_solution(14465745295756467509)
XLA Ops:
  0.6 1.7 %shard_map.77 = (f32[16,16,256]{2,1,0:T(8,128)S(1)}, f32[16,16,256]{2,1,0:T(8,128)S(1)}, f32[16,16,256]{2,1,0:T(8,128)S(1)}, s32[16,256]{1,0:T(8,128)S(1)}, f32[...) custom-call(f32[16,16,256]{2,1,0:T(8,128)} %tracer_far.1, ...), custom_call_target="tpu_custom_call" | custom-call | tf_op jit(solution)/shard_map/pallas_call | solution.py:634
  2.3 0.6 %collective-permute-start = (f32[88,256]{1,0:T(8,128)S(1)}, f32[88,256]{1,0:T(8,128)S(1)}, u32[]{:S(2)}, u32[]{:S(2)}) collective-permute-start(f32[88,256]{1,0:T(8,128)S(1)} %get-tuple-element.49), channel_id=1, source_target_pairs={{0,8},{8,0},{16,24},{24,16},{1,9},{9,1},{17,25},{25,17},{2,10},{10... | collective-permute-start | bytes 270344 | tf_op jit(solution)/shard_map/ppermute | solution.py:602
  2.9 4.3 %collective-permute-start.1 = (f32[88,256]{1,0:T(8,128)S(1)}, f32[88,256]{1,0:T(8,128)S(1)}, u32[]{:S(2)}, u32[]{:S(2)}) collective-permute-start(f32[88,256]{1,0:T(8,128)S(1)} %get-tuple-element.50), channel_id=1, source_target_pairs={{8,16},{16,8},{9,17},{17,9},{10,18},{18,10},{11,19},{19,11},{12,20... | collective-permute-start | bytes 270344 | tf_op jit(solution)/shard_map/ppermute | solution.py:603
  7.3 1.9 %collective-permute-start.2 = (f32[16,384]{1,0:T(8,128)S(1)}, f32[16,384]{1,0:T(8,128)S(1)}, u32[]{:S(2)}, u32[]{:S(2)}) collective-permute-start(f32[16,384]{1,0:T(8,128)S(1)} %get-tuple-element.51), channel_id=1, source_target_pairs={{1,2},{2,1},{3,4},{4,3},{5,6},{6,5},{9,10},{10,9},{11,12},{12,11},... | collective-permute-start | bytes 73736 | tf_op jit(solution)/shard_map/ppermute | solution.py:604
  9.2 1.7 %collective-permute-start.3 = (f32[16,384]{1,0:T(8,128)S(1)}, f32[16,384]{1,0:T(8,128)S(1)}, u32[]{:S(2)}, u32[]{:S(2)}) collective-permute-start(f32[16,384]{1,0:T(8,128)S(1)} %get-tuple-element.52), channel_id=1, source_target_pairs={{0,1},{1,0},{2,3},{3,2},{4,5},{5,4},{6,7},{7,6},{8,9},{9,8},{10,11... | collective-permute-start | bytes 73736 | tf_op jit(solution)/shard_map/ppermute | solution.py:604
  11.0 1.0 %shard_map.78 = (f32[16,16,256]{2,1,0:T(8,128)S(1)}, f32[16,16,256]{2,1,0:T(8,128)S(1)}) custom-call(f32[16,16,256]{2,1,0:T(8,128)S(1)} %get-tuple-element.41.c_ref.tracer, f32[16,16,256]{2,1,0:T(8,128)S(1)} %get-tuple-element.40.h_ref.weight, f32[16,16,256]{2,1,0:T(8,128)S(1)} %get-tuple-element.42.east, f32[16,16,256]{2,1,0:T(8,128)S(1)} %get-tuple-element.39.north, ...), custom_call_target="tpu_custom_call" | custom-call | flops 5242880 | bytes 1572864 | tf_op jit(solution)/shard_map/pallas_call | solution.py:649
  12.0 0.5 %collective-permute-done.2.got_chip.got1_chip = f32[16,384]{1,0:T(8,128)S(1)} collective-permute-done((f32[16,384]{1,0:T(8,128)S(1)}, f32[16,384]{1,0:T(8,128)S(1)}, u32[]{:S(2)}, u32[]{:S(2)}) %collective-permute-start.2) | collective-permute-done | bytes 24608 | tf_op jit(solution)/shard_map/ppermute | solution.py:604
  12.4 0.0 collective-permute-done.3.got_core.got1_core
  12.4 0.0 collective-permute-done.got_even.got1_even
  12.4 0.0 collective-permute-done.1.got_odd.got1_odd
  12.4 0.6 %shard_map.79 = (f32[16,16,256]{2,1,0:T(8,128)S(1)}, f32[16,16,256]{2,1,0:T(8,128)S(1)}, f32[72,256]{1,0:T(8,128)S(1)}, f32[72,256]{1,0:T(8,128)S(1)}, f32[72,256]{1,0:T(8,128)S(1)}, /*index=5*/f32[72,256]{1,0:T(8,128)S(1)}) custom-call(f32[16,16,256]{2,1,0:T(8,128)S(1)} %get-tuple-element.39.north, s32[16,256]{1,0:T(8,128)S(1)} %get-tuple-element.35.depth, ...), custom_call_target="tpu_custom_call" | custom-call | tf_op jit(solution)/shard_map/pallas_call | solution.py:652
  13.0 0.1 collective-permute-start.4
  13.1 2.4 %collective-permute-start.5 = (f32[72,256]{1,0:T(8,128)S(1)}, f32[72,256]{1,0:T(8,128)S(1)}, u32[]{:S(2)}, u32[]{:S(2)}) collective-permute-start(f32[72,256]{1,0:T(8,128)S(1)} %get-tuple-element.67), channel_id=1, source_target_pairs={{8,16},{16,8},{9,17},{17,9},{10,18},{18,10},{11,19},{19,11},{12,20... | collective-permute-start | bytes 221192 | tf_op jit(solution)/shard_map/ppermute | solution.py:603
  15.5 1.3 %shard_map.80 = (f32[16,16,256]{2,1,0:T(8,128)S(1)}, f32[16,16,256]{2,1,0:T(8,128)S(1)}, f32[16,256]{1,0:T(8,128)S(1)}, f32[15,16,128]{2,1,0:T(8,128)S(1)}, f32[...) custom-call(f32[16,16,256]{2,1,0:T(8,128)S(1)} %get-tuple-element.53, ...), custom_call_target="tpu_custom_call" | custom-call | flops 5242880 | bytes 1572864 | tf_op jit(solution)/shard_map/pallas_call | solution.py:662
  16.7 0.1 collective-permute-start.6
  16.8 1.2 %collective-permute-done.6.got_core = f32[16,256]{1,0:T(8,128)S(1)} collective-permute-done((f32[16,256]{1,0:T(8,128)S(1)}, f32[16,256]{1,0:T(8,128)S(1)}, u32[]{:S(2)}, u32[]{:S(2)}) %collective-permute-start.6) | collective-permute-done | bytes 16416 | tf_op jit(solution)/shard_map/ppermute | solution.py:604
  18.0 0.0 collective-permute-done.4.got_even
  18.0 2.2 %collective-permute-done.5.got_odd = f32[72,256]{1,0:T(8,128)S(1)} collective-permute-done((f32[72,256]{1,0:T(8,128)S(1)}, f32[72,256]{1,0:T(8,128)S(1)}, u32[]{:S(2)}, u32[]{:S(2)}) %collective-permute-start.5) | collective-permute-done | bytes 73760 | tf_op jit(solution)/shard_map/ppermute | solution.py:603
  20.2 1.4 %shard_map.81 = (f32[16,16,256]{2,1,0:T(8,128)}, f32[16,16,256]{2,1,0:T(8,128)}) custom-call(s32[16,256]{1,0:T(8,128)S(1)} %get-tuple-element.35.depth, f32[15,16,256]{2,1,0:T(8,128)S(1)} %get-tuple-element.36.links, f32[16,16,256]{2,1,0:T(8,128)S(1)} %get-tuple-element.37.inverse, f32[16,256]{1,0:T(8,128)S(1)} %get-tuple-element.38.joint, ...), custom_call_target="tpu_custom_call" | custom-call | tf_op jit(solution)/shard_map/pallas_call | solution.py:670
Async XLA Ops:
  2.3 10.1 %collective-permute-start = (f32[88,256]{1,0:T(8,128)S(1)}, f32[88,256]{1,0:T(8,128)S(1)}, u32[]{:S(2)}, u32[]{:S(2)}) collective-permute-start(f32[88,256]{1,0:T(8,128)S(1)} %get-tuple-element.49), channel_id=1, source_target_pairs={{0,8},{8,0},{16,24},{24,16},{1,9},{9,1},{17,25},{25,17},{2,10},{10... | collective-permute-start | bytes 270344 | tf_op jit(solution)/shard_map/ppermute | solution.py:602
  2.9 9.5 %collective-permute-start.1 = (f32[88,256]{1,0:T(8,128)S(1)}, f32[88,256]{1,0:T(8,128)S(1)}, u32[]{:S(2)}, u32[]{:S(2)}) collective-permute-start(f32[88,256]{1,0:T(8,128)S(1)} %get-tuple-element.50), channel_id=1, source_target_pairs={{8,16},{16,8},{9,17},{17,9},{10,18},{18,10},{11,19},{19,11},{12,20... | collective-permute-start | bytes 270344 | tf_op jit(solution)/shard_map/ppermute | solution.py:603
  7.3 5.1 %collective-permute-start.2 = (f32[16,384]{1,0:T(8,128)S(1)}, f32[16,384]{1,0:T(8,128)S(1)}, u32[]{:S(2)}, u32[]{:S(2)}) collective-permute-start(f32[16,384]{1,0:T(8,128)S(1)} %get-tuple-element.51), channel_id=1, source_target_pairs={{1,2},{2,1},{3,4},{4,3},{5,6},{6,5},{9,10},{10,9},{11,12},{12,11},... | collective-permute-start | bytes 73736 | tf_op jit(solution)/shard_map/ppermute | solution.py:604
  9.2 3.2 %collective-permute-start.3 = (f32[16,384]{1,0:T(8,128)S(1)}, f32[16,384]{1,0:T(8,128)S(1)}, u32[]{:S(2)}, u32[]{:S(2)}) collective-permute-start(f32[16,384]{1,0:T(8,128)S(1)} %get-tuple-element.52), channel_id=1, source_target_pairs={{0,1},{1,0},{2,3},{3,2},{4,5},{5,4},{6,7},{7,6},{8,9},{9,8},{10,11... | collective-permute-start | bytes 73736 | tf_op jit(solution)/shard_map/ppermute | solution.py:604
  13.0 5.0 %collective-permute-start.4 = (f32[72,256]{1,0:T(8,128)S(1)}, f32[72,256]{1,0:T(8,128)S(1)}, u32[]{:S(2)}, u32[]{:S(2)}) collective-permute-start(f32[72,256]{1,0:T(8,128)S(1)} %get-tuple-element.66), channel_id=1, source_target_pairs={{0,8},{8,0},{16,24},{24,16},{1,9},{9,1},{17,25},{25,17},{2,10},{10... | collective-permute-start | bytes 221192 | tf_op jit(solution)/shard_map/ppermute | solution.py:602
  13.1 7.1 %collective-permute-start.5 = (f32[72,256]{1,0:T(8,128)S(1)}, f32[72,256]{1,0:T(8,128)S(1)}, u32[]{:S(2)}, u32[]{:S(2)}) collective-permute-start(f32[72,256]{1,0:T(8,128)S(1)} %get-tuple-element.67), channel_id=1, source_target_pairs={{8,16},{16,8},{9,17},{17,9},{10,18},{18,10},{11,19},{19,11},{12,20... | collective-permute-start | bytes 221192 | tf_op jit(solution)/shard_map/ppermute | solution.py:603
  16.7 1.2 %collective-permute-start.6 = (f32[16,256]{1,0:T(8,128)S(1)}, f32[16,256]{1,0:T(8,128)S(1)}, u32[]{:S(2)}, u32[]{:S(2)}) collective-permute-start(f32[16,256]{1,0:T(8,128)S(1)} %get-tuple-element.65.own), channel_id=1, source_target_pairs={{0,1},{1,0},{2,3},{3,2},{4,5},{5,4},{6,7},{7,6},{8,9},{9,8},{10,11... | collective-permute-start | bytes 49160 | tf_op jit(solution)/shard_map/ppermute | solution.py:604

commit v8 on v7

--- a/solution.py
+++ b/solution.py
@@ -94,18 +94,23 @@
     return value
 
 
-def pack_rows(k, levels, c, h, speed, open_y, up, down):
+def edge_rows(c, h, speed, open_y):
     size = c.shape[0]
     last = slice(size - sublanes, size)
     first = slice(0, sublanes)
     g_last = jnp.where(open_y[last], speed[last] * (h[last] - turned(h[last], 1, 0)), 0.0)
     g_first = jnp.where(open_y[first], speed[first] * (h[first] - turned(h[first], 1, 0)), 0.0)
-    above = (c[size - 2 : size - 1], c[size - 1 :], h[size - 1 :], g_last[sublanes - 1 :])
-    below = (c[0:1], c[1:2], h[0:1], g_first[1:2])
-    for item in range(4):
-        at = item * levels + k
-        up[at : at + 1, :] = above[item]
-        down[at : at + 1, :] = below[item]
+    end = size - 1
+    up = [c[end - 1 : end], c[end:], h[end:], g_last[sublanes - 1 :]]
+    return up, [c[0:1], c[1:2], h[0:1], g_first[1:2]]
+
+
+def store_rows(found, ref):
+    levels = len(found)
+    for item in range(len(found[0])):
+        for k in range(0, levels, sublanes):
+            tile = jnp.concatenate([found[i][item] for i in range(k, k + sublanes)], axis=0)
+            ref[item * levels + k : item * levels + k + sublanes, :] = tile
 
 
 def inward(levels, scaled, links, inverse, joint, passed):
@@ -161,6 +166,14 @@
         next(down, None)
     link = links[middle - 1]
     return 1.0 / (1.0 - (link * inverse[middle - 1]) * (link * inverse[middle]))
+
+
+class Either:
+    def __init__(self, flag, first, second):
+        self.flag, self.first, self.second = flag, first, second
+
+    def __getitem__(self, where):
+        return jnp.where(self.flag, self.first[where], self.second[where])
 
 
 def choose(flag, ref_true, ref_false, into):
@@ -199,6 +212,7 @@
     for copy in copies[3:]:
         copy.wait()
     packed = [jnp.zeros((rows, lanes), jnp.float32)] * 5
+    rows_up, rows_down, rows_beside = {}, {}, {}
     for k, current in outward(levels, ends, links, inverse, passed):
         h = jnp.where(k < deep, current, 0.0)
         weight[k] = h
@@ -208,11 +222,12 @@
         items = (c, h, speed_x, speed_y) + ((mixing[k],) if k < levels - 1 else ())
         ahead = (0, slot // 2, 0, slot // 2, slot // 2)
         packed[: len(items)] = [pack_columns(k, *each) for each in zip(items, packed, ahead)]
-        pack_rows(k, levels, c, h, speed_y, k < shallow_y, up, down)
-        at = 4 * levels + k
-        down[at : at + 1, :] = speed_y[0:1]
-        up[at : at + 1, :] = speed_y[rows - 1 :]
-        beside[k : k + 1, :] = speed_y[1:2]
+        rows_up[k], rows_down[k] = edge_rows(c, h, speed_y, k < shallow_y)
+        rows_up[k].append(speed_y[rows - 1 :])
+        rows_down[k].append(speed_y[0:1])
+        rows_beside[k] = [speed_y[1:2]]
+    for found, ref in ((rows_up, up), (rows_down, down), (rows_beside, beside)):
+        store_rows(found, ref)
     start = lax.rem(index((rows, lanes), 1), slot) < slot // 2
     twice = ((packed[0], packed[1]), (packed[2], packed[3]), (packed_depth, packed[4]))
     first = jnp.concatenate([jnp.where(start, a, b) for a, b in twice], axis=1)
@@ -492,24 +507,41 @@
     return packed_state, packed_weight
 
 
-def first_kernel(
-    north, depth, links, inverse, joint, weight, forward, linear, own_up, own_down, beside, own,
-    got_even, got_odd, got_chip, got_core,
-    state, weight_next, pay_even, pay_odd, up, down,
-    passed, scaled, lower, upper, border,
+def outer_rows(value):
+    axis = value.ndim - 2
+    size = value.shape[axis]
+    first = lax.slice_in_dim(value, 0, sublanes, axis=axis)
+    last = lax.slice_in_dim(value, size - sublanes, size, axis=axis)
+    return jnp.where(index(first.shape, axis) < sublanes // 2, first, last)
+
+
+def first_inner_kernel(
+    c_ref, h_ref, east, north, depth, links, inverse, joint,
+    forward, linear, north_rows, depth_rows, links_rows, inverse_rows, joint_rows, h_rows, forward_rows, linear_rows,
 ):
-    levels, rows, columns = weight.shape
-    even_y, even_x = parities()
-    choose(even_y, got_odd, got_even, lower)
-    choose(even_y, got_even, got_odd, upper)
-    before, after = take(even_x, got_core[...], got_chip[...])
+    inner_kernel(c_ref, h_ref, east, north, depth, forward, linear)
+    depth_rows[...] = outer_rows(depth[...])
+    joint_rows[...] = outer_rows(joint[...])
+    pairs_of = ((north, north_rows), (links, links_rows), (inverse, inverse_rows), (h_ref, h_rows))
+    for whole, rows in pairs_of + ((forward, forward_rows), (linear, linear_rows)):
+        for k in range(whole.shape[0]):
+            rows[k] = outer_rows(whole[k])
+
+
+def first_step(
+    depth, links, inverse, joint, weight, forward, linear, own_up, own_down, beside, sides, got, state, passed, scaled, border
+):
+    levels = weight.shape[0]
+    even_y, _ = parities()
+    got_even, got_odd = got
+    lower, upper = Either(even_y, got_odd, got_even), Either(even_y, got_even, got_odd)
     deep = depth[...]
     depth_float = deep.astype(jnp.float32)
     at = 5 * levels
     speeds = (rows_of(own_down, 4, levels), beside[...], rows_of(own_up, 4, levels), rows_of(upper, 4, levels))
     deeps = (lower[at : at + 1, :], upper[at : at + 1, :])
     borders_y(levels, lower, upper, own_up, own_down, speeds, depth_float, deeps, border)
-    packed = borders_x(four_items(before), four_items(after), own_items(own))
+    packed = borders_x(*sides)
     for k in range(levels):
         scaled[k] = with_rows(k, levels, forward[k], border, 0)
         state[k] = with_rows(k, levels, linear[k], border, 4)
@@ -520,16 +552,55 @@
     for k, current in outward(levels, ends, links, inverse, passed):
         scaled[k] = (state[k] - (2.0 * uptake) * current * weight[k]) * inverse[k]
         state[k] = current
-    ends = inward(levels, lambda k: scaled[k], links, inverse, joint[...], passed)
+    return inward(levels, lambda k: scaled[k], links, inverse, joint[...], passed)
+
+
+def sides_of(got_chip, got_core, own):
+    _, even = parities()
+    before, after = take(even, got_core[...], got_chip[...])
+    return four_items(before), four_items(after), own_items(own)
+
+
+def edge_kernel(
+    north, depth, links, inverse, joint, weight, forward, linear, own_up, own_down, beside, own,
+    got_even, got_odd, got_chip, got_core,
+    pay_even, pay_odd, up, down,
+    state, passed, scaled, border,
+):
+    levels = weight.shape[0]
+    even_y, _ = parities()
+    sides = [[outer_rows(item) for item in side] for side in sides_of(got_chip, got_core, own)]
+    deep = depth[...]
+    ends = first_step(
+        depth, links, inverse, joint, weight, forward, linear, own_up, own_down, beside,
+        sides, (got_even, got_odd), state, passed, scaled, border,
+    )
     shallow_y = jnp.minimum(deep, turned(deep, 1, 0))
+    rows_up, rows_down = {}, {}
     for k, current in outward(levels, ends, links, inverse, passed):
         h = jnp.where(k < deep, current, 0.0)
-        weight_next[k] = h
-        c = state[k]
-        pack_rows(k, levels, c, h, north[k] * (1.0 / 12.0), k < shallow_y, up, down)
+        rows_up[k], rows_down[k] = edge_rows(state[k], h, north[k] * (1.0 / 12.0), k < shallow_y)
+    store_rows(rows_up, up)
+    store_rows(rows_down, down)
     strip_rows(levels, got_chip[...], up, down)
     choose(even_y, up, down, pay_even)
     choose(even_y, down, up, pay_odd)
+
+
+def first_kernel(
+    depth, links, inverse, joint, weight, forward, linear, own_up, own_down, beside, own,
+    got_even, got_odd, got_chip, got_core,
+    state, weight_next,
+    passed, scaled, border,
+):
+    levels = weight.shape[0]
+    ends = first_step(
+        depth, links, inverse, joint, weight, forward, linear, own_up, own_down, beside,
+        sides_of(got_chip, got_core, own), (got_even, got_odd), state, passed, scaled, border,
+    )
+    deep = depth[...]
+    for k, current in outward(levels, ends, links, inverse, passed):
+        weight_next[k] = jnp.where(k < deep, current, 0.0)
 
 
 def second_kernel(
@@ -537,7 +608,7 @@
     own_up, own_down, own, first_up, first_down, beside, first_own,
     got1_even, got1_odd, got1_chip, got1_core, got_even, got_odd, got_core,
     final_far, adjoint_far,
-    final, adjoint, passed, scaled, lower, upper, border, sent,
+    final, adjoint, passed, scaled, border, sent,
 ):
     copies = []
 
@@ -548,8 +619,7 @@
 
     levels, rows, columns = forward.shape
     even_y, even_x = parities()
-    choose(even_y, got_odd, got_even, lower)
-    choose(even_y, got_even, got_odd, upper)
+    lower, upper = Either(even_y, got_odd, got_even), Either(even_y, got_even, got_odd)
     before1, after1 = take(even_x, got1_core[...], got1_chip[...])
     factors = (strip_links, strip_inverse, strip_joint[...])
     strip = strip_states(levels, strip_values, base, factors, strip_weight, lower, upper)
@@ -557,11 +627,9 @@
     deep = depth[...]
     depth_float = deep.astype(jnp.float32)
     at = 5 * levels
-    deeps = (
-        jnp.where(even_y, got1_odd[at : at + 1, :], got1_even[at : at + 1, :]),
-        jnp.where(even_y, got1_even[at : at + 1, :], got1_odd[at : at + 1, :]),
-    )
-    speed = jnp.where(even_y, rows_of(got1_even, 4, levels), rows_of(got1_odd, 4, levels))
+    lower1, upper1 = Either(even_y, got1_odd, got1_even), Either(even_y, got1_even, got1_odd)
+    deeps = (lower1[at : at + 1, :], upper1[at : at + 1, :])
+    speed = rows_of(upper1, 4, levels)
     speeds = (rows_of(first_down, 4, levels), beside[...], rows_of(first_up, 4, levels), speed)
     borders_y(levels, lower, upper, own_up, own_down, speeds, depth_float, deeps, border)
 
@@ -646,15 +714,29 @@
     inner = pl.CostEstimate(flops=80 * cells, bytes_accessed=24 * cells, transcendentals=0)
 
     got1 = exchange(pay_even, pay_odd, pay_chip, pay_core)
-    parts = pl.pallas_call(inner_kernel, out_shape=(field, field), compiler_params=params, cost_estimate=inner)(
-        tracer, weight, east_speed, north_speed, depth_levels
-    )
-    state, weight_next, pay_even, pay_odd, up2, down2 = pl.pallas_call(
+    tile = lambda *shape, kind=f32: jax.ShapeDtypeStruct(shape[:-1] + (sublanes, shape[-1]), kind)
+    rows_shape = tile(levels, columns)
+    outer_shapes = (rows_shape, tile(columns, kind=depth_levels.dtype), tile(levels - 1, columns), rows_shape, tile(columns))
+    forward, linear, *outers = pl.pallas_call(
+        first_inner_kernel,
+        out_shape=(field, field) + outer_shapes + (rows_shape,) * 3,
+        compiler_params=params,
+        cost_estimate=inner,
+    )(tracer, weight, east_speed, north_speed, depth_levels, *factors)
+    small = pltpu.VMEM(rows_shape.shape, f32)
+    pay_even, pay_odd, up2, down2 = pl.pallas_call(
+        edge_kernel,
+        out_shape=(lines(second_size),) * 4,
+        scratch_shapes=[small, small, small, space(border_size)],
+        compiler_params=params,
+    )(*outers, up, down, beside, outer, *got1)
+    state, weight_next = pl.pallas_call(
         first_kernel,
-        out_shape=(field, field) + (lines(second_size),) * 4,
-        scratch_shapes=[block, block, space(first_size), space(first_size), space(border_size)],
+        out_shape=(field, field),
+        scratch_shapes=[block, block, space(border_size)],
         compiler_params=params,
-    )(north_speed, depth_levels, *factors, weight, *parts, up, down, beside, outer, *got1)
+        cost_estimate=inner,
+    )(depth_levels, *factors, weight, forward, linear, up, down, beside, outer, *got1)
 
     def strips(count):
         return jax.ShapeDtypeStruct((count, rows, lanes), f32)
@@ -671,7 +753,7 @@
         second_kernel,
         out_specs=[far] * 2,
         out_shape=(field, field),
-        scratch_shapes=[block] * 4 + [space(second_size), space(second_size), space(border_size), sends],
+        scratch_shapes=[block] * 4 + [space(border_size), sends],
         compiler_params=params,
     )(depth_levels, *factors, *parts, up2, down2, outer2, up, down, beside, outer, *got1, *got2)
     return final, adjoint

time: 21.9 us -> 21.8 us (level)
  waiting for transfers between devices: 3.89 us -> 3.29 us
  Pallas kernels: 5.89 us -> 6.38 us
    ppermute x2, waiting for transfers between devices: 2.24 us -> 1.74 us  [exchange(): got_odd = lax.ppermute(pay_odd, 'group', pairs('group', 1))]
    pallas_call x2 -> x3, Pallas kernels: 1.56 us -> 2.02 us  [the longest x1 1.09 us: shards(): pl.pallas_call(first_inner_kernel, out_shape=(field, field) + outer_shape...]
  transfers between devices with their start and end apart: 7 -> 7, of which waited for: 3 -> 3; matrix products, arithmetic and copies ran while one was open for 0% -> 0% of each run, Pallas kernels for 10% -> 13%
where the time goes in v8:
time: 21.8 us; the launch traced here: 21.5 us
  starting transfers between devices  11.1 us (51%)
  Pallas kernels  6.38 us (29%)
  waiting for transfers between devices  3.29 us (15%)
  between operations  0.71 us (3%)
    ppermute x2, starting transfers between devices, exchange(): got_odd = lax.ppermute(pay_odd, 'group', pairs('group', 1))  6.73 us
    ppermute x3, starting transfers between devices, exchange(): lax.ppermute(each, 'tile', pairs('tile', len(pay) - 1 - i))  3.74 us
    ppermute x2, waiting for transfers between devices, exchange(): got_odd = lax.ppermute(pay_odd, 'group', pairs('group', 1))  1.74 us
    pallas_call x1, Pallas kernels, shards(): pl.pallas_call(factor_kernel, in_specs=[far] * 6, out_shape=near + (links...  1.71 us
    ppermute x3, waiting for transfers between devices, exchange(): lax.ppermute(each, 'tile', pairs('tile', len(pay) - 1 - i))  1.55 us
    pallas_call x1, Pallas kernels, shards(): pl.pallas_call(second_kernel, out_specs=[far] * 2, out_shape=(field, fiel...  1.39 us
    pallas_call x1, Pallas kernels, shards(): pl.pallas_call(second_inner_kernel, out_shape=(field, field, tiles(2), st...  1.26 us
    pallas_call x1, Pallas kernels, shards(): pl.pallas_call(first_inner_kernel, out_shape=(field, field) + outer_shape...  1.09 us
  transfers between devices with their start and end apart: 7, of which 3 were waited for; matrix products, arithmetic and copies ran while one was open for 0% of the time, Pallas kernels for 13%

profile of v8, /device:TPU:10, one launch (start us, length us, event | category | flops | bytes accessed | tf_op | source)
XLA Modules:
  0.0 21.5 jit_solution(3461146915148248172)
XLA Ops:
  0.6 1.7 %shard_map.77 = (f32[16,16,256]{2,1,0:T(8,128)S(1)}, f32[16,16,256]{2,1,0:T(8,128)S(1)}, f32[16,16,256]{2,1,0:T(8,128)S(1)}, s32[16,256]{1,0:T(8,128)S(1)}, f32[...) custom-call(f32[16,16,256]{2,1,0:T(8,128)} %tracer_far.1, ...), custom_call_target="tpu_custom_call" | custom-call | tf_op jit(solution)/shard_map/pallas_call | solution.py:702
  2.3 0.6 %collective-permute-start = (f32[88,256]{1,0:T(8,128)S(1)}, f32[88,256]{1,0:T(8,128)S(1)}, u32[]{:S(2)}, u32[]{:S(2)}) collective-permute-start(f32[88,256]{1,0:T(8,128)S(1)} %get-tuple-element.57), channel_id=1, source_target_pairs={{0,8},{8,0},{16,24},{24,16},{1,9},{9,1},{17,25},{25,17},{2,10},{10... | collective-permute-start | bytes 270344 | tf_op jit(solution)/shard_map/ppermute | solution.py:670
  2.9 4.3 %collective-permute-start.1 = (f32[88,256]{1,0:T(8,128)S(1)}, f32[88,256]{1,0:T(8,128)S(1)}, u32[]{:S(2)}, u32[]{:S(2)}) collective-permute-start(f32[88,256]{1,0:T(8,128)S(1)} %get-tuple-element.58), channel_id=1, source_target_pairs={{8,16},{16,8},{9,17},{17,9},{10,18},{18,10},{11,19},{19,11},{12,20... | collective-permute-start | bytes 270344 | tf_op jit(solution)/shard_map/ppermute | solution.py:671
  7.3 1.9 %collective-permute-start.2 = (f32[16,384]{1,0:T(8,128)S(1)}, f32[16,384]{1,0:T(8,128)S(1)}, u32[]{:S(2)}, u32[]{:S(2)}) collective-permute-start(f32[16,384]{1,0:T(8,128)S(1)} %get-tuple-element.59), channel_id=1, source_target_pairs={{1,2},{2,1},{3,4},{4,3},{5,6},{6,5},{9,10},{10,9},{11,12},{12,11},... | collective-permute-start | bytes 73736 | tf_op jit(solution)/shard_map/ppermute | solution.py:672
  9.2 1.7 %collective-permute-start.3 = (f32[16,384]{1,0:T(8,128)S(1)}, f32[16,384]{1,0:T(8,128)S(1)}, u32[]{:S(2)}, u32[]{:S(2)}) collective-permute-start(f32[16,384]{1,0:T(8,128)S(1)} %get-tuple-element.60), channel_id=1, source_target_pairs={{0,1},{1,0},{2,3},{3,2},{4,5},{5,4},{6,7},{7,6},{8,9},{9,8},{10,11... | collective-permute-start | bytes 73736 | tf_op jit(solution)/shard_map/ppermute | solution.py:672
  11.0 1.1 %shard_map.78 = (f32[16,16,256]{2,1,0:T(8,128)S(1)}, f32[16,16,256]{2,1,0:T(8,128)S(1)}, f32[16,8,256]{2,1,0:T(8,128)S(1)}, s32[8,256]{1,0:T(8,128)S(1)}, f32[15...) custom-call(f32[16,16,256]{2,1,0:T(8,128)S(1)} %get-tuple-element.48, ...), custom_call_target="tpu_custom_call" | custom-call | flops 5242880 | bytes 1572864 | tf_op jit(solution)/shard_map/pallas_call | solution.py:720
  12.1 0.4 %collective-permute-done.2.got_chip.got1_chip = f32[16,384]{1,0:T(8,128)S(1)} collective-permute-done((f32[16,384]{1,0:T(8,128)S(1)}, f32[16,384]{1,0:T(8,128)S(1)}, u32[]{:S(2)}, u32[]{:S(2)}) %collective-permute-start.2) | collective-permute-done | bytes 24608 | tf_op jit(solution)/shard_map/ppermute | solution.py:672
  12.4 0.0 collective-permute-done.3.got_core.got1_core
  12.4 0.0 collective-permute-done.got_even.got1_even
  12.5 0.0 collective-permute-done.1.got_odd.got1_odd
  12.5 0.4 %shard_map.81 = (f32[72,256]{1,0:T(8,128)S(1)}, f32[72,256]{1,0:T(8,128)S(1)}, f32[72,256]{1,0:T(8,128)S(1)}, f32[72,256]{1,0:T(8,128)S(1)}) custom-call(f32[16,8,256]{2,1,0:T(8,128)S(1)} %get-tuple-element.71.north, s32[8,256]{1,0:T(8,128)S(1)} %get-tuple-element.72.depth, f32[15,8,256]{2,1,0:T(8,128)S(1)} %get-tuple-element.73.links, ...), custom_call_target="tpu_custom_call" | custom-call | tf_op jit(solution)/shard_map/pallas_call | solution.py:727
  12.9 0.1 collective-permute-start.4
  13.0 2.4 %collective-permute-start.5 = (f32[72,256]{1,0:T(8,128)S(1)}, f32[72,256]{1,0:T(8,128)S(1)}, u32[]{:S(2)}, u32[]{:S(2)}) collective-permute-start(f32[72,256]{1,0:T(8,128)S(1)} %get-tuple-element.83), channel_id=1, source_target_pairs={{8,16},{16,8},{9,17},{17,9},{10,18},{18,10},{11,19},{19,11},{12,20... | collective-permute-start | bytes 221192 | tf_op jit(solution)/shard_map/ppermute | solution.py:671
  15.4 0.5 %shard_map.79 = (f32[16,16,256]{2,1,0:T(8,128)S(1)}, f32[16,16,256]{2,1,0:T(8,128)S(1)}) custom-call(s32[16,256]{1,0:T(8,128)S(1)} %get-tuple-element.43.depth, f32[15,16,256]{2,1,0:T(8,128)S(1)} %get-tuple-element.44.links, f32[16,16,256]{2,1,0:T(8,128)S(1)} %get-tuple-element.45.inverse, f32[16,256]{1,0:T(8,128)S(1)} %get-tuple-element.46.joint, ...), custom_call_target="tpu_custom_call" | custom-call | flops 5242880 | bytes 1572864 | tf_op jit(solution)/shard_map/pallas_call | solution.py:733
  15.9 1.3 %shard_map.80 = (f32[16,16,256]{2,1,0:T(8,128)S(1)}, f32[16,16,256]{2,1,0:T(8,128)S(1)}, f32[16,256]{1,0:T(8,128)S(1)}, f32[15,16,128]{2,1,0:T(8,128)S(1)}, f32[...) custom-call(f32[16,16,256]{2,1,0:T(8,128)S(1)} %get-tuple-element.61, ...), custom_call_target="tpu_custom_call" | custom-call | flops 5242880 | bytes 1572864 | tf_op jit(solution)/shard_map/pallas_call | solution.py:744
  17.1 0.1 collective-permute-start.6
  17.2 1.2 %collective-permute-done.6.got_core = f32[16,256]{1,0:T(8,128)S(1)} collective-permute-done((f32[16,256]{1,0:T(8,128)S(1)}, f32[16,256]{1,0:T(8,128)S(1)}, u32[]{:S(2)}, u32[]{:S(2)}) %collective-permute-start.6) | collective-permute-done | bytes 16416 | tf_op jit(solution)/shard_map/ppermute | solution.py:672
  18.4 0.0 collective-permute-done.4.got_even
  18.4 1.7 %collective-permute-done.5.got_odd = f32[72,256]{1,0:T(8,128)S(1)} collective-permute-done((f32[72,256]{1,0:T(8,128)S(1)}, f32[72,256]{1,0:T(8,128)S(1)}, u32[]{:S(2)}, u32[]{:S(2)}) %collective-permute-start.5) | collective-permute-done | bytes 73760 | tf_op jit(solution)/shard_map/ppermute | solution.py:671
  20.1 1.4 %shard_map.82 = (f32[16,16,256]{2,1,0:T(8,128)}, f32[16,16,256]{2,1,0:T(8,128)}) custom-call(s32[16,256]{1,0:T(8,128)S(1)} %get-tuple-element.43.depth, f32[15,16,256]{2,1,0:T(8,128)S(1)} %get-tuple-element.44.links, f32[16,16,256]{2,1,0:T(8,128)S(1)} %get-tuple-element.45.inverse, f32[16,256]{1,0:T(8,128)S(1)} %get-tuple-element.46.joint, ...), custom_call_target="tpu_custom_call" | custom-call | tf_op jit(solution)/shard_map/pallas_call | solution.py:752
Async XLA Ops:
  2.3 10.1 %collective-permute-start = (f32[88,256]{1,0:T(8,128)S(1)}, f32[88,256]{1,0:T(8,128)S(1)}, u32[]{:S(2)}, u32[]{:S(2)}) collective-permute-start(f32[88,256]{1,0:T(8,128)S(1)} %get-tuple-element.57), channel_id=1, source_target_pairs={{0,8},{8,0},{16,24},{24,16},{1,9},{9,1},{17,25},{25,17},{2,10},{10... | collective-permute-start | bytes 270344 | tf_op jit(solution)/shard_map/ppermute | solution.py:670
  2.9 9.5 %collective-permute-start.1 = (f32[88,256]{1,0:T(8,128)S(1)}, f32[88,256]{1,0:T(8,128)S(1)}, u32[]{:S(2)}, u32[]{:S(2)}) collective-permute-start(f32[88,256]{1,0:T(8,128)S(1)} %get-tuple-element.58), channel_id=1, source_target_pairs={{8,16},{16,8},{9,17},{17,9},{10,18},{18,10},{11,19},{19,11},{12,20... | collective-permute-start | bytes 270344 | tf_op jit(solution)/shard_map/ppermute | solution.py:671
  7.3 5.1 %collective-permute-start.2 = (f32[16,384]{1,0:T(8,128)S(1)}, f32[16,384]{1,0:T(8,128)S(1)}, u32[]{:S(2)}, u32[]{:S(2)}) collective-permute-start(f32[16,384]{1,0:T(8,128)S(1)} %get-tuple-element.59), channel_id=1, source_target_pairs={{1,2},{2,1},{3,4},{4,3},{5,6},{6,5},{9,10},{10,9},{11,12},{12,11},... | collective-permute-start | bytes 73736 | tf_op jit(solution)/shard_map/ppermute | solution.py:672
  9.2 3.2 %collective-permute-start.3 = (f32[16,384]{1,0:T(8,128)S(1)}, f32[16,384]{1,0:T(8,128)S(1)}, u32[]{:S(2)}, u32[]{:S(2)}) collective-permute-start(f32[16,384]{1,0:T(8,128)S(1)} %get-tuple-element.60), channel_id=1, source_target_pairs={{0,1},{1,0},{2,3},{3,2},{4,5},{5,4},{6,7},{7,6},{8,9},{9,8},{10,11... | collective-permute-start | bytes 73736 | tf_op jit(solution)/shard_map/ppermute | solution.py:672
  12.9 5.5 %collective-permute-start.4 = (f32[72,256]{1,0:T(8,128)S(1)}, f32[72,256]{1,0:T(8,128)S(1)}, u32[]{:S(2)}, u32[]{:S(2)}) collective-permute-start(f32[72,256]{1,0:T(8,128)S(1)} %get-tuple-element.82), channel_id=1, source_target_pairs={{0,8},{8,0},{16,24},{24,16},{1,9},{9,1},{17,25},{25,17},{2,10},{10... | collective-permute-start | bytes 221192 | tf_op jit(solution)/shard_map/ppermute | solution.py:670
  13.0 7.1 %collective-permute-start.5 = (f32[72,256]{1,0:T(8,128)S(1)}, f32[72,256]{1,0:T(8,128)S(1)}, u32[]{:S(2)}, u32[]{:S(2)}) collective-permute-start(f32[72,256]{1,0:T(8,128)S(1)} %get-tuple-element.83), channel_id=1, source_target_pairs={{8,16},{16,8},{9,17},{17,9},{10,18},{18,10},{11,19},{19,11},{12,20... | collective-permute-start | bytes 221192 | tf_op jit(solution)/shard_map/ppermute | solution.py:671
  17.1 1.2 %collective-permute-start.6 = (f32[16,256]{1,0:T(8,128)S(1)}, f32[16,256]{1,0:T(8,128)S(1)}, u32[]{:S(2)}, u32[]{:S(2)}) collective-permute-start(f32[16,256]{1,0:T(8,128)S(1)} %get-tuple-element.81.own), channel_id=1, source_target_pairs={{0,1},{1,0},{2,3},{3,2},{4,5},{5,4},{6,7},{7,6},{8,9},{9,8},{10,11... | collective-permute-start | bytes 49160 | tf_op jit(solution)/shard_map/ppermute | solution.py:672

commit v9 on v8

--- a/solution.py
+++ b/solution.py
@@ -1,3 +1,5 @@
+import functools
+
 import jax
 import jax.numpy as jnp
 from jax import lax
@@ -166,6 +168,14 @@
         next(down, None)
     link = links[middle - 1]
     return 1.0 / (1.0 - (link * inverse[middle - 1]) * (link * inverse[middle]))
+
+
+class Half:
+    def __init__(self, ref, start):
+        self.ref, self.start = ref, start
+
+    def __getitem__(self, k):
+        return self.ref[k, pl.ds(self.start, sublanes), :]
 
 
 class Either:
@@ -339,6 +349,18 @@
     return jnp.concatenate(tiles, axis=0)
 
 
+def with_half_rows(k, levels, value, border, item, is_last):
+    row = index(value.shape, 0)
+
+    def line(which):
+        at = (item + which) * levels + k
+        return jnp.broadcast_to(border[at : at + 1, :], value.shape)
+
+    first = jnp.where(row == 0, line(0), jnp.where(row == 1, line(1), 0.0))
+    last = jnp.where(row == sublanes - 2, line(2), jnp.where(row == sublanes - 1, line(3), 0.0))
+    return value + jnp.where(is_last, last, first)
+
+
 def with_columns(k, value, packed):
     lead = turned(packed, -slot * k, 1)
     lane = index(lead.shape, 1)
@@ -419,13 +441,9 @@
 
 def second_inner_kernel(
     c_ref, h_ref, east, north, depth, tracer, outer, got_chip,
-    forward, linear, base, strip_links, strip_inverse, strip_joint, strip_weight, strip_values, outer_next,
+    forward, linear, base, strip_links, strip_inverse, strip_joint, strip_weight, strip_values,
 ):
     levels = c_ref.shape[0]
-    packed = [jnp.zeros((outer.shape[0], lanes), jnp.float32)] * 2
-    for k in range(levels):
-        packed = [pack_columns(k, *each) for each in zip((c_ref[k], h_ref[k]), packed)]
-    outer_next[...] = jnp.concatenate(packed, axis=1)
     inner_kernel(c_ref, h_ref, east, north, depth, tracer, forward, linear)
     _, even = parities()
     place, level = placed((outer.shape[0], lanes))
@@ -456,10 +474,12 @@
     strip_joint[...] = factorized(levels, strip_links, strip_inverse)
 
 
-def strip_states(levels, values, base, factors, weights, lower, upper):
+def strip_states(levels, values, base, factors, weights, got, is_last):
     links, inverse, joint = factors
     c, h, deep, side = (item_of(values, i) for i in range(4))
     place, level = placed(c.shape)
+    lower = upper = got
+    half = lambda value: jnp.where(is_last, value[-sublanes:], value[:sublanes])
     end = c.shape[0] - 1
 
     def line(ref, item):
@@ -481,11 +501,11 @@
     row = index((sublanes, lanes), 0)
 
     def bordered(value, rows):
-        tiles = split(value, 0)
-        tiles[0] = tiles[0] + jnp.where(row == 0, rows[0], jnp.where(row == 1, rows[1], 0.0))
-        tiles[-1] = tiles[-1] + jnp.where(row == sublanes - 2, rows[2], jnp.where(row == sublanes - 1, rows[3], 0.0))
-        return jnp.concatenate(tiles, axis=0)
-
+        first = jnp.where(row == 0, rows[0], jnp.where(row == 1, rows[1], 0.0))
+        last = jnp.where(row == sublanes - 2, rows[2], jnp.where(row == sublanes - 1, rows[3], 0.0))
+        return half(value) + jnp.where(is_last, last, first)
+
+    deep, level = half(deep), level[:sublanes]
     right = jnp.where(level < deep, bordered(base[:, :lanes], added[:4]), 0.0)
     linear = bordered(base[:, lanes:], added[4:])
     right, linear = ([turned(value, -slot * k, 1) for k in range(levels)] for value in (right, linear))
@@ -498,7 +518,7 @@
 
     ends = inward(levels, scaled, links, inverse, joint, passed)
     weight = dict(outward(levels, ends, links, inverse, passed))
-    packed_state = packed_weight = jnp.zeros(c.shape, jnp.float32)
+    packed_state = packed_weight = jnp.zeros(deep.shape, jnp.float32)
     for k in range(levels):
         here = level == float(k)
         packed_state = jnp.where(here, turned(state[k], slot * k, 1), packed_state)
@@ -590,7 +610,7 @@
 def first_kernel(
     depth, links, inverse, joint, weight, forward, linear, own_up, own_down, beside, own,
     got_even, got_odd, got_chip, got_core,
-    state, weight_next,
+    state, weight_next, outer_next,
     passed, scaled, border,
 ):
     levels = weight.shape[0]
@@ -599,31 +619,40 @@
         sides_of(got_chip, got_core, own), (got_even, got_odd), state, passed, scaled, border,
     )
     deep = depth[...]
+    packed = [jnp.zeros((deep.shape[0], lanes), jnp.float32)] * 2
     for k, current in outward(levels, ends, links, inverse, passed):
-        weight_next[k] = jnp.where(k < deep, current, 0.0)
+        h = jnp.where(k < deep, current, 0.0)
+        weight_next[k] = h
+        packed = [pack_columns(k, *each) for each in zip((state[k], h), packed)]
+    outer_next[...] = jnp.concatenate(packed, axis=1)
 
 
 def second_kernel(
+    on_odd,
     depth, links, inverse, joint, forward, linear, base, strip_links, strip_inverse, strip_joint, strip_weight, strip_values,
     own_up, own_down, own, first_up, first_down, beside, first_own,
-    got1_even, got1_odd, got1_chip, got1_core, got_even, got_odd, got_core,
-    final_far, adjoint_far,
-    final, adjoint, passed, scaled, border, sent,
+    got1_even, got1_odd, got1_chip, got1_core, got, got_core,
+    *rest,
 ):
+    final_far, adjoint_far, final, adjoint, passed, scaled, border, sent = rest[-8:]
     copies = []
+    even_y, even_x = parities()
+    is_last = even_y != on_odd
+    start = pl.multiple_of(jnp.where(is_last, sublanes, 0), sublanes)
 
     def send(near, far, part):
-        copy = pltpu.make_async_copy(near.at[part], far.at[part], sent.at[len(copies)])
+        copy = pltpu.make_async_copy(near.at[part], far.at[part, pl.ds(start, sublanes), :], sent.at[len(copies)])
         copy.start()
         copies.append(copy)
 
-    levels, rows, columns = forward.shape
-    even_y, even_x = parities()
-    lower, upper = Either(even_y, got_odd, got_even), Either(even_y, got_even, got_odd)
+    levels = forward.shape[0]
+    halves = lambda ref: Half(ref, start)
+    plane = lambda ref: ref[pl.ds(start, sublanes), :]
+    cut = lambda items: [jnp.where(is_last, item[-sublanes:], item[:sublanes]) for item in items]
     before1, after1 = take(even_x, got1_core[...], got1_chip[...])
-    factors = (strip_links, strip_inverse, strip_joint[...])
-    strip = strip_states(levels, strip_values, base, factors, strip_weight, lower, upper)
-    before, after = take(even_x, got_core[...], jnp.concatenate(strip, axis=1))
+    factors = (halves(strip_links), halves(strip_inverse), plane(strip_joint))
+    strip = strip_states(levels, strip_values, base, factors, halves(strip_weight), got, is_last)
+    before, after = take(even_x, plane(got_core), jnp.concatenate(strip, axis=1))
     deep = depth[...]
     depth_float = deep.astype(jnp.float32)
     at = 5 * levels
@@ -631,21 +660,23 @@
     deeps = (lower1[at : at + 1, :], upper1[at : at + 1, :])
     speed = rows_of(upper1, 4, levels)
     speeds = (rows_of(first_down, 4, levels), beside[...], rows_of(first_up, 4, levels), speed)
-    borders_y(levels, lower, upper, own_up, own_down, speeds, depth_float, deeps, border)
+    borders_y(levels, got, got, own_up, own_down, speeds, depth_float, deeps, border)
 
     pair = lambda value: [item_of(value, 0), item_of(value, 1)]
-    ends = (pair(before) + four_items(before1)[2:], pair(after) + four_items(after1)[2:])
-    mine = pair(own) + [item_of(first_own, 2), item_of(first_own, 3)]
+    ends = (pair(before) + cut(four_items(before1)[2:]), pair(after) + cut(four_items(after1)[2:]))
+    mine = cut(pair(own) + [item_of(first_own, 2), item_of(first_own, 3)])
+    deep = plane(depth)
+    forward, linear, links, inverse = (halves(ref) for ref in (forward, linear, links, inverse))
     packed = borders_x(*ends, mine)
     for k in range(levels):
-        adjoint[k] = with_rows(k, levels, linear[k], border, 4)
-        scaled[k] = with_rows(k, levels, forward[k], border, 0)
+        adjoint[k] = with_half_rows(k, levels, linear[k], border, 4, is_last)
+        scaled[k] = with_half_rows(k, levels, forward[k], border, 0, is_last)
     for k in range(levels):
         scaled[k] = jnp.where(k < deep, with_columns(k, scaled[k], packed[0]), 0.0) * inverse[k]
     for k in range(levels):
         adjoint[k] = with_columns(k, adjoint[k], packed[1])
     send(adjoint, adjoint_far, slice(0, levels))
-    ends = inward(levels, lambda k: scaled[k], links, inverse, joint[...], passed)
+    ends = inward(levels, lambda k: scaled[k], links, inverse, plane(joint), passed)
     middle = levels // 2
     quarter = middle // 2
     for k, current in outward(levels, ends, links, inverse, passed):
@@ -675,7 +706,7 @@
 
 def shards(tracer, east_speed, north_speed, mixing, depth_levels, sensitivity):
     levels, rows, columns = tracer.shape
-    assert levels * slot == lanes and rows % sublanes == 0 and columns % lanes == 0
+    assert levels * slot == lanes and rows == 2 * sublanes and columns % lanes == 0
     f32 = jnp.float32
     field = jax.ShapeDtypeStruct((levels, rows, columns), f32)
     first_size = 5 * levels + sublanes
@@ -730,9 +761,9 @@
         scratch_shapes=[small, small, small, space(border_size)],
         compiler_params=params,
     )(*outers, up, down, beside, outer, *got1)
-    state, weight_next = pl.pallas_call(
+    state, weight_next, outer2 = pl.pallas_call(
         first_kernel,
-        out_shape=(field, field),
+        out_shape=(field, field, tiles(2)),
         scratch_shapes=[block, block, space(border_size)],
         compiler_params=params,
         cost_estimate=inner,
@@ -741,21 +772,33 @@
     def strips(count):
         return jax.ShapeDtypeStruct((count, rows, lanes), f32)
 
-    *parts, outer2 = pl.pallas_call(
+    parts = pl.pallas_call(
         second_inner_kernel,
-        out_shape=(field, field, tiles(2), strips(levels - 1), strips(levels), tiles(1), strips(levels), tiles(4), tiles(2)),
+        out_shape=(field, field, tiles(2), strips(levels - 1), strips(levels), tiles(1), strips(levels), tiles(4)),
         compiler_params=params,
         cost_estimate=inner,
     )(state, weight_next, east_speed, north_speed, depth_levels, tracer, outer, got1[2])
     got2 = exchange(pay_even, pay_odd, outer2)
     sends = pltpu.SemaphoreType.DMA((4,))
-    final, adjoint = pl.pallas_call(
-        second_kernel,
-        out_specs=[far] * 2,
-        out_shape=(field, field),
-        scratch_shapes=[block] * 4 + [space(border_size), sends],
-        compiler_params=params,
-    )(depth_levels, *factors, *parts, up2, down2, outer2, up, down, beside, outer, *got1, *got2)
+    shared = (depth_levels, *factors, *parts, up2, down2, outer2, up, down, beside, outer, *got1)
+
+    def half(on_odd, got, *partial):
+        operands = shared + (got, got2[2]) + partial
+        count = len(operands)
+        whole = pl.BlockSpec(memory_space=pltpu.VMEM)
+        return pl.pallas_call(
+            functools.partial(second_kernel, on_odd),
+            in_specs=[whole] * (count - len(partial)) + [far] * len(partial),
+            out_specs=[far] * 2,
+            out_shape=(field, field),
+            scratch_shapes=[small] * 4 + [space(border_size), sends],
+            input_output_aliases={count - 2: 0, count - 1: 1} if partial else {},
+            compiler_params=params,
+            cost_estimate=inner,
+        )(*operands)
+
+    partial = half(False, got2[0])
+    final, adjoint = half(True, got2[1], *partial)
     return final, adjoint
 
 

time: 21.8 us -> 21.6 us (level)
  waiting for transfers between devices: 3.29 us -> 2.07 us
  Pallas kernels: 6.38 us -> 7.38 us
    ppermute x3, waiting for transfers between devices: 1.55 us -> 0.38 us  [exchange(): lax.ppermute(each, 'tile', pairs('tile', len(pay) - 1 - i))]
    pallas_call x2 -> x3, Pallas kernels: 1.87 us -> 2.94 us  [the longest x2 2.35 us: half(): pl.pallas_call(functools.partial(second_kernel, on_odd), in_specs=[whole]...]
  transfers between devices with their start and end apart: 7 -> 7, of which waited for: 3 -> 3; matrix products, arithmetic and copies ran while one was open for 0% -> 0% of each run, Pallas kernels for 13% -> 19%
where the time goes in v9:
time: 21.6 us; the launch traced here: 21.3 us
  starting transfers between devices  11.1 us (51%)
  Pallas kernels  7.38 us (34%)
  waiting for transfers between devices  2.07 us (10%)
  between operations  0.72 us (3%)
    ppermute x2, starting transfers between devices, exchange(): got_odd = lax.ppermute(pay_odd, 'group', pairs('group', 1))  6.73 us
    ppermute x3, starting transfers between devices, exchange(): lax.ppermute(each, 'tile', pairs('tile', len(pay) - 1 - i))  3.74 us
    pallas_call x2, Pallas kernels, half(): pl.pallas_call(functools.partial(second_kernel, on_odd), in_specs=[whole]...  2.35 us
    pallas_call x1, Pallas kernels, shards(): pl.pallas_call(factor_kernel, in_specs=[far] * 6, out_shape=near + (links...  1.71 us
    ppermute x2, waiting for transfers between devices, exchange(): got_odd = lax.ppermute(pay_odd, 'group', pairs('group', 1))  1.62 us
    pallas_call x1, Pallas kernels, shards(): pl.pallas_call(second_inner_kernel, out_shape=(field, field, tiles(2), st...  1.2 us
    pallas_call x1, Pallas kernels, shards(): pl.pallas_call(first_inner_kernel, out_shape=(field, field) + outer_shape...  1.09 us
    ppermute x2, starting transfers between devices, exchange(): got_even = lax.ppermute(pay_even, 'group', pairs('group', 0))  0.67 us
  transfers between devices with their start and end apart: 7, of which 3 were waited for; matrix products, arithmetic and copies ran while one was open for 0% of the time, Pallas kernels for 19%

profile of v9, /device:TPU:10, one launch (start us, length us, event | category | flops | bytes accessed | tf_op | source)
XLA Modules:
  0.0 21.3 jit_solution(13562812509524495262)
XLA Ops:
  0.6 1.7 %shard_map.77 = (f32[16,16,256]{2,1,0:T(8,128)S(1)}, f32[16,16,256]{2,1,0:T(8,128)S(1)}, f32[16,16,256]{2,1,0:T(8,128)S(1)}, s32[16,256]{1,0:T(8,128)S(1)}, f32[...) custom-call(f32[16,16,256]{2,1,0:T(8,128)} %tracer_far.1, ...), custom_call_target="tpu_custom_call" | custom-call | tf_op jit(solution)/shard_map/pallas_call | solution.py:733
  2.3 0.6 %collective-permute-start = (f32[88,256]{1,0:T(8,128)S(1)}, f32[88,256]{1,0:T(8,128)S(1)}, u32[]{:S(2)}, u32[]{:S(2)}) collective-permute-start(f32[88,256]{1,0:T(8,128)S(1)} %get-tuple-element.59), channel_id=1, source_target_pairs={{0,8},{8,0},{16,24},{24,16},{1,9},{9,1},{17,25},{25,17},{2,10},{10... | collective-permute-start | bytes 270344 | tf_op jit(solution)/shard_map/ppermute | solution.py:701
  2.9 4.3 %collective-permute-start.1 = (f32[88,256]{1,0:T(8,128)S(1)}, f32[88,256]{1,0:T(8,128)S(1)}, u32[]{:S(2)}, u32[]{:S(2)}) collective-permute-start(f32[88,256]{1,0:T(8,128)S(1)} %get-tuple-element.60), channel_id=1, source_target_pairs={{8,16},{16,8},{9,17},{17,9},{10,18},{18,10},{11,19},{19,11},{12,20... | collective-permute-start | bytes 270344 | tf_op jit(solution)/shard_map/ppermute | solution.py:702
  7.3 1.9 %collective-permute-start.2 = (f32[16,384]{1,0:T(8,128)S(1)}, f32[16,384]{1,0:T(8,128)S(1)}, u32[]{:S(2)}, u32[]{:S(2)}) collective-permute-start(f32[16,384]{1,0:T(8,128)S(1)} %get-tuple-element.61), channel_id=1, source_target_pairs={{1,2},{2,1},{3,4},{4,3},{5,6},{6,5},{9,10},{10,9},{11,12},{12,11},... | collective-permute-start | bytes 73736 | tf_op jit(solution)/shard_map/ppermute | solution.py:703
  9.2 1.7 %collective-permute-start.3 = (f32[16,384]{1,0:T(8,128)S(1)}, f32[16,384]{1,0:T(8,128)S(1)}, u32[]{:S(2)}, u32[]{:S(2)}) collective-permute-start(f32[16,384]{1,0:T(8,128)S(1)} %get-tuple-element.62), channel_id=1, source_target_pairs={{0,1},{1,0},{2,3},{3,2},{4,5},{5,4},{6,7},{7,6},{8,9},{9,8},{10,11... | collective-permute-start | bytes 73736 | tf_op jit(solution)/shard_map/ppermute | solution.py:703
  11.0 1.1 %shard_map.78 = (f32[16,16,256]{2,1,0:T(8,128)S(1)}, f32[16,16,256]{2,1,0:T(8,128)S(1)}, f32[16,8,256]{2,1,0:T(8,128)S(1)}, s32[8,256]{1,0:T(8,128)S(1)}, f32[15...) custom-call(f32[16,16,256]{2,1,0:T(8,128)S(1)} %get-tuple-element.50, ...), custom_call_target="tpu_custom_call" | custom-call | flops 5242880 | bytes 1572864 | tf_op jit(solution)/shard_map/pallas_call | solution.py:751
  12.1 0.4 %collective-permute-done.2.got_chip.got1_chip = f32[16,384]{1,0:T(8,128)S(1)} collective-permute-done((f32[16,384]{1,0:T(8,128)S(1)}, f32[16,384]{1,0:T(8,128)S(1)}, u32[]{:S(2)}, u32[]{:S(2)}) %collective-permute-start.2) | collective-permute-done | bytes 24608 | tf_op jit(solution)/shard_map/ppermute | solution.py:703
  12.4 0.0 collective-permute-done.3.got_core.got1_core
  12.4 0.0 collective-permute-done.got_even.got1_even
  12.5 0.0 collective-permute-done.1.got_odd.got1_odd
  12.5 0.4 %shard_map.81 = (f32[72,256]{1,0:T(8,128)S(1)}, f32[72,256]{1,0:T(8,128)S(1)}, f32[72,256]{1,0:T(8,128)S(1)}, f32[72,256]{1,0:T(8,128)S(1)}) custom-call(f32[16,8,256]{2,1,0:T(8,128)S(1)} %get-tuple-element.73.north, s32[8,256]{1,0:T(8,128)S(1)} %get-tuple-element.74.depth, f32[15,8,256]{2,1,0:T(8,128)S(1)} %get-tuple-element.75.links, ...), custom_call_target="tpu_custom_call" | custom-call | tf_op jit(solution)/shard_map/pallas_call | solution.py:758
  12.9 0.1 collective-permute-start.6
  13.0 2.4 %collective-permute-start.4 = (f32[72,256]{1,0:T(8,128)S(1)}, f32[72,256]{1,0:T(8,128)S(1)}, u32[]{:S(2)}, u32[]{:S(2)}) collective-permute-start(f32[72,256]{1,0:T(8,128)S(1)} %get-tuple-element.84), channel_id=1, source_target_pairs={{8,16},{16,8},{9,17},{17,9},{10,18},{18,10},{11,19},{19,11},{12,20... | collective-permute-start | bytes 221192 | tf_op jit(solution)/shard_map/ppermute | solution.py:702
  15.4 0.6 %shard_map.79 = (f32[16,16,256]{2,1,0:T(8,128)S(1)}, f32[16,16,256]{2,1,0:T(8,128)S(1)}, f32[16,256]{1,0:T(8,128)S(1)}) custom-call(s32[16,256]{1,0:T(8,128)S(1)} %get-tuple-element.45.depth, f32[15,16,256]{2,1,0:T(8,128)S(1)} %get-tuple-element.46.links, f32[16,16,256]{2,1,0:T(8,128)S(1)} %get-tuple-element.47.inverse, ...), custom_call_target="tpu_custom_call" | custom-call | flops 5242880 | bytes 1572864 | tf_op jit(solution)/shard_map/pallas_call | solution.py:764
  16.0 0.1 collective-permute-start.5
  16.1 1.2 %shard_map.80 = (f32[16,16,256]{2,1,0:T(8,128)S(1)}, f32[16,16,256]{2,1,0:T(8,128)S(1)}, f32[16,256]{1,0:T(8,128)S(1)}, f32[15,16,128]{2,1,0:T(8,128)S(1)}, f32[...) custom-call(f32[16,16,256]{2,1,0:T(8,128)S(1)} %get-tuple-element.63.c_ref, ...), custom_call_target="tpu_custom_call" | custom-call | flops 5242880 | bytes 1572864 | tf_op jit(solution)/shard_map/pallas_call | solution.py:775
  17.3 0.0 collective-permute-done.5.got_core
  17.3 0.1 collective-permute-done.6.got
  17.3 1.2 %shard_map.82 = (f32[16,16,256]{2,1,0:T(8,128)}, f32[16,16,256]{2,1,0:T(8,128)}) custom-call(s32[16,256]{1,0:T(8,128)S(1)} %get-tuple-element.45.depth, f32[15,16,256]{2,1,0:T(8,128)S(1)} %get-tuple-element.46.links, f32[16,16,256]{2,1,0:T(8,128)S(1)} %get-tuple-element.47.inverse, f32[16,256]{1,0:T(8,128)S(1)} %get-tuple-element.48.joint, ...), custom_call_target="tpu_custom_call" | custom-call | flops 5242880 | bytes 1572864 | tf_op jit(solution)/shard_map/pallas_call | solution.py:789
  18.5 1.6 %collective-permute-done.4.got = f32[72,256]{1,0:T(8,128)S(1)} collective-permute-done((f32[72,256]{1,0:T(8,128)S(1)}, f32[72,256]{1,0:T(8,128)S(1)}, u32[]{:S(2)}, u32[]{:S(2)}) %collective-permute-start.4) | collective-permute-done | bytes 73760 | tf_op jit(solution)/shard_map/ppermute | solution.py:702
  20.1 1.2 %shard_map.83 = (f32[16,16,256]{2,1,0:T(8,128)}, f32[16,16,256]{2,1,0:T(8,128)}) custom-call(s32[16,256]{1,0:T(8,128)S(1)} %get-tuple-element.45.depth, f32[15,16,256]{2,1,0:T(8,128)S(1)} %get-tuple-element.46.links, f32[16,16,256]{2,1,0:T(8,128)S(1)} %get-tuple-element.47.inverse, ...), custom_call_target="tpu_custom_call", output_to_operand_aliasing={{0}: (25, {}), {1}: (26, {})} | custom-call | flops 5242880 | bytes 1572864 | tf_op jit(solution)/shard_map/pallas_call | solution.py:789
Async XLA Ops:
  2.3 10.1 %collective-permute-start = (f32[88,256]{1,0:T(8,128)S(1)}, f32[88,256]{1,0:T(8,128)S(1)}, u32[]{:S(2)}, u32[]{:S(2)}) collective-permute-start(f32[88,256]{1,0:T(8,128)S(1)} %get-tuple-element.59), channel_id=1, source_target_pairs={{0,8},{8,0},{16,24},{24,16},{1,9},{9,1},{17,25},{25,17},{2,10},{10... | collective-permute-start | bytes 270344 | tf_op jit(solution)/shard_map/ppermute | solution.py:701
  2.9 9.5 %collective-permute-start.1 = (f32[88,256]{1,0:T(8,128)S(1)}, f32[88,256]{1,0:T(8,128)S(1)}, u32[]{:S(2)}, u32[]{:S(2)}) collective-permute-start(f32[88,256]{1,0:T(8,128)S(1)} %get-tuple-element.60), channel_id=1, source_target_pairs={{8,16},{16,8},{9,17},{17,9},{10,18},{18,10},{11,19},{19,11},{12,20... | collective-permute-start | bytes 270344 | tf_op jit(solution)/shard_map/ppermute | solution.py:702
  7.3 5.1 %collective-permute-start.2 = (f32[16,384]{1,0:T(8,128)S(1)}, f32[16,384]{1,0:T(8,128)S(1)}, u32[]{:S(2)}, u32[]{:S(2)}) collective-permute-start(f32[16,384]{1,0:T(8,128)S(1)} %get-tuple-element.61), channel_id=1, source_target_pairs={{1,2},{2,1},{3,4},{4,3},{5,6},{6,5},{9,10},{10,9},{11,12},{12,11},... | collective-permute-start | bytes 73736 | tf_op jit(solution)/shard_map/ppermute | solution.py:703
  9.2 3.2 %collective-permute-start.3 = (f32[16,384]{1,0:T(8,128)S(1)}, f32[16,384]{1,0:T(8,128)S(1)}, u32[]{:S(2)}, u32[]{:S(2)}) collective-permute-start(f32[16,384]{1,0:T(8,128)S(1)} %get-tuple-element.62), channel_id=1, source_target_pairs={{0,1},{1,0},{2,3},{3,2},{4,5},{5,4},{6,7},{7,6},{8,9},{9,8},{10,11... | collective-permute-start | bytes 73736 | tf_op jit(solution)/shard_map/ppermute | solution.py:703
  12.9 4.4 %collective-permute-start.6 = (f32[72,256]{1,0:T(8,128)S(1)}, f32[72,256]{1,0:T(8,128)S(1)}, u32[]{:S(2)}, u32[]{:S(2)}) collective-permute-start(f32[72,256]{1,0:T(8,128)S(1)} %get-tuple-element.85), channel_id=1, source_target_pairs={{0,8},{8,0},{16,24},{24,16},{1,9},{9,1},{17,25},{25,17},{2,10},{10... | collective-permute-start | bytes 221192 | tf_op jit(solution)/shard_map/ppermute | solution.py:701
  13.0 7.1 %collective-permute-start.4 = (f32[72,256]{1,0:T(8,128)S(1)}, f32[72,256]{1,0:T(8,128)S(1)}, u32[]{:S(2)}, u32[]{:S(2)}) collective-permute-start(f32[72,256]{1,0:T(8,128)S(1)} %get-tuple-element.84), channel_id=1, source_target_pairs={{8,16},{16,8},{9,17},{17,9},{10,18},{18,10},{11,19},{19,11},{12,20... | collective-permute-start | bytes 221192 | tf_op jit(solution)/shard_map/ppermute | solution.py:702
  16.0 1.3 %collective-permute-start.5 = (f32[16,256]{1,0:T(8,128)S(1)}, f32[16,256]{1,0:T(8,128)S(1)}, u32[]{:S(2)}, u32[]{:S(2)}) collective-permute-start(f32[16,256]{1,0:T(8,128)S(1)} %get-tuple-element.83.own), channel_id=1, source_target_pairs={{0,1},{1,0},{2,3},{3,2},{4,5},{5,4},{6,7},{7,6},{8,9},{9,8},{10,11... | collective-permute-start | bytes 49160 | tf_op jit(solution)/shard_map/ppermute | solution.py:703

commit v10 on v9

--- a/solution.py
+++ b/solution.py
@@ -287,12 +287,15 @@
     )
 
 
-def borders_y(levels, lower, upper, up, down, speeds, deep, deeps, border):
+def borders_y(levels, lower, upper, up, down, speeds, deep, deeps, border, is_last=None):
     end = deep.shape[0] - 1
     deeps = (deeps[0], deep[0:1], deep[1:2], deep[end - 1 : end], deep[end:], deeps[1])
     several = lambda ref, count: [rows_of(ref, i, levels) for i in range(count)]
     level = index((levels, deep.shape[1]), 0).astype(jnp.float32)
     values = border_rows(level, several(lower, 4), several(upper, 4), several(up, 3), several(down, 3), speeds, deeps)
+    if is_last is not None:
+        ends = ((values[0], values[2]), (values[1], values[3]), (values[4], values[6]), (values[5], values[7]))
+        values = [jnp.where(is_last, last, first) for first, last in ends]
     for item, value in enumerate(values):
         border[item * levels : (item + 1) * levels, :] = value
 
@@ -350,15 +353,13 @@
 
 
 def with_half_rows(k, levels, value, border, item, is_last):
-    row = index(value.shape, 0)
+    row = index(value.shape, 0) - jnp.where(is_last, sublanes - 2, 0)
 
     def line(which):
         at = (item + which) * levels + k
         return jnp.broadcast_to(border[at : at + 1, :], value.shape)
 
-    first = jnp.where(row == 0, line(0), jnp.where(row == 1, line(1), 0.0))
-    last = jnp.where(row == sublanes - 2, line(2), jnp.where(row == sublanes - 1, line(3), 0.0))
-    return value + jnp.where(is_last, last, first)
+    return value + jnp.where(row == 0, line(0), jnp.where(row == 1, line(1), 0.0))
 
 
 def with_columns(k, value, packed):
@@ -660,7 +661,7 @@
     deeps = (lower1[at : at + 1, :], upper1[at : at + 1, :])
     speed = rows_of(upper1, 4, levels)
     speeds = (rows_of(first_down, 4, levels), beside[...], rows_of(first_up, 4, levels), speed)
-    borders_y(levels, got, got, own_up, own_down, speeds, depth_float, deeps, border)
+    borders_y(levels, got, got, own_up, own_down, speeds, depth_float, deeps, border, is_last)
 
     pair = lambda value: [item_of(value, 0), item_of(value, 1)]
     ends = (pair(before) + cut(four_items(before1)[2:]), pair(after) + cut(four_items(after1)[2:]))
@@ -669,7 +670,7 @@
     forward, linear, links, inverse = (halves(ref) for ref in (forward, linear, links, inverse))
     packed = borders_x(*ends, mine)
     for k in range(levels):
-        adjoint[k] = with_half_rows(k, levels, linear[k], border, 4, is_last)
+        adjoint[k] = with_half_rows(k, levels, linear[k], border, 2, is_last)
         scaled[k] = with_half_rows(k, levels, forward[k], border, 0, is_last)
     for k in range(levels):
         scaled[k] = jnp.where(k < deep, with_columns(k, scaled[k], packed[0]), 0.0) * inverse[k]

time: 21.6 us -> 21.5 us (level)
  no operation moved by 1% of the time
where the time goes in v10:
time: 21.5 us; the launch traced here: 21.3 us
  starting transfers between devices  11.1 us (52%)
  Pallas kernels  7.31 us (34%)
  waiting for transfers between devices  2.1 us (10%)
  between operations  0.72 us (3%)
    ppermute x2, starting transfers between devices, exchange(): got_odd = lax.ppermute(pay_odd, 'group', pairs('group', 1))  6.73 us
    ppermute x3, starting transfers between devices, exchange(): lax.ppermute(each, 'tile', pairs('tile', len(pay) - 1 - i))  3.74 us
    pallas_call x2, Pallas kernels, half(): pl.pallas_call(functools.partial(second_kernel, on_odd), in_specs=[whole]...  2.28 us
    pallas_call x1, Pallas kernels, shards(): pl.pallas_call(factor_kernel, in_specs=[far] * 6, out_shape=near + (links...  1.71 us
    ppermute x2, waiting for transfers between devices, exchange(): got_odd = lax.ppermute(pay_odd, 'group', pairs('group', 1))  1.66 us
    pallas_call x1, Pallas kernels, shards(): pl.pallas_call(second_inner_kernel, out_shape=(field, field, tiles(2), st...  1.2 us
    pallas_call x1, Pallas kernels, shards(): pl.pallas_call(first_inner_kernel, out_shape=(field, field) + outer_shape...  1.09 us
    ppermute x2, starting transfers between devices, exchange(): got_even = lax.ppermute(pay_even, 'group', pairs('group', 0))  0.67 us
  transfers between devices with their start and end apart: 7, of which 3 were waited for; matrix products, arithmetic and copies ran while one was open for 0% of the time, Pallas kernels for 19%

profile of v10, /device:TPU:10, one launch (start us, length us, event | category | flops | bytes accessed | tf_op | source)
XLA Modules:
  0.0 21.3 jit_solution(9734020398266288734)
XLA Ops:
  0.6 1.7 %shard_map.77 = (f32[16,16,256]{2,1,0:T(8,128)S(1)}, f32[16,16,256]{2,1,0:T(8,128)S(1)}, f32[16,16,256]{2,1,0:T(8,128)S(1)}, s32[16,256]{1,0:T(8,128)S(1)}, f32[...) custom-call(f32[16,16,256]{2,1,0:T(8,128)} %tracer_far.1, ...), custom_call_target="tpu_custom_call" | custom-call | tf_op jit(solution)/shard_map/pallas_call | solution.py:734
  2.3 0.6 %collective-permute-start = (f32[88,256]{1,0:T(8,128)S(1)}, f32[88,256]{1,0:T(8,128)S(1)}, u32[]{:S(2)}, u32[]{:S(2)}) collective-permute-start(f32[88,256]{1,0:T(8,128)S(1)} %get-tuple-element.59), channel_id=1, source_target_pairs={{0,8},{8,0},{16,24},{24,16},{1,9},{9,1},{17,25},{25,17},{2,10},{10... | collective-permute-start | bytes 270344 | tf_op jit(solution)/shard_map/ppermute | solution.py:702
  2.9 4.3 %collective-permute-start.1 = (f32[88,256]{1,0:T(8,128)S(1)}, f32[88,256]{1,0:T(8,128)S(1)}, u32[]{:S(2)}, u32[]{:S(2)}) collective-permute-start(f32[88,256]{1,0:T(8,128)S(1)} %get-tuple-element.60), channel_id=1, source_target_pairs={{8,16},{16,8},{9,17},{17,9},{10,18},{18,10},{11,19},{19,11},{12,20... | collective-permute-start | bytes 270344 | tf_op jit(solution)/shard_map/ppermute | solution.py:703
  7.3 1.9 %collective-permute-start.2 = (f32[16,384]{1,0:T(8,128)S(1)}, f32[16,384]{1,0:T(8,128)S(1)}, u32[]{:S(2)}, u32[]{:S(2)}) collective-permute-start(f32[16,384]{1,0:T(8,128)S(1)} %get-tuple-element.61), channel_id=1, source_target_pairs={{1,2},{2,1},{3,4},{4,3},{5,6},{6,5},{9,10},{10,9},{11,12},{12,11},... | collective-permute-start | bytes 73736 | tf_op jit(solution)/shard_map/ppermute | solution.py:704
  9.2 1.7 %collective-permute-start.3 = (f32[16,384]{1,0:T(8,128)S(1)}, f32[16,384]{1,0:T(8,128)S(1)}, u32[]{:S(2)}, u32[]{:S(2)}) collective-permute-start(f32[16,384]{1,0:T(8,128)S(1)} %get-tuple-element.62), channel_id=1, source_target_pairs={{0,1},{1,0},{2,3},{3,2},{4,5},{5,4},{6,7},{7,6},{8,9},{9,8},{10,11... | collective-permute-start | bytes 73736 | tf_op jit(solution)/shard_map/ppermute | solution.py:704
  11.0 1.1 %shard_map.78 = (f32[16,16,256]{2,1,0:T(8,128)S(1)}, f32[16,16,256]{2,1,0:T(8,128)S(1)}, f32[16,8,256]{2,1,0:T(8,128)S(1)}, s32[8,256]{1,0:T(8,128)S(1)}, f32[15...) custom-call(f32[16,16,256]{2,1,0:T(8,128)S(1)} %get-tuple-element.50, ...), custom_call_target="tpu_custom_call" | custom-call | flops 5242880 | bytes 1572864 | tf_op jit(solution)/shard_map/pallas_call | solution.py:752
  12.1 0.4 %collective-permute-done.2.got_chip.got1_chip = f32[16,384]{1,0:T(8,128)S(1)} collective-permute-done((f32[16,384]{1,0:T(8,128)S(1)}, f32[16,384]{1,0:T(8,128)S(1)}, u32[]{:S(2)}, u32[]{:S(2)}) %collective-permute-start.2) | collective-permute-done | bytes 24608 | tf_op jit(solution)/shard_map/ppermute | solution.py:704
  12.4 0.0 collective-permute-done.3.got_core.got1_core
  12.4 0.0 collective-permute-done.got_even.got1_even
  12.5 0.0 collective-permute-done.1.got_odd.got1_odd
  12.5 0.4 %shard_map.81 = (f32[72,256]{1,0:T(8,128)S(1)}, f32[72,256]{1,0:T(8,128)S(1)}, f32[72,256]{1,0:T(8,128)S(1)}, f32[72,256]{1,0:T(8,128)S(1)}) custom-call(f32[16,8,256]{2,1,0:T(8,128)S(1)} %get-tuple-element.73.north, s32[8,256]{1,0:T(8,128)S(1)} %get-tuple-element.74.depth, f32[15,8,256]{2,1,0:T(8,128)S(1)} %get-tuple-element.75.links, ...), custom_call_target="tpu_custom_call" | custom-call | tf_op jit(solution)/shard_map/pallas_call | solution.py:759
  12.9 0.1 collective-permute-start.6
  13.0 2.4 %collective-permute-start.4 = (f32[72,256]{1,0:T(8,128)S(1)}, f32[72,256]{1,0:T(8,128)S(1)}, u32[]{:S(2)}, u32[]{:S(2)}) collective-permute-start(f32[72,256]{1,0:T(8,128)S(1)} %get-tuple-element.84), channel_id=1, source_target_pairs={{8,16},{16,8},{9,17},{17,9},{10,18},{18,10},{11,19},{19,11},{12,20... | collective-permute-start | bytes 221192 | tf_op jit(solution)/shard_map/ppermute | solution.py:703
  15.4 0.6 %shard_map.79 = (f32[16,16,256]{2,1,0:T(8,128)S(1)}, f32[16,16,256]{2,1,0:T(8,128)S(1)}, f32[16,256]{1,0:T(8,128)S(1)}) custom-call(s32[16,256]{1,0:T(8,128)S(1)} %get-tuple-element.45.depth, f32[15,16,256]{2,1,0:T(8,128)S(1)} %get-tuple-element.46.links, f32[16,16,256]{2,1,0:T(8,128)S(1)} %get-tuple-element.47.inverse, ...), custom_call_target="tpu_custom_call" | custom-call | flops 5242880 | bytes 1572864 | tf_op jit(solution)/shard_map/pallas_call | solution.py:765
  16.0 0.1 collective-permute-start.5
  16.1 1.2 %shard_map.80 = (f32[16,16,256]{2,1,0:T(8,128)S(1)}, f32[16,16,256]{2,1,0:T(8,128)S(1)}, f32[16,256]{1,0:T(8,128)S(1)}, f32[15,16,128]{2,1,0:T(8,128)S(1)}, f32[...) custom-call(f32[16,16,256]{2,1,0:T(8,128)S(1)} %get-tuple-element.63.c_ref, ...), custom_call_target="tpu_custom_call" | custom-call | flops 5242880 | bytes 1572864 | tf_op jit(solution)/shard_map/pallas_call | solution.py:776
  17.3 0.0 collective-permute-done.5.got_core
  17.3 0.1 collective-permute-done.6.got
  17.3 1.1 %shard_map.82 = (f32[16,16,256]{2,1,0:T(8,128)}, f32[16,16,256]{2,1,0:T(8,128)}) custom-call(s32[16,256]{1,0:T(8,128)S(1)} %get-tuple-element.45.depth, f32[15,16,256]{2,1,0:T(8,128)S(1)} %get-tuple-element.46.links, f32[16,16,256]{2,1,0:T(8,128)S(1)} %get-tuple-element.47.inverse, f32[16,256]{1,0:T(8,128)S(1)} %get-tuple-element.48.joint, ...), custom_call_target="tpu_custom_call" | custom-call | flops 5242880 | bytes 1572864 | tf_op jit(solution)/shard_map/pallas_call | solution.py:790
  18.5 1.7 %collective-permute-done.4.got = f32[72,256]{1,0:T(8,128)S(1)} collective-permute-done((f32[72,256]{1,0:T(8,128)S(1)}, f32[72,256]{1,0:T(8,128)S(1)}, u32[]{:S(2)}, u32[]{:S(2)}) %collective-permute-start.4) | collective-permute-done | bytes 73760 | tf_op jit(solution)/shard_map/ppermute | solution.py:703
  20.1 1.1 %shard_map.83 = (f32[16,16,256]{2,1,0:T(8,128)}, f32[16,16,256]{2,1,0:T(8,128)}) custom-call(s32[16,256]{1,0:T(8,128)S(1)} %get-tuple-element.45.depth, f32[15,16,256]{2,1,0:T(8,128)S(1)} %get-tuple-element.46.links, f32[16,16,256]{2,1,0:T(8,128)S(1)} %get-tuple-element.47.inverse, ...), custom_call_target="tpu_custom_call", output_to_operand_aliasing={{0}: (25, {}), {1}: (26, {})} | custom-call | flops 5242880 | bytes 1572864 | tf_op jit(solution)/shard_map/pallas_call | solution.py:790
Async XLA Ops:
  2.3 10.1 %collective-permute-start = (f32[88,256]{1,0:T(8,128)S(1)}, f32[88,256]{1,0:T(8,128)S(1)}, u32[]{:S(2)}, u32[]{:S(2)}) collective-permute-start(f32[88,256]{1,0:T(8,128)S(1)} %get-tuple-element.59), channel_id=1, source_target_pairs={{0,8},{8,0},{16,24},{24,16},{1,9},{9,1},{17,25},{25,17},{2,10},{10... | collective-permute-start | bytes 270344 | tf_op jit(solution)/shard_map/ppermute | solution.py:702
  2.9 9.5 %collective-permute-start.1 = (f32[88,256]{1,0:T(8,128)S(1)}, f32[88,256]{1,0:T(8,128)S(1)}, u32[]{:S(2)}, u32[]{:S(2)}) collective-permute-start(f32[88,256]{1,0:T(8,128)S(1)} %get-tuple-element.60), channel_id=1, source_target_pairs={{8,16},{16,8},{9,17},{17,9},{10,18},{18,10},{11,19},{19,11},{12,20... | collective-permute-start | bytes 270344 | tf_op jit(solution)/shard_map/ppermute | solution.py:703
  7.3 5.1 %collective-permute-start.2 = (f32[16,384]{1,0:T(8,128)S(1)}, f32[16,384]{1,0:T(8,128)S(1)}, u32[]{:S(2)}, u32[]{:S(2)}) collective-permute-start(f32[16,384]{1,0:T(8,128)S(1)} %get-tuple-element.61), channel_id=1, source_target_pairs={{1,2},{2,1},{3,4},{4,3},{5,6},{6,5},{9,10},{10,9},{11,12},{12,11},... | collective-permute-start | bytes 73736 | tf_op jit(solution)/shard_map/ppermute | solution.py:704
  9.2 3.2 %collective-permute-start.3 = (f32[16,384]{1,0:T(8,128)S(1)}, f32[16,384]{1,0:T(8,128)S(1)}, u32[]{:S(2)}, u32[]{:S(2)}) collective-permute-start(f32[16,384]{1,0:T(8,128)S(1)} %get-tuple-element.62), channel_id=1, source_target_pairs={{0,1},{1,0},{2,3},{3,2},{4,5},{5,4},{6,7},{7,6},{8,9},{9,8},{10,11... | collective-permute-start | bytes 73736 | tf_op jit(solution)/shard_map/ppermute | solution.py:704
  12.9 4.4 %collective-permute-start.6 = (f32[72,256]{1,0:T(8,128)S(1)}, f32[72,256]{1,0:T(8,128)S(1)}, u32[]{:S(2)}, u32[]{:S(2)}) collective-permute-start(f32[72,256]{1,0:T(8,128)S(1)} %get-tuple-element.85), channel_id=1, source_target_pairs={{0,8},{8,0},{16,24},{24,16},{1,9},{9,1},{17,25},{25,17},{2,10},{10... | collective-permute-start | bytes 221192 | tf_op jit(solution)/shard_map/ppermute | solution.py:702
  13.0 7.1 %collective-permute-start.4 = (f32[72,256]{1,0:T(8,128)S(1)}, f32[72,256]{1,0:T(8,128)S(1)}, u32[]{:S(2)}, u32[]{:S(2)}) collective-permute-start(f32[72,256]{1,0:T(8,128)S(1)} %get-tuple-element.84), channel_id=1, source_target_pairs={{8,16},{16,8},{9,17},{17,9},{10,18},{18,10},{11,19},{19,11},{12,20... | collective-permute-start | bytes 221192 | tf_op jit(solution)/shard_map/ppermute | solution.py:703
  16.0 1.3 %collective-permute-start.5 = (f32[16,256]{1,0:T(8,128)S(1)}, f32[16,256]{1,0:T(8,128)S(1)}, u32[]{:S(2)}, u32[]{:S(2)}) collective-permute-start(f32[16,256]{1,0:T(8,128)S(1)} %get-tuple-element.83.own), channel_id=1, source_target_pairs={{0,1},{1,0},{2,3},{3,2},{4,5},{5,4},{6,7},{7,6},{8,9},{9,8},{10,11... | collective-permute-start | bytes 49160 | tf_op jit(solution)/shard_map/ppermute | solution.py:704
